TPU v7x, 32 devices: a whole 2x2x4 slice. The times are simulated.
32 devices in a mesh: group: 1, tile: 32 (over z, y, x, core).
Axes of the slice: x: 2, y: 2, z: 4, core: 2. Of those that a mesh axis runs over, the one named last changes fastest.
Arguments:
- profiles: bfloat16 [16384, 384], P(('group', 'tile')), may hold values from -6 to 6
- radiances: bfloat16 [16384, 512], P(('group', 'tile')), may hold values from -6 to 6
- inner_weight: bfloat16 [384, 4096], replicated, may hold values from -0.3125 to 0.3125
- inner_bias: float32 [4096], replicated, may hold values from -4 to 4
- outer_weight: bfloat16 [4096, 512], replicated, may hold values from -0.09375 to 0.09375
- outer_bias: float32 [512], replicated, may hold values from -4 to 4
- channel_weight: float32 [512], replicated, may hold values from 0.25 to 4
- counts: int32 [32], P(('group', 'tile')), may hold values from 1 to 512, as said below
- owner: int32 [16384, 1], P(('group', 'tile')), may hold values from 0 to 31; in each aligned block of 512 rows (0 to 511, 512 to 1023, ...) at most 32 rows name the same one
- column: int32 [16384], P(('group', 'tile')), may hold values from 0 to 127
Outputs:
- state_gradient: float32 [4096, 384], P(('group', 'tile'))
Inputs may be any that keep to these rules, and one draw needn't show every extreme that they name: `counts`: the largest count equals 512 in every draw. Among the 512 slots of one tile at most 32 name one owner, a bound that some block reaches.
All inputs are finite; a program needn't handle non-finite values.
Results may differ from a plain program's by a relative error of at most 0.0035.
Values may be sent and summed in bfloat16 or wider, within the bound.
No kernel may reach another device: no remote copies, remote signals or barrier semaphores. Data moves between devices by JAX's collectives and lax.ppermute only.
A program may use at most 64 MiB of HBM per device.

v0:
```python
import jax
import jax.numpy as jnp
from jax import lax
from jax.sharding import PartitionSpec as P

COL_DEV = 128


def sounding_block(
    prof_rows, rad_rows, alive, inner_weight, inner_bias, outer_weight, outer_bias, channel_weight
):
    preact = jnp.dot(prof_rows, inner_weight, preferred_element_type=jnp.float32) + inner_bias
    hidden = jax.nn.silu(preact).astype(jnp.bfloat16)
    output = jnp.dot(hidden, outer_weight, preferred_element_type=jnp.float32) + outer_bias
    misfit = jnp.where(
        alive[:, None], channel_weight * (output - rad_rows.astype(jnp.float32)), 0.0
    ).astype(jnp.bfloat16)
    back = lax.dot_general(
        misfit, outer_weight, (((1,), (1,)), ((), ())), preferred_element_type=jnp.float32
    )
    sigma = jax.nn.sigmoid(preact)
    slope = (back * sigma * (1.0 + preact * (1.0 - sigma))).astype(jnp.bfloat16)
    return lax.dot_general(
        slope, inner_weight, (((1,), (1,)), ((), ())), preferred_element_type=jnp.float32
    )


def run_blocks(prof_rows, rad_rows, alive, live_total, weights):
    row_count = prof_rows.shape[0]
    height = min(128, row_count)
    result = jnp.zeros((row_count, prof_rows.shape[1]), jnp.float32)

    def one_block(number, result):
        start = number * height
        piece_prof = lax.dynamic_slice_in_dim(prof_rows, start, height, 0)
        piece_rad = lax.dynamic_slice_in_dim(rad_rows, start, height, 0)
        piece_alive = lax.dynamic_slice_in_dim(alive, start, height, 0)
        grads = sounding_block(piece_prof, piece_rad, piece_alive, *weights)
        return lax.dynamic_update_slice_in_dim(result, grads, start, 0)

    turns = (live_total + height - 1) // height
    return lax.fori_loop(0, turns, one_block, result)


def per_device(
    profiles,
    radiances,
    inner_weight,
    inner_bias,
    outer_weight,
    outer_bias,
    channel_weight,
    counts,
    owner,
    column,
):
    tiles = lax.axis_size("tile")
    row_count = profiles.shape[0]
    width = profiles.shape[1]
    weights = (inner_weight, inner_bias, outer_weight, outer_bias, channel_weight)
    order = jnp.arange(row_count, dtype=jnp.int32)
    alive = order < counts[0]
    grad_rows = run_blocks(profiles, radiances, alive, counts[0], weights)
    most = max(2, 2 * row_count // tiles)
    target = owner[:, 0]
    one_hot = (target[:, None] == jnp.arange(tiles, dtype=jnp.int32)[None, :]).astype(jnp.int32)
    ranks = jnp.sum(jnp.cumsum(one_hot, axis=0) * one_hot, axis=1) - 1
    placing = target * most + ranks
    bucket = jnp.zeros((tiles * most, width), jnp.float32).at[placing].set(grad_rows)
    labels = (
        jnp.full((tiles * most,), -1.0, jnp.float32).at[placing].set(column.astype(jnp.float32))
    )
    got_grad, got_label = (
        lax.all_to_all(
            bucket.reshape(tiles, most, width), "tile", split_axis=0, concat_axis=0, tiled=True
        ),
        lax.all_to_all(
            labels.reshape(tiles, most), "tile", split_axis=0, concat_axis=0, tiled=True
        ),
    )
    selector = (
        jnp.arange(COL_DEV, dtype=jnp.float32)[:, None] == got_label.reshape(1, tiles * most)
    ).astype(jnp.float32)
    return jnp.dot(
        selector,
        got_grad.reshape(tiles * most, width),
        precision=lax.Precision.HIGHEST,
        preferred_element_type=jnp.float32,
    )


def solution(mesh):
    placed = (
        P(("group", "tile"), None),
        P(("group", "tile"), None),
        P(),
        P(),
        P(),
        P(),
        P(),
        P(("group", "tile")),
        P(("group", "tile"), None),
        P(("group", "tile")),
    )
    return jax.shard_map(
        per_device,
        mesh=mesh,
        in_specs=placed,
        out_specs=P(("group", "tile"), None),
        check_vma=False,
    )
```

profile of v0, /device:TPU:0, one launch (start us, length us, event | category | flops | bytes accessed | tf_op | source)
XLA Modules:
  0.0 110.5 jit_solution(17880444689906724303)
XLA Ops:
  0.0 0.7 fusion.17
  0.7 1.2 %reduce-window.6 = s32[32,4,128]{2,0,1:T(8,128)S(1)} reduce-window(s32[32,4,128]{2,0,1:T(8,128)S(1)} %fusion.17, s32[]{:T(128)} %constant.43.clone.1), window={size=1x1x128 pad=0_0x0_0x127_0}, to_apply=%region_0.1 | reduce-window | flops 2080768 | bytes 131076 | tf_op jit(solution)/shard_map/reduce-window
  1.8 0.2 slice_reduce_fusion
  2.1 0.8 fusion.16
  2.9 0.7 compare_select_fusion
  3.6 0.7 convert_element_type.22
  4.3 2.4 %scatter_custom_fusion = f32[1024]{0:T(1024)S(1)} fusion(s32[512]{0:T(512)S(1)} %bitcast.44, f32[512]{0:T(512)S(1)} %convert_element_type.22, f32[]{:T(128)} %constant.41.clone.1), kind=kCustom, calls=%fused_computation.34 | custom fusion | bytes 4100 | tf_op jit(solution)/shard_map/scatter | solution.py:71
  6.7 0.7 all_to_all.9
  7.4 7.3 %all-to-all-start = ((f32[32,1,32]{2,1,0:T(1,128)}), f32[32,1,32]{2,1,0:T(1,128)S(1)}, u32[]{:S(2)}, u32[]{:S(2)}) async-start(f32[32,1,32]{2,1,0:T(1,128)} %all_to_all.9), calls=%async_computation | async-start | bytes 32768 | tf_op jit(solution)/shard_map/all_to_all | solution.py:77
  15.4 1.0 broadcast_in_dim.31
  16.4 11.6 %while.10 = (s32[]{:T(128)}, f32[512,384]{1,0:T(8,128)}, s32[]{:T(128)}, pred[512]{0:T(512)(128)(4,1)S(1)}, f32[512]{0:T(512)}, /*index=5*/bf16[512,384]{1,0:T(8...) while((s32[]{:T(128)}, f32[512,384]{1,0:T(8,128)}, ...), condition=%wide.region_5.6_spmd, body=%wide.region_4.5_spmd.sunk | while | flops 1887305728 | bytes 59445976 | solution.py:42
  16.4 2.8 %convolution_add_fusion.3 = f32[128,4096]{1,0:T(8,128)S(1)} fusion(bf16[384,4096]{1,0:T(8,128)(2,1)} %get-tuple-element.190, f32[4096]{0:T(1024)} %get-tuple-element.191, bf16[512,384]{1,0:T(8,128)(2,1)} %get-tuple-element.189, s32[]{:T(128)S(6)} %select_n.29), kind=kOutput, calls=%fused_computation.4.clone.1 | convolution fusion | flops 403177472 | bytes 5357572 | tf_op jit(solution)/shard_map/while/body/dot_general | solution.py:12
  19.2 0.1 dynamic_slice.17
  19.2 0.3 copy-done.2
  19.6 2.1 %fusion.39 = bf16[128,512]{1,0:T(8,128)(2,1)S(1)} fusion(bf16[4096,512]{1,0:T(8,128)(2,1)S(1)} %copy-done.2, f32[128,4096]{1,0:T(8,128)S(1)} %convolution_add_fusion.3, bf16[512,512]{1,0:T(8,128)(2,1)} %get-tuple-element.194, s32[]{:T(128)S(6)} %select_n.29, f32[512]{0:T(512)S(1)} %copy-done.4, f32[512]{0:T(512)S(1)} %copy-done.3, ...), kind=kOutput, calls=%fused_computation.13.clone.1 | convolution fusion | flops 539885568 | bytes 6557828 | tf_op jit(solution)/shard_map/while/body/dot_general | solution.py:14
  21.7 0.2 copy-done
  21.8 6.1 %convolution_dynamic-update-slice_fusion.2 = f32[512,384]{1,0:T(8,128)} fusion(f32[512,384]{1,0:T(8,128)} %get-tuple-element.170, s32[]{:T(128)S(6)} %select_n.29, bf16[384,4096]{1,0:T(8,128)(2,1)S(1)} %copy-done, bf16[128,512]{1,0:T(8,128)(2,1)S(1)} %fusion.39, bf16[4096,512]{1,0:T(8,128)(2,1)} %get-tuple-element.192, f32[128,4096]{1,0:T(8,128)} %copy-done.1), kind=kOutput, calls=%fused_computation.8.clone.1 | convolution fusion | flops 944242688 | bytes 9764868 | tf_op jit(solution)/shard_map/while/body/dot_general | solution.py:23
  28.0 4.0 %scatter_custom_fusion.1 = f32[1024,384]{1,0:T(8,128)} fusion(s32[512]{0:T(512)S(1)} %bitcast.45, f32[512,384]{1,0:T(8,128)} %get-tuple-element.63, f32[]{:T(128)} %constant.46.clone.1), kind=kCustom, calls=%fused_computation.19 | custom fusion | bytes 1573376 | tf_op jit(solution)/shard_map/scatter | solution.py:69
  32.0 39.3 %all-to-all-start.1 = ((f32[32,32,384]{2,1,0:T(8,128)}), f32[32,32,384]{2,1,0:T(8,128)S(1)}, u32[]{:S(2)}, u32[]{:S(2)}) async-start(f32[32,32,384]{2,1,0:T(8,128)} %bitcast.6), calls=%async_computation.1 | async-start | bytes 3145728 | tf_op jit(solution)/shard_map/all_to_all | solution.py:74
  71.3 0.5 broadcast.57
  71.8 0.7 reduce.5
  72.5 0.1 eq.49
  72.5 36.5 %all-to-all-done.1 = f32[32,32,384]{2,1,0:T(8,128)S(1)} async-done(((f32[32,32,384]{2,1,0:T(8,128)}), f32[32,32,384]{2,1,0:T(8,128)S(1)}, u32[]{:S(2)}, u32[]{:S(2)}) %all-to-all-start.1) | async-done | bytes 1572896 | tf_op jit(solution)/shard_map/all_to_all | solution.py:74
  109.0 1.5 %fusion.13 = f32[128,384]{1,0:T(8,128)} fusion(f32[1024,384]{1,0:T(8,128)S(1)} %bitcast.40, f32[1024]{0:T(1024)S(1)} %eq.49), kind=kOutput, calls=%fused_computation.22 | convolution fusion | flops 604110848 | bytes 1773568 | tf_op jit(solution)/shard_map/dot_general | solution.py:84
  (13 shorter events, 0.1 us)
Async XLA Ops:
  7.4 24.6 %all-to-all-start = ((f32[32,1,32]{2,1,0:T(1,128)}), f32[32,1,32]{2,1,0:T(1,128)S(1)}, u32[]{:S(2)}, u32[]{:S(2)}) async-start(f32[32,1,32]{2,1,0:T(1,128)} %all_to_all.9), calls=%async_computation | async-start | bytes 32768 | tf_op jit(solution)/shard_map/all_to_all | solution.py:77
  16.4 3.2 %copy-start.2 = (bf16[4096,512]{1,0:T(8,128)(2,1)S(1)}, bf16[4096,512]{1,0:T(8,128)(2,1)}, u32[]{:S(2)}) copy-start(bf16[4096,512]{1,0:T(8,128)(2,1)} %get-tuple-element.192) | copy-start | bytes 12582916 | tf_op jit(solution)/shard_map/while
  16.4 3.2 %copy-start.3 = (f32[512]{0:T(512)S(1)}, f32[512]{0:T(512)}, u32[]{:S(2)}) copy-start(f32[512]{0:T(512)} %get-tuple-element.188) | copy-start | bytes 6148 | tf_op jit(solution)/shard_map/while
  16.4 3.2 %copy-start.4 = (f32[512]{0:T(512)S(1)}, f32[512]{0:T(512)}, u32[]{:S(2)}) copy-start(f32[512]{0:T(512)} %get-tuple-element.193) | copy-start | bytes 6148 | tf_op jit(solution)/shard_map/while
  19.1 2.5 %copy-start.1 = (f32[128,4096]{1,0:T(8,128)}, f32[128,4096]{1,0:T(8,128)S(1)}, u32[]{:S(2)}) copy-start(f32[128,4096]{1,0:T(8,128)S(1)} %convolution_add_fusion.3) | copy-start | bytes 6291460 | tf_op jit(solution)/shard_map/while
  19.6 2.3 %copy-start = (bf16[384,4096]{1,0:T(8,128)(2,1)S(1)}, bf16[384,4096]{1,0:T(8,128)(2,1)}, u32[]{:S(2)}) copy-start(bf16[384,4096]{1,0:T(8,128)(2,1)} %get-tuple-element.190) | copy-start | bytes 9437188 | tf_op jit(solution)/shard_map/while
  32.0 77.0 %all-to-all-start.1 = ((f32[32,32,384]{2,1,0:T(8,128)}), f32[32,32,384]{2,1,0:T(8,128)S(1)}, u32[]{:S(2)}, u32[]{:S(2)}) async-start(f32[32,32,384]{2,1,0:T(8,128)} %bitcast.6), calls=%async_computation.1 | async-start | bytes 3145728 | tf_op jit(solution)/shard_map/all_to_all | solution.py:74
where the time goes:
time: 111 us; the launch traced here: 110 us
  starting transfers between devices  46.6 us (42%)
  waiting for transfers between devices  36.5 us (33%)
  matrix products  12.4 us (11%)
  local copies, waits for them, and re-layouts  9.51 us (9%)
  other arithmetic  4.74 us (4%)
    all_to_all x1, starting transfers between devices, per_device(): lax.all_to_all(bucket.reshape(tiles, most, width), 'tile', split_axis=0,...  39.3 us
    all_to_all x1, waiting for transfers between devices, per_device(): lax.all_to_all(bucket.reshape(tiles, most, width), 'tile', split_axis=0,...  36.5 us
    all_to_all x1, starting transfers between devices, per_device(): lax.all_to_all(labels.reshape(tiles, most), 'tile', split_axis=0, concat_...  7.3 us
    dot_general x1, matrix products, sounding_block(): lax.dot_general(slope, inner_weight, (((1,), (1,)), ((), ())), preferred_...  6.11 us
    scatter x1, local copies, waits for them, and re-layouts, per_device(): jnp.zeros((tiles * most, width), jnp.float32).at[placing].set(grad_rows)  4.03 us
    dot_general x1, matrix products, sounding_block(): jnp.dot(prof_rows, inner_weight, preferred_element_type=jnp.float32)  2.75 us
    scatter x1, local copies, waits for them, and re-layouts, per_device(): jnp.full((tiles * most,), -1.0, jnp.float32).at[placing]  2.44 us
  transfers between devices with their start and end apart: 2, of which 1 were waited for; matrix products, arithmetic and copies ran while one was open for 16% of the time, Pallas kernels for 0%

commit v1 on v0

v1 whole, which is shorter than its diff:
```python
import functools

import jax
import jax.numpy as jnp
from jax import lax
from jax.experimental import pallas as pl
from jax.experimental.pallas import tpu as pltpu
from jax.sharding import PartitionSpec as P

COL_DEV = 128
CHUNK = 512
NT = (((1,), (1,)), ((), ()))


def rows_kernel(
    most,
    count_ref,
    code_ref,
    prof_ref,
    rad_ref,
    w1_hbm,
    b1_ref,
    w2_hbm,
    b2_ref,
    cw_ref,
    out_ref,
    w1_ref,
    w2_ref,
    factor_ref,
    sem1,
    sem2,
):
    rows, width = prof_ref.shape
    hid = w1_ref.shape[1]
    chunks = hid // CHUNK
    copies = []
    for i in range(chunks):
        part = pl.ds(i * CHUNK, CHUNK)
        one = pltpu.make_async_copy(w1_hbm.at[:, part], w1_ref.at[:, part], sem1.at[i])
        two = pltpu.make_async_copy(w2_hbm.at[part, :], w2_ref.at[part, :], sem2.at[i])
        one.start()
        two.start()
        copies.append((one, two))

    code = code_ref[...]
    owner = lax.shift_right_arithmetic(code, 7)
    slots = out_ref.shape[0]
    tiles = slots // most
    one_hot = (lax.broadcasted_iota(jnp.int32, (tiles, rows), 0) == owner).astype(jnp.float32)
    upper = (
        lax.broadcasted_iota(jnp.int32, (rows, rows), 0)
        <= lax.broadcasted_iota(jnp.int32, (rows, rows), 1)
    ).astype(jnp.float32)
    running = jnp.dot(
        one_hot.astype(jnp.bfloat16),
        upper.astype(jnp.bfloat16),
        preferred_element_type=jnp.float32,
    )
    rank = jnp.sum(running * one_hot, axis=0, keepdims=True).astype(jnp.int32) - 1
    slot = jnp.where(code < 0, -1, owner * most + rank)
    placing = (
        (lax.broadcasted_iota(jnp.int32, (slots, rows), 0) == slot)
        .astype(jnp.float32)
        .astype(jnp.bfloat16)
    )

    prof = prof_ref[...]
    output = jnp.zeros((rows, rad_ref.shape[1]), jnp.float32)
    for i in range(chunks):
        part = pl.ds(i * CHUNK, CHUNK)
        copies[i][0].wait()
        preact = jnp.dot(prof, w1_ref[:, part], preferred_element_type=jnp.float32)
        preact = preact + b1_ref[:, part]
        sigma = 0.5 * jnp.tanh(0.5 * preact) + 0.5
        hidden = preact * sigma
        factor_ref[:, part] = sigma + hidden * (1.0 - sigma)
        copies[i][1].wait()
        output += jnp.dot(
            hidden.astype(jnp.bfloat16), w2_ref[part, :], preferred_element_type=jnp.float32
        )
    alive = lax.broadcasted_iota(jnp.int32, (rows, 1), 0) < count_ref[0]
    misfit = cw_ref[...] * (output + b2_ref[...] - rad_ref[...].astype(jnp.float32))
    misfit = jnp.where(alive, misfit, 0.0).astype(jnp.bfloat16)
    grads = jnp.zeros((rows, width), jnp.float32)
    for i in range(chunks):
        part = pl.ds(i * CHUNK, CHUNK)
        back = lax.dot_general(misfit, w2_ref[part, :], NT, preferred_element_type=jnp.float32)
        slope = (back * factor_ref[:, part]).astype(jnp.bfloat16)
        grads += lax.dot_general(slope, w1_ref[:, part], NT, preferred_element_type=jnp.float32)
    out_ref[...] = jnp.dot(
        placing, grads.astype(jnp.bfloat16), preferred_element_type=jnp.float32
    ).astype(jnp.bfloat16)


def selector_kernel(most, me_ref, codes_ref, out_ref):
    tiles, rows = codes_ref.shape
    me = me_ref[0]
    upper = (
        (
            lax.broadcasted_iota(jnp.int32, (rows, rows), 0)
            <= lax.broadcasted_iota(jnp.int32, (rows, rows), 1)
        )
        .astype(jnp.float32)
        .astype(jnp.bfloat16)
    )
    codes = codes_ref[...]
    mine = (lax.shift_right_arithmetic(codes, 7) == me).astype(jnp.float32)
    rank = (
        jnp.dot(mine.astype(jnp.bfloat16), upper, preferred_element_type=jnp.float32) * mine
    ).astype(jnp.int32) - 1
    column = jnp.where(mine > 0.0, codes & (COL_DEV - 1), -1)
    for t in range(tiles):
        col_hot = (
            (lax.broadcasted_iota(jnp.int32, (COL_DEV, rows), 0) == column[t : t + 1, :])
            .astype(jnp.float32)
            .astype(jnp.bfloat16)
        )
        rank_hot = (
            (lax.broadcasted_iota(jnp.int32, (most, rows), 0) == rank[t : t + 1, :])
            .astype(jnp.float32)
            .astype(jnp.bfloat16)
        )
        out_ref[:, t * most : (t + 1) * most] = lax.dot_general(
            col_hot, rank_hot, NT, preferred_element_type=jnp.float32
        ).astype(jnp.bfloat16)


def per_device(
    profiles,
    radiances,
    inner_weight,
    inner_bias,
    outer_weight,
    outer_bias,
    channel_weight,
    counts,
    owner,
    column,
):
    tiles = lax.axis_size("tile")
    rows, width = profiles.shape
    hid = inner_weight.shape[1]
    chan = radiances.shape[1]
    most = max(2, 2 * rows // tiles)
    slots = tiles * most
    chunks = hid // CHUNK
    alive = jnp.arange(rows, dtype=jnp.int32) < counts[0]
    code = jnp.where(alive, owner[:, 0] * COL_DEV + column, -1)
    codes = lax.all_gather(code, "tile", axis=0, tiled=False)
    vmem = pl.BlockSpec(memory_space=pltpu.VMEM)
    smem = pl.BlockSpec(memory_space=pltpu.SMEM)
    anywhere = pl.BlockSpec(memory_space=pl.ANY)
    flops = 4 * rows * hid * (width + chan)
    bucket = pl.pallas_call(
        functools.partial(rows_kernel, most),
        out_shape=jax.ShapeDtypeStruct((slots, width), jnp.bfloat16),
        in_specs=[smem, vmem, vmem, vmem, anywhere, vmem, anywhere, vmem, vmem],
        out_specs=vmem,
        scratch_shapes=[
            pltpu.VMEM((width, hid), jnp.bfloat16),
            pltpu.VMEM((hid, chan), jnp.bfloat16),
            pltpu.VMEM((rows, hid), jnp.float32),
            pltpu.SemaphoreType.DMA((chunks,)),
            pltpu.SemaphoreType.DMA((chunks,)),
        ],
        compiler_params=pltpu.CompilerParams(vmem_limit_bytes=48 * 1024 * 1024),
        cost_estimate=pl.CostEstimate(flops=flops, bytes_accessed=9 << 20, transcendentals=0),
        name="rows_kernel",
    )(
        counts,
        code.reshape(1, rows),
        profiles,
        radiances,
        inner_weight,
        inner_bias.reshape(1, hid),
        outer_weight,
        outer_bias.reshape(1, chan),
        channel_weight.reshape(1, chan),
    )
    got = lax.all_to_all(bucket, "tile", split_axis=0, concat_axis=0, tiled=True)
    me = lax.axis_index("tile").astype(jnp.int32).reshape(1)
    selector = pl.pallas_call(
        functools.partial(selector_kernel, most),
        out_shape=jax.ShapeDtypeStruct((COL_DEV, slots), jnp.bfloat16),
        in_specs=[smem, vmem],
        out_specs=vmem,
        compiler_params=pltpu.CompilerParams(vmem_limit_bytes=16 * 1024 * 1024),
        cost_estimate=pl.CostEstimate(flops=1 << 30, bytes_accessed=1 << 20, transcendentals=0),
        name="selector_kernel",
    )(me, codes)
    return jnp.dot(selector, got, preferred_element_type=jnp.float32)


def solution(mesh):
    placed = (
        P(("group", "tile"), None),
        P(("group", "tile"), None),
        P(),
        P(),
        P(),
        P(),
        P(),
        P(("group", "tile")),
        P(("group", "tile"), None),
        P(("group", "tile")),
    )
    return jax.shard_map(
        per_device,
        mesh=mesh,
        in_specs=placed,
        out_specs=P(("group", "tile"), None),
        check_vma=False,
    )
```

time: 111 us -> 81.2 us (0.73)
  blocking collectives: 0 us -> 48.2 us
  starting transfers between devices: 46.6 us -> 7.3 us
  waiting for transfers between devices: 36.5 us -> 0.01 us
  Pallas kernels: 0 us -> 16.2 us
  matrix products: 12.4 us -> 0.98 us
  local copies, waits for them, and re-layouts: 9.51 us -> 6.01 us
  other arithmetic: 4.74 us -> 1.37 us
    all_gather x0 -> x1, blocking collectives: none -> 48.2 us  [per_device(): codes = lax.all_gather(code, 'tile', axis=0, tiled=False)]
    all_to_all x2 -> x1, starting transfers between devices: 46.6 us -> 7.3 us  [per_device(): lax.all_to_all(bucket, 'tile', split_axis=0, concat_axis=0, tiled=True)]
    all_to_all x2 -> x1, waiting for transfers between devices: 36.5 us -> 0.01 us  [per_device(): lax.all_to_all(bucket, 'tile', split_axis=0, concat_axis=0, tiled=True)]
    pallas_call x0 -> x2, Pallas kernels: none -> 16.2 us  [the longest x1 14.7 us: per_device(): pl.pallas_call(functools.partial(rows_kernel, most), out_shape=jax.ShapeD...]
    dot_general x4 -> x1, matrix products: 12.4 us -> 0.98 us  [per_device(): return jnp.dot(selector, got, preferred_element_type=jnp.float32)]
    scatter x2 -> x0, local copies, waits for them, and re-layouts: 6.47 us -> none  [the longest x1 4.03 us: per_device(): jnp.zeros((tiles * most, width), jnp.float32).at[placing].set(grad_rows)]
    unnamed x0 -> x13, local copies, waits for them, and re-layouts: none -> 6.01 us
    convert_element_type x2 -> x0, other arithmetic: 1.37 us -> none  [the longest x1 0.69 us: per_device(): (target[:, None] == jnp.arange(tiles, dtype=jnp.int32)[None, :]).astype(j...]
  transfers between devices with their start and end apart: 2 -> 1, of which waited for: 1 -> 0; matrix products, arithmetic and copies ran while one was open for 16% -> 0% of each run, Pallas kernels for 0% -> 2%
where the time goes in v1:
time: 81.2 us; the launch traced here: 80.7 us
  blocking collectives  48.2 us (59%)
  Pallas kernels  16.2 us (20%)
  starting transfers between devices  7.3 us (9%)
  local copies, waits for them, and re-layouts  6.01 us (7%)
  other arithmetic  1.37 us (2%)
  matrix products  0.98 us (1%)
    all_gather x1, blocking collectives, per_device(): codes = lax.all_gather(code, 'tile', axis=0, tiled=False)  48.2 us
    pallas_call x1, Pallas kernels, per_device(): pl.pallas_call(functools.partial(rows_kernel, most), out_shape=jax.ShapeD...  14.7 us
    all_to_all x1, starting transfers between devices, per_device(): lax.all_to_all(bucket, 'tile', split_axis=0, concat_axis=0, tiled=True)  7.3 us
    unnamed x13, local copies, waits for them, and re-layouts  6.01 us
  transfers between devices with their start and end apart: 1, of which 0 were waited for; matrix products, arithmetic and copies ran while one was open for 0% of the time, Pallas kernels for 2%

profile of v1, /device:TPU:0, one launch (start us, length us, event | category | flops | bytes accessed | tf_op | source)
XLA Modules:
  0.0 80.7 jit_solution(7633194489328476630)
XLA Ops:
  0.7 0.7 broadcast_multiply_fusion
  1.3 0.7 add_select_fusion
  2.0 0.0 copy-start
  2.0 1.9 %copy-done = bf16[384,4096]{1,0:T(8,128)(2,1)S(1)} copy-done((bf16[384,4096]{1,0:T(8,128)(2,1)S(1)}, bf16[384,4096]{1,0:T(8,128)(2,1)}, u32[]{:S(2)}) %copy-start) | copy-done | bytes 3145752
  3.9 0.0 copy-start.1
  3.9 1.0 %copy-done.1 = bf16[512,512]{1,0:T(8,128)(2,1)S(1)} copy-done((bf16[512,512]{1,0:T(8,128)(2,1)S(1)}, bf16[512,512]{1,0:T(8,128)(2,1)}, u32[]{:S(2)}) %copy-start.1) | copy-done | bytes 524312
  5.0 0.0 copy-start.2
  5.0 1.0 %copy-done.2 = bf16[512,384]{1,0:T(8,128)(2,1)S(1)} copy-done((bf16[512,384]{1,0:T(8,128)(2,1)S(1)}, bf16[512,384]{1,0:T(8,128)(2,1)}, u32[]{:S(2)}) %copy-start.2) | copy-done | bytes 393240
  6.0 0.0 copy-start.3
  6.0 0.7 copy-done.3
  6.7 0.0 copy-start.4
  6.7 0.7 copy-done.4
  7.4 0.0 copy-start.5
  7.4 0.7 copy-done.5
  8.0 14.7 %rows_kernel.1 = bf16[1024,384]{1,0:T(8,128)(2,1)} custom-call(s32[1]{0:T(128)} %copy.14.count_ref, s32[1,512]{1,0:T(1,128)S(1)} %bitcast.17, bf16[512,384]{1,0:T(8,128)(2,1)S(1)} %copy-done.2, bf16[512,512]{1,0:T(8,128)(2,1)S(1)} %copy-done.1, bf16[384,4096]{1,0:T(8,128)(2,1)S(1)} %copy-done, f32[1,4096]{1,0:T(1,128)S(1)} %bitcast.19, ...), custom_call_target="tpu_custom_call" | custom-call | flops 7516192768 | bytes 9437184 | tf_op jit(solution)/shard_map/rows_kernel/pallas_call | solution.py:154
  22.7 7.3 %all-to-all-start = ((bf16[32,32,384]{2,1,0:T(8,128)(2,1)}), bf16[32,32,384]{2,1,0:T(8,128)(2,1)S(1)}, u32[]{:S(2)}, u32[]{:S(2)}) async-start(bf16[32,32,384]{2,1,0:T(8,128)(2,1)} %bitcast.8), calls=%async_computation | async-start | bytes 1572864 | tf_op jit(solution)/shard_map/all_to_all | solution.py:180
  30.0 48.2 %all-gather.1 = s32[32,1,512]{2,1,0:T(1,128)S(1)} all-gather(s32[1,1,512]{2,1,0:T(1,128)S(1)} %bitcast.18), channel_id=2, replica_groups=mesh['group'=1,'tile'=32] {'tile'}, dimensions={0}, use_global_device_ids=true | all-gather | bytes 67584 | tf_op jit(solution)/shard_map/all_gather | solution.py:149
  78.2 1.5 %selector_kernel.1 = bf16[128,1024]{1,0:T(8,128)(2,1)S(1)} custom-call(s32[1]{0:T(128)} %bitcast.me_ref, s32[32,512]{1,0:T(8,128)S(1)} %bitcast.16), custom_call_target="tpu_custom_call" | custom-call | flops 1073741824 | bytes 1048576 | tf_op jit(solution)/shard_map/selector_kernel/pallas_call | solution.py:182
  79.7 0.0 all-to-all-done
  79.8 1.0 %fusion = f32[128,384]{1,0:T(8,128)} fusion(bf16[128,1024]{1,0:T(8,128)(2,1)S(1)} %selector_kernel.1, bf16[1024,384]{1,0:T(8,128)(2,1)S(1)} %bitcast.22), kind=kOutput, calls=%fused_computation.4 | convolution fusion | flops 100663296 | bytes 1245184 | tf_op jit(solution)/shard_map/dot_general | solution.py:191
  (1 shorter events, 0.0 us)
Async XLA Ops:
  2.0 1.9 %copy-start = (bf16[384,4096]{1,0:T(8,128)(2,1)S(1)}, bf16[384,4096]{1,0:T(8,128)(2,1)}, u32[]{:S(2)}) copy-start(bf16[384,4096]{1,0:T(8,128)(2,1)} %w1_hbm.1) | copy-start | bytes 9437188
  3.9 1.0 %copy-start.1 = (bf16[512,512]{1,0:T(8,128)(2,1)S(1)}, bf16[512,512]{1,0:T(8,128)(2,1)}, u32[]{:S(2)}) copy-start(bf16[512,512]{1,0:T(8,128)(2,1)} %rad_ref.1) | copy-start | bytes 1572868
  5.0 1.0 %copy-start.2 = (bf16[512,384]{1,0:T(8,128)(2,1)S(1)}, bf16[512,384]{1,0:T(8,128)(2,1)}, u32[]{:S(2)}) copy-start(bf16[512,384]{1,0:T(8,128)(2,1)} %prof_ref.1) | copy-start | bytes 1179652
  6.0 0.7 copy-start.3
  6.7 0.7 copy-start.4
  7.4 0.7 copy-start.5
  22.7 57.0 %all-to-all-start = ((bf16[32,32,384]{2,1,0:T(8,128)(2,1)}), bf16[32,32,384]{2,1,0:T(8,128)(2,1)S(1)}, u32[]{:S(2)}, u32[]{:S(2)}) async-start(bf16[32,32,384]{2,1,0:T(8,128)(2,1)} %bitcast.8), calls=%async_computation | async-start | bytes 1572864 | tf_op jit(solution)/shard_map/all_to_all | solution.py:180

commit v2 on v1

v2 whole, which is shorter than its diff:
```python
import functools

import jax
import jax.numpy as jnp
from jax import lax
from jax.experimental import pallas as pl
from jax.experimental.pallas import tpu as pltpu
from jax.sharding import PartitionSpec as P

COL_DEV = 128
CHUNK = 512
LANES = 128
LABEL_ROWS = 8
NT = (((1,), (1,)), ((), ()))


def as_bf16(mask):
    return mask.astype(jnp.float32).astype(jnp.bfloat16)


def rows_kernel(
    most,
    me_ref,
    count_ref,
    owner_ref,
    column_ref,
    prof_hbm,
    rad_hbm,
    w1_hbm,
    b1_hbm,
    w2_hbm,
    b2_hbm,
    cw_hbm,
    out_ref,
    prof_ref,
    rad_ref,
    w1_ref,
    b1_ref,
    w2_ref,
    b2_ref,
    cw_ref,
    hidden_ref,
    factor_ref,
    sems,
):
    rows, width = prof_ref.shape
    hid = w1_ref.shape[1]
    chan = rad_ref.shape[1]
    half = hid // 2
    low, high = pl.ds(0, half), pl.ds(half, half)
    pairs = (
        (prof_hbm, prof_ref),
        (b1_hbm, b1_ref),
        (w1_hbm.at[:, low], w1_ref.at[:, low]),
        (w1_hbm.at[:, high], w1_ref.at[:, high]),
        (w2_hbm, w2_ref),
        (rad_hbm, rad_ref),
        (b2_hbm, b2_ref),
        (cw_hbm, cw_ref),
    )
    copies = [
        pltpu.make_async_copy(src, dst, sems.at[i]) for i, (src, dst) in enumerate(pairs)
    ]
    for copy in copies:
        copy.start()

    tiles = out_ref.shape[0]
    slots = tiles * most
    live = lax.broadcasted_iota(jnp.int32, (1, rows), 1) < count_ref[0]
    owner = jnp.where(live, owner_ref[...], -1)
    mine = lax.broadcasted_iota(jnp.int32, (tiles, rows), 0) == owner
    one_hot = mine.astype(jnp.float32)
    upper = as_bf16(
        lax.broadcasted_iota(jnp.int32, (rows, rows), 0)
        <= lax.broadcasted_iota(jnp.int32, (rows, rows), 1)
    )
    running = jnp.dot(one_hot.astype(jnp.bfloat16), upper, preferred_element_type=jnp.float32)
    rank = jnp.sum(running * one_hot, axis=0, keepdims=True).astype(jnp.int32) - 1
    slot = jnp.where(live, owner * most + rank, -1)
    placing = as_bf16(lax.broadcasted_iota(jnp.int32, (slots, rows), 0) == slot)
    lane = rank + lax.rem(me_ref[0], LANES // most) * most
    lane_hot = as_bf16(lax.broadcasted_iota(jnp.int32, (LANES, rows), 0) == lane)
    marked = jnp.where(mine, (column_ref[...] + 1).astype(jnp.float32), 0.0)
    labels = lax.dot_general(
        marked.astype(jnp.bfloat16), lane_hot, NT, preferred_element_type=jnp.float32
    )

    copies[0].wait()
    copies[1].wait()
    prof = (prof_ref[...].astype(jnp.float32) * 0.5).astype(jnp.bfloat16)
    for i in range(hid // CHUNK):
        part = pl.ds(i * CHUNK, CHUNK)
        if i == 0:
            copies[2].wait()
        if i == hid // CHUNK // 2:
            copies[3].wait()
        u = jnp.dot(prof, w1_ref[:, part], preferred_element_type=jnp.float32)
        u = u + 0.5 * b1_ref[:, part]
        p = jnp.tanh(u) + 1.0
        hidden = u * p
        hidden_ref[:, part] = hidden.astype(jnp.bfloat16)
        factor_ref[:, part] = p + hidden * (2.0 - p)
    for copy in copies[4:]:
        copy.wait()
    output = jnp.dot(hidden_ref[...], w2_ref[...], preferred_element_type=jnp.float32)
    misfit = (0.5 * cw_ref[...]) * (output + b2_ref[...] - rad_ref[...].astype(jnp.float32))
    alive = lax.broadcasted_iota(jnp.int32, (rows, 1), 0) < count_ref[0]
    misfit = jnp.where(alive, misfit, 0.0).astype(jnp.bfloat16)
    for i in range(hid // CHUNK):
        part = pl.ds(i * CHUNK, CHUNK)
        back = lax.dot_general(misfit, w2_ref[part, :], NT, preferred_element_type=jnp.float32)
        hidden_ref[:, part] = (back * factor_ref[:, part]).astype(jnp.bfloat16)
    grads = lax.dot_general(
        hidden_ref[...], w1_ref[...], NT, preferred_element_type=jnp.float32
    ).astype(jnp.bfloat16)
    placed = jnp.dot(placing, grads, preferred_element_type=jnp.float32).astype(jnp.bfloat16)
    parts = width // LANES
    for k in range(parts):
        out_ref[:, k * most : (k + 1) * most, :] = placed[
            :, k * LANES : (k + 1) * LANES
        ].reshape(tiles, most, LANES)
    out_ref[:, parts * most :, :] = jnp.broadcast_to(
        labels.reshape(tiles, 1, LANES), (tiles, LABEL_ROWS, LANES)
    ).astype(jnp.bfloat16)


def sums_kernel(most, got_ref, out_ref):
    tiles = got_ref.shape[0]
    parts = out_ref.shape[1] // LANES
    group = LANES // most
    marks = got_ref[:, parts * most :, :].astype(jnp.float32)[:, 0, :]
    index = lax.broadcasted_iota(jnp.int32, (COL_DEV, LANES), 0) + 1
    total = [jnp.zeros((COL_DEV, LANES), jnp.float32) for _ in range(parts)]
    for g in range(tiles // group):
        label = jnp.sum(marks[g * group : (g + 1) * group], axis=0, keepdims=True)
        chosen = as_bf16(index == label.astype(jnp.int32))
        for k in range(parts):
            block = got_ref[g * group : (g + 1) * group, k * most : (k + 1) * most, :]
            total[k] += jnp.dot(
                chosen, block.reshape(LANES, LANES), preferred_element_type=jnp.float32
            )
    for k in range(parts):
        out_ref[:, k * LANES : (k + 1) * LANES] = total[k]


def per_device(
    profiles,
    radiances,
    inner_weight,
    inner_bias,
    outer_weight,
    outer_bias,
    channel_weight,
    counts,
    owner,
    column,
):
    tiles = lax.axis_size("tile")
    rows, width = profiles.shape
    hid = inner_weight.shape[1]
    chan = radiances.shape[1]
    most = max(2, 2 * rows // tiles)
    high = width // LANES * most + LABEL_ROWS
    vmem = pl.BlockSpec(memory_space=pltpu.VMEM)
    smem = pl.BlockSpec(memory_space=pltpu.SMEM)
    anywhere = pl.BlockSpec(memory_space=pl.ANY)
    me = lax.axis_index("tile").astype(jnp.int32).reshape(1)
    bucket = pl.pallas_call(
        functools.partial(rows_kernel, most),
        out_shape=jax.ShapeDtypeStruct((tiles, high, LANES), jnp.bfloat16),
        in_specs=[smem, smem, vmem, vmem] + [anywhere] * 7,
        out_specs=vmem,
        scratch_shapes=[
            pltpu.VMEM((rows, width), jnp.bfloat16),
            pltpu.VMEM((rows, chan), jnp.bfloat16),
            pltpu.VMEM((width, hid), jnp.bfloat16),
            pltpu.VMEM((1, hid), jnp.float32),
            pltpu.VMEM((hid, chan), jnp.bfloat16),
            pltpu.VMEM((1, chan), jnp.float32),
            pltpu.VMEM((1, chan), jnp.float32),
            pltpu.VMEM((rows, hid), jnp.bfloat16),
            pltpu.VMEM((rows, hid), jnp.float32),
            pltpu.SemaphoreType.DMA((8,)),
        ],
        compiler_params=pltpu.CompilerParams(vmem_limit_bytes=60 * 1024 * 1024),
        name="rows_kernel",
    )(
        me,
        counts,
        owner.reshape(1, rows),
        column.reshape(1, rows),
        profiles,
        radiances,
        inner_weight,
        inner_bias.reshape(1, hid),
        outer_weight,
        outer_bias.reshape(1, chan),
        channel_weight.reshape(1, chan),
    )
    got = lax.all_to_all(bucket, "tile", split_axis=0, concat_axis=0, tiled=True)
    return pl.pallas_call(
        functools.partial(sums_kernel, most),
        out_shape=jax.ShapeDtypeStruct((COL_DEV, width), jnp.float32),
        in_specs=[vmem],
        out_specs=vmem,
        compiler_params=pltpu.CompilerParams(vmem_limit_bytes=16 * 1024 * 1024),
        name="sums_kernel",
    )(got)


def solution(mesh):
    placed = (
        P(("group", "tile"), None),
        P(("group", "tile"), None),
        P(),
        P(),
        P(),
        P(),
        P(),
        P(("group", "tile")),
        P(("group", "tile"), None),
        P(("group", "tile")),
    )
    return jax.shard_map(
        per_device,
        mesh=mesh,
        in_specs=placed,
        out_specs=P(("group", "tile"), None),
        check_vma=False,
    )
```

time: 81.2 us -> 45.1 us (0.56)
  blocking collectives: 48.2 us -> 29.3 us
  starting transfers between devices: 7.3 us -> 0 us
  local copies, waits for them, and re-layouts: 6.01 us -> 0 us
  Pallas kernels: 16.2 us -> 14.8 us
  other arithmetic: 1.37 us -> 0 us
  matrix products: 0.98 us -> 0 us
    all_gather x1 -> x0, blocking collectives: 48.2 us -> none  [per_device(): codes = lax.all_gather(code, 'tile', axis=0, tiled=False)]
    all_to_all x0 -> x1, blocking collectives: none -> 29.3 us  [per_device(): lax.all_to_all(bucket, 'tile', split_axis=0, concat_axis=0, tiled=True)]
    all_to_all x1 -> x0, starting transfers between devices: 7.3 us -> none  [per_device(): lax.all_to_all(bucket, 'tile', split_axis=0, concat_axis=0, tiled=True)]
    unnamed x13 -> x0, local copies, waits for them, and re-layouts: 6.01 us -> none
    dot_general x1 -> x0, matrix products: 0.98 us -> none  [per_device(): return jnp.dot(selector, got, preferred_element_type=jnp.float32)]
    pallas_call x1, Pallas kernels: 14.7 us -> 13.8 us  [per_device(): pl.pallas_call(functools.partial(rows_kernel, most), out_shape=jax.ShapeD...]
  transfers between devices with their start and end apart: 1 -> 0, of which waited for: 0 -> 0; matrix products, arithmetic and copies ran while one was open for 0% -> 0% of each run, Pallas kernels for 2% -> 0%
where the time goes in v2:
time: 45.1 us; the launch traced here: 44.8 us
  blocking collectives  29.3 us (65%)
  Pallas kernels  14.8 us (33%)
  between operations  0.66 us (1%)
    all_to_all x1, blocking collectives, per_device(): lax.all_to_all(bucket, 'tile', split_axis=0, concat_axis=0, tiled=True)  29.3 us
    pallas_call x1, Pallas kernels, per_device(): pl.pallas_call(functools.partial(rows_kernel, most), out_shape=jax.ShapeD...  13.8 us
    pallas_call x1, Pallas kernels, per_device(): pl.pallas_call(functools.partial(sums_kernel, most), out_shape=jax.ShapeD...  1.04 us

profile of v2, /device:TPU:0, one launch (start us, length us, event | category | flops | bytes accessed | tf_op | source)
XLA Modules:
  0.0 44.8 jit_solution(4602659102636895554)
XLA Ops:
  0.7 13.8 %rows_kernel.1 = bf16[32,104,128]{2,1,0:T(8,128)(2,1)} custom-call(s32[1]{0:T(128)} %bitcast.me_ref, s32[1]{0:T(128)S(6)} %copy.11.count_ref, s32[1,512]{1,0:T(1,128)} %bitcast.7, s32[1,512]{1,0:T(1,128)} %bitcast.8, bf16[512,384]{1,0:T(8,128)(2,1)} %prof_hbm.1, bf16[512,512]{1,0:T(8,128)(2,1)} %rad_hbm.1, bf16[384,4096]{1,0:T(8,128)(2,1)} %w1_hbm.1, ...), custom_call_target="tpu_custom_call" | custom-call | tf_op jit(solution)/shard_map/rows_kernel/pallas_call | solution.py:168
  14.5 29.3 %all_to_all.5.got_ref = bf16[32,104,128]{2,1,0:T(8,128)(2,1)S(1)} all-to-all(bf16[32,104,128]{2,1,0:T(8,128)(2,1)} %rows_kernel.1), channel_id=1, replica_groups=mesh['group'=1,'tile'=32] {'tile'}, dimensions={0} | all-to-all | bytes 1703936 | tf_op jit(solution)/shard_map/all_to_all | solution.py:200
  43.8 1.0 %sums_kernel.1 = f32[128,384]{1,0:T(8,128)} custom-call(bf16[32,104,128]{2,1,0:T(8,128)(2,1)S(1)} %all_to_all.5.got_ref), custom_call_target="tpu_custom_call" | custom-call | tf_op jit(solution)/shard_map/sums_kernel/pallas_call | solution.py:201

commit v3 on v2

--- a/solution.py
+++ b/solution.py
@@ -11,6 +11,7 @@
 CHUNK = 512
 LANES = 128
 LABEL_ROWS = 8
+INNER = 8
 NT = (((1,), (1,)), ((), ()))
 
 
@@ -19,8 +20,8 @@
 
 
 def rows_kernel(
+    tiles,
     most,
-    me_ref,
     count_ref,
     owner_ref,
     column_ref,
@@ -64,8 +65,7 @@
     for copy in copies:
         copy.start()
 
-    tiles = out_ref.shape[0]
-    slots = tiles * most
+    inner = out_ref.shape[0]
     live = lax.broadcasted_iota(jnp.int32, (1, rows), 1) < count_ref[0]
     owner = jnp.where(live, owner_ref[...], -1)
     mine = lax.broadcasted_iota(jnp.int32, (tiles, rows), 0) == owner
@@ -76,11 +76,13 @@
     )
     running = jnp.dot(one_hot.astype(jnp.bfloat16), upper, preferred_element_type=jnp.float32)
     rank = jnp.sum(running * one_hot, axis=0, keepdims=True).astype(jnp.int32) - 1
-    slot = jnp.where(live, owner * most + rank, -1)
-    placing = as_bf16(lax.broadcasted_iota(jnp.int32, (slots, rows), 0) == slot)
-    lane = rank + lax.rem(me_ref[0], LANES // most) * most
+    place = owner & (inner - 1)
+    lane = lax.shift_right_arithmetic(owner, inner.bit_length() - 1) * most + rank
+    slot = jnp.where(live, place * LANES + lane, -1)
+    placing = as_bf16(lax.broadcasted_iota(jnp.int32, (inner * LANES, rows), 0) == slot)
     lane_hot = as_bf16(lax.broadcasted_iota(jnp.int32, (LANES, rows), 0) == lane)
-    marked = jnp.where(mine, (column_ref[...] + 1).astype(jnp.float32), 0.0)
+    here = live & (lax.broadcasted_iota(jnp.int32, (inner, rows), 0) == place)
+    marked = jnp.where(here, (column_ref[...] + 1).astype(jnp.float32), 0.0)
     labels = lax.dot_general(
         marked.astype(jnp.bfloat16), lane_hot, NT, preferred_element_type=jnp.float32
     )
@@ -116,31 +118,34 @@
     placed = jnp.dot(placing, grads, preferred_element_type=jnp.float32).astype(jnp.bfloat16)
     parts = width // LANES
     for k in range(parts):
-        out_ref[:, k * most : (k + 1) * most, :] = placed[
+        out_ref[:, k * LANES : (k + 1) * LANES, :] = placed[
             :, k * LANES : (k + 1) * LANES
-        ].reshape(tiles, most, LANES)
-    out_ref[:, parts * most :, :] = jnp.broadcast_to(
-        labels.reshape(tiles, 1, LANES), (tiles, LABEL_ROWS, LANES)
+        ].reshape(inner, LANES, LANES)
+    out_ref[:, parts * LANES :, :] = jnp.broadcast_to(
+        labels.reshape(inner, 1, LANES), (inner, LABEL_ROWS, LANES)
     ).astype(jnp.bfloat16)
 
 
-def sums_kernel(most, got_ref, out_ref):
-    tiles = got_ref.shape[0]
-    parts = out_ref.shape[1] // LANES
-    group = LANES // most
-    marks = got_ref[:, parts * most :, :].astype(jnp.float32)[:, 0, :]
-    index = lax.broadcasted_iota(jnp.int32, (COL_DEV, LANES), 0) + 1
-    total = [jnp.zeros((COL_DEV, LANES), jnp.float32) for _ in range(parts)]
-    for g in range(tiles // group):
-        label = jnp.sum(marks[g * group : (g + 1) * group], axis=0, keepdims=True)
-        chosen = as_bf16(index == label.astype(jnp.int32))
-        for k in range(parts):
-            block = got_ref[g * group : (g + 1) * group, k * most : (k + 1) * most, :]
-            total[k] += jnp.dot(
-                chosen, block.reshape(LANES, LANES), preferred_element_type=jnp.float32
-            )
+def blocks_kernel(most, me_ref, got_ref, *out_refs):
+    inner = got_ref.shape[0]
+    outer = len(out_refs)
+    parts = out_refs[0].shape[1] // LANES
+    marks = got_ref[:, parts * LANES :, :].astype(jnp.float32)[:, 0, :].astype(jnp.int32)
+    lane = lax.broadcasted_iota(jnp.int32, (inner, LANES), 1)
+    turn = lax.shift_right_arithmetic(lane, most.bit_length() - 1) - me_ref[0]
+    turn = jnp.where(turn < 0, turn + outer, turn)
+    code = jnp.where(marks > 0, turn * COL_DEV + marks - 1, -1)
+    index = lax.broadcasted_iota(jnp.int32, (outer * COL_DEV, LANES), 0)
+    chosen = jnp.concatenate(
+        [as_bf16(index == code[s : s + 1, :]) for s in range(inner)], axis=1
+    )
     for k in range(parts):
-        out_ref[:, k * LANES : (k + 1) * LANES] = total[k]
+        block = got_ref[:, k * LANES : (k + 1) * LANES, :].reshape(inner * LANES, LANES)
+        total = jnp.dot(chosen, block, preferred_element_type=jnp.float32)
+        for d in range(outer):
+            out_refs[d][:, k * LANES : (k + 1) * LANES] = total[
+                d * COL_DEV : (d + 1) * COL_DEV
+            ].astype(jnp.bfloat16)
 
 
 def per_device(
@@ -160,15 +165,16 @@
     hid = inner_weight.shape[1]
     chan = radiances.shape[1]
     most = max(2, 2 * rows // tiles)
-    high = width // LANES * most + LABEL_ROWS
+    inner = INNER
+    outer = tiles // inner
+    high = width + LABEL_ROWS
     vmem = pl.BlockSpec(memory_space=pltpu.VMEM)
     smem = pl.BlockSpec(memory_space=pltpu.SMEM)
     anywhere = pl.BlockSpec(memory_space=pl.ANY)
-    me = lax.axis_index("tile").astype(jnp.int32).reshape(1)
     bucket = pl.pallas_call(
-        functools.partial(rows_kernel, most),
-        out_shape=jax.ShapeDtypeStruct((tiles, high, LANES), jnp.bfloat16),
-        in_specs=[smem, smem, vmem, vmem] + [anywhere] * 7,
+        functools.partial(rows_kernel, tiles, most),
+        out_shape=jax.ShapeDtypeStruct((inner, high, LANES), jnp.bfloat16),
+        in_specs=[smem, vmem, vmem] + [anywhere] * 7,
         out_specs=vmem,
         scratch_shapes=[
             pltpu.VMEM((rows, width), jnp.bfloat16),
@@ -185,7 +191,6 @@
         compiler_params=pltpu.CompilerParams(vmem_limit_bytes=60 * 1024 * 1024),
         name="rows_kernel",
     )(
-        me,
         counts,
         owner.reshape(1, rows),
         column.reshape(1, rows),
@@ -197,15 +202,24 @@
         outer_bias.reshape(1, chan),
         channel_weight.reshape(1, chan),
     )
-    got = lax.all_to_all(bucket, "tile", split_axis=0, concat_axis=0, tiled=True)
-    return pl.pallas_call(
-        functools.partial(sums_kernel, most),
-        out_shape=jax.ShapeDtypeStruct((COL_DEV, width), jnp.float32),
-        in_specs=[vmem],
-        out_specs=vmem,
-        compiler_params=pltpu.CompilerParams(vmem_limit_bytes=16 * 1024 * 1024),
-        name="sums_kernel",
-    )(got)
+    planes = [[o * inner + i for i in range(inner)] for o in range(outer)]
+    got = lax.all_to_all(
+        bucket, "tile", split_axis=0, concat_axis=0, axis_index_groups=planes, tiled=True
+    )
+    me = lax.div(lax.axis_index("tile"), inner).astype(jnp.int32).reshape(1)
+    blocks = pl.pallas_call(
+        functools.partial(blocks_kernel, most),
+        out_shape=[jax.ShapeDtypeStruct((COL_DEV, width), jnp.bfloat16)] * outer,
+        in_specs=[smem, vmem],
+        out_specs=[vmem] * outer,
+        compiler_params=pltpu.CompilerParams(vmem_limit_bytes=24 * 1024 * 1024),
+        name="blocks_kernel",
+    )(me, got)
+    total = blocks[0].astype(jnp.float32)
+    for d in range(1, outer):
+        pairs = [(t, (t + d * inner) % tiles) for t in range(tiles)]
+        total = total + lax.ppermute(blocks[d], "tile", pairs).astype(jnp.float32)
+    return total
 
 
 def solution(mesh):

time: 45.1 us -> 44.1 us (0.978)
  blocking collectives: 29.3 us -> 0 us
  waiting for transfers between devices: 0 us -> 16.7 us
  starting transfers between devices: 0 us -> 10.7 us
  other arithmetic: 0 us -> 0.73 us
    all_to_all x1 -> x0, blocking collectives: 29.3 us -> none  [per_device(): lax.all_to_all(bucket, 'tile', split_axis=0, concat_axis=0, tiled=True)]
    all_to_all x0 -> x1, waiting for transfers between devices: none -> 12.8 us  [per_device(): lax.all_to_all(bucket, 'tile', split_axis=0, concat_axis=0, axis_index_gr...]
    ppermute x0 -> x3, starting transfers between devices: none -> 5.56 us  [per_device(): total = total + lax.ppermute(blocks[d], 'tile', pairs).astype(jnp.float32)]
    all_to_all x0 -> x1, starting transfers between devices: none -> 5.19 us  [per_device(): lax.all_to_all(bucket, 'tile', split_axis=0, concat_axis=0, axis_index_gr...]
    ppermute x0 -> x3, waiting for transfers between devices: none -> 3.95 us  [per_device(): total = total + lax.ppermute(blocks[d], 'tile', pairs).astype(jnp.float32)]
    add x0 -> x1, other arithmetic: none -> 0.73 us  [per_device(): total = total + lax.ppermute(blocks[d], 'tile', pairs).astype(jnp.float32)]
  transfers between devices with their start and end apart: 0 -> 4, of which waited for: 0 -> 4; matrix products, arithmetic and copies ran while one was open for 0% -> 0% of each run, Pallas kernels for 0% -> 0%
where the time goes in v3:
time: 44.1 us; the launch traced here: 43.6 us
  waiting for transfers between devices  16.7 us (38%)
  Pallas kernels  14.8 us (34%)
  starting transfers between devices  10.7 us (24%)
  other arithmetic  0.73 us (2%)
  between operations  0.67 us (2%)
    pallas_call x1, Pallas kernels, per_device(): pl.pallas_call(functools.partial(rows_kernel, tiles, most), out_shape=jax...  13.8 us
    all_to_all x1, waiting for transfers between devices, per_device(): lax.all_to_all(bucket, 'tile', split_axis=0, concat_axis=0, axis_index_gr...  12.8 us
    ppermute x3, starting transfers between devices, per_device(): total = total + lax.ppermute(blocks[d], 'tile', pairs).astype(jnp.float32)  5.56 us
    all_to_all x1, starting transfers between devices, per_device(): lax.all_to_all(bucket, 'tile', split_axis=0, concat_axis=0, axis_index_gr...  5.19 us
    ppermute x3, waiting for transfers between devices, per_device(): total = total + lax.ppermute(blocks[d], 'tile', pairs).astype(jnp.float32)  3.95 us
    pallas_call x1, Pallas kernels, per_device(): pl.pallas_call(functools.partial(blocks_kernel, most), out_shape=[jax.Sha...  0.98 us
  transfers between devices with their start and end apart: 4, of which 4 were waited for; matrix products, arithmetic and copies ran while one was open for 0% of the time, Pallas kernels for 0%

profile of v3, /device:TPU:0, one launch (start us, length us, event | category | flops | bytes accessed | tf_op | source)
XLA Modules:
  0.0 43.6 jit_solution(6961779902990523528)
XLA Ops:
  0.7 13.8 %rows_kernel.1 = bf16[8,392,128]{2,1,0:T(8,128)(2,1)} custom-call(s32[1]{0:T(128)S(6)} %copy.11.count_ref, s32[1,512]{1,0:T(1,128)} %bitcast.7, s32[1,512]{1,0:T(1,128)} %bitcast.8, bf16[512,384]{1,0:T(8,128)(2,1)} %prof_hbm.1, bf16[512,512]{1,0:T(8,128)(2,1)} %rad_hbm.1, bf16[384,4096]{1,0:T(8,128)(2,1)} %w1_hbm.1, f32[1,4096]{1,0:T(1,128)} %bitcast.6, ...), custom_call_target="tpu_custom_call" | custom-call | tf_op jit(solution)/shard_map/rows_kernel/pallas_call | solution.py:174
  14.4 5.2 %all-to-all-start = ((bf16[8,392,128]{2,1,0:T(8,128)(2,1)}), bf16[8,392,128]{2,1,0:T(8,128)(2,1)S(1)}, u32[]{:S(2)}, u32[]{:S(2)}) async-start(bf16[8,392,128]{2,1,0:T(8,128)(2,1)} %rows_kernel.1), calls=%async_computation | async-start | bytes 1605632 | tf_op jit(solution)/shard_map/all_to_all | solution.py:206
  19.6 12.8 %all-to-all-done.got_ref = bf16[8,392,128]{2,1,0:T(8,128)(2,1)S(1)} async-done(((bf16[8,392,128]{2,1,0:T(8,128)(2,1)}), bf16[8,392,128]{2,1,0:T(8,128)(2,1)S(1)}, u32[]{:S(2)}, u32[]{:S(2)}) %all-to-all-start) | async-done | bytes 802848 | tf_op jit(solution)/shard_map/all_to_all | solution.py:206
  32.4 1.0 %blocks_kernel.1 = (bf16[128,384]{1,0:T(8,128)(2,1)S(1)}, bf16[128,384]{1,0:T(8,128)(2,1)S(1)}, bf16[128,384]{1,0:T(8,128)(2,1)S(1)}, bf16[128,384]{1,0:T(8,128)(2,1)S(1)}) custom-call(s32[1]{0:T(128)} %bitcast.me_ref, bf16[8,392,128]{2,1,0:T(8,128)(2,1)S(1)} %all-to-all-done.got_ref), custom_call_target="tpu_custom_call" | custom-call | tf_op jit(solution)/shard_map/blocks_kernel/pallas_call | solution.py:210
  33.4 1.6 %collective-permute-start = (bf16[128,384]{1,0:T(8,128)(2,1)S(1)}, bf16[128,384]{1,0:T(8,128)(2,1)S(1)}, u32[]{:S(2)}, u32[]{:S(2)}) collective-permute-start(bf16[128,384]{1,0:T(8,128)(2,1)S(1)} %get-tuple-element.10), channel_id=1, source_target_pairs={{0,8},{1,9},{2,10},{3,11},{4,12},{5,13},{6,14},{7,15},{8,16},{9,17... | collective-permute-start | bytes 294920 | tf_op jit(solution)/shard_map/ppermute | solution.py:221
  35.0 2.6 %collective-permute-start.1 = (bf16[128,384]{1,0:T(8,128)(2,1)S(1)}, bf16[128,384]{1,0:T(8,128)(2,1)S(1)}, u32[]{:S(2)}, u32[]{:S(2)}) collective-permute-start(bf16[128,384]{1,0:T(8,128)(2,1)S(1)} %get-tuple-element.11), channel_id=1, source_target_pairs={{0,16},{1,17},{2,18},{3,19},{4,20},{5,21},{6,22},{7,23},{8,24},{9,... | collective-permute-start | bytes 294920 | tf_op jit(solution)/shard_map/ppermute | solution.py:221
  37.6 1.3 %collective-permute-start.2 = (bf16[128,384]{1,0:T(8,128)(2,1)S(1)}, bf16[128,384]{1,0:T(8,128)(2,1)S(1)}, u32[]{:S(2)}, u32[]{:S(2)}) collective-permute-start(bf16[128,384]{1,0:T(8,128)(2,1)S(1)} %get-tuple-element.12), channel_id=1, source_target_pairs={{0,24},{1,25},{2,26},{3,27},{4,28},{5,29},{6,30},{7,31},{8,0},{9,1... | collective-permute-start | bytes 294920 | tf_op jit(solution)/shard_map/ppermute | solution.py:221
  39.0 1.0 %collective-permute-done = bf16[128,384]{1,0:T(8,128)(2,1)S(1)} collective-permute-done((bf16[128,384]{1,0:T(8,128)(2,1)S(1)}, bf16[128,384]{1,0:T(8,128)(2,1)S(1)}, u32[]{:S(2)}, u32[]{:S(2)}) %collective-permute-start) | collective-permute-done | bytes 98336 | tf_op jit(solution)/shard_map/ppermute | solution.py:221
  40.0 2.5 %collective-permute-done.1 = bf16[128,384]{1,0:T(8,128)(2,1)S(1)} collective-permute-done((bf16[128,384]{1,0:T(8,128)(2,1)S(1)}, bf16[128,384]{1,0:T(8,128)(2,1)S(1)}, u32[]{:S(2)}, u32[]{:S(2)}) %collective-permute-start.1) | collective-permute-done | bytes 98336 | tf_op jit(solution)/shard_map/ppermute | solution.py:221
  42.4 0.5 %collective-permute-done.2 = bf16[128,384]{1,0:T(8,128)(2,1)S(1)} collective-permute-done((bf16[128,384]{1,0:T(8,128)(2,1)S(1)}, bf16[128,384]{1,0:T(8,128)(2,1)S(1)}, u32[]{:S(2)}, u32[]{:S(2)}) %collective-permute-start.2) | collective-permute-done | bytes 98336 | tf_op jit(solution)/shard_map/ppermute | solution.py:221
  42.9 0.7 %convert_add_fusion = f32[128,384]{1,0:T(8,128)} fusion(bf16[128,384]{1,0:T(8,128)(2,1)S(1)} %collective-permute-done.2, bf16[128,384]{1,0:T(8,128)(2,1)S(1)} %collective-permute-done.1, bf16[128,384]{1,0:T(8,128)(2,1)S(1)} %collective-permute-done, bf16[128,384]{1,0:T(8,128)(2,1)S(1)} %get-tuple-element.9), kind=kLoop, calls=%fused_computation | loop fusion | flops 344064 | bytes 589824 | tf_op jit(solution)/shard_map/add | solution.py:221
Async XLA Ops:
  14.4 18.0 %all-to-all-start = ((bf16[8,392,128]{2,1,0:T(8,128)(2,1)}), bf16[8,392,128]{2,1,0:T(8,128)(2,1)S(1)}, u32[]{:S(2)}, u32[]{:S(2)}) async-start(bf16[8,392,128]{2,1,0:T(8,128)(2,1)} %rows_kernel.1), calls=%async_computation | async-start | bytes 1605632 | tf_op jit(solution)/shard_map/all_to_all | solution.py:206
  33.4 6.6 %collective-permute-start = (bf16[128,384]{1,0:T(8,128)(2,1)S(1)}, bf16[128,384]{1,0:T(8,128)(2,1)S(1)}, u32[]{:S(2)}, u32[]{:S(2)}) collective-permute-start(bf16[128,384]{1,0:T(8,128)(2,1)S(1)} %get-tuple-element.10), channel_id=1, source_target_pairs={{0,8},{1,9},{2,10},{3,11},{4,12},{5,13},{6,14},{7,15},{8,16},{9,17... | collective-permute-start | bytes 294920 | tf_op jit(solution)/shard_map/ppermute | solution.py:221
  35.0 7.4 %collective-permute-start.1 = (bf16[128,384]{1,0:T(8,128)(2,1)S(1)}, bf16[128,384]{1,0:T(8,128)(2,1)S(1)}, u32[]{:S(2)}, u32[]{:S(2)}) collective-permute-start(bf16[128,384]{1,0:T(8,128)(2,1)S(1)} %get-tuple-element.11), channel_id=1, source_target_pairs={{0,16},{1,17},{2,18},{3,19},{4,20},{5,21},{6,22},{7,23},{8,24},{9,... | collective-permute-start | bytes 294920 | tf_op jit(solution)/shard_map/ppermute | solution.py:221
  37.6 5.3 %collective-permute-start.2 = (bf16[128,384]{1,0:T(8,128)(2,1)S(1)}, bf16[128,384]{1,0:T(8,128)(2,1)S(1)}, u32[]{:S(2)}, u32[]{:S(2)}) collective-permute-start(bf16[128,384]{1,0:T(8,128)(2,1)S(1)} %get-tuple-element.12), channel_id=1, source_target_pairs={{0,24},{1,25},{2,26},{3,27},{4,28},{5,29},{6,30},{7,31},{8,0},{9,1... | collective-permute-start | bytes 294920 | tf_op jit(solution)/shard_map/ppermute | solution.py:221

commit v4 on v3

--- a/solution.py
+++ b/solution.py
@@ -11,7 +11,7 @@
 CHUNK = 512
 LANES = 128
 LABEL_ROWS = 8
-INNER = 8
+OUTER = 2
 NT = (((1,), (1,)), ((), ()))
 
 
@@ -22,6 +22,7 @@
 def rows_kernel(
     tiles,
     most,
+    me_ref,
     count_ref,
     owner_ref,
     column_ref,
@@ -76,10 +77,12 @@
     )
     running = jnp.dot(one_hot.astype(jnp.bfloat16), upper, preferred_element_type=jnp.float32)
     rank = jnp.sum(running * one_hot, axis=0, keepdims=True).astype(jnp.int32) - 1
+    pool = tiles // inner * most
     place = owner & (inner - 1)
-    lane = lax.shift_right_arithmetic(owner, inner.bit_length() - 1) * most + rank
-    slot = jnp.where(live, place * LANES + lane, -1)
-    placing = as_bf16(lax.broadcasted_iota(jnp.int32, (inner * LANES, rows), 0) == slot)
+    order = lax.shift_right_arithmetic(owner, inner.bit_length() - 1) * most + rank
+    slot = jnp.where(live, place * pool + order, -1)
+    placing = as_bf16(lax.broadcasted_iota(jnp.int32, (inner * pool, rows), 0) == slot)
+    lane = order + lax.rem(me_ref[0], LANES // pool) * pool
     lane_hot = as_bf16(lax.broadcasted_iota(jnp.int32, (LANES, rows), 0) == lane)
     here = live & (lax.broadcasted_iota(jnp.int32, (inner, rows), 0) == place)
     marked = jnp.where(here, (column_ref[...] + 1).astype(jnp.float32), 0.0)
@@ -118,34 +121,38 @@
     placed = jnp.dot(placing, grads, preferred_element_type=jnp.float32).astype(jnp.bfloat16)
     parts = width // LANES
     for k in range(parts):
-        out_ref[:, k * LANES : (k + 1) * LANES, :] = placed[
+        out_ref[:, k * pool : (k + 1) * pool, :] = placed[
             :, k * LANES : (k + 1) * LANES
-        ].reshape(inner, LANES, LANES)
-    out_ref[:, parts * LANES :, :] = jnp.broadcast_to(
+        ].reshape(inner, pool, LANES)
+    out_ref[:, parts * pool :, :] = jnp.broadcast_to(
         labels.reshape(inner, 1, LANES), (inner, LABEL_ROWS, LANES)
     ).astype(jnp.bfloat16)
 
 
-def blocks_kernel(most, me_ref, got_ref, *out_refs):
+def blocks_kernel(tiles, most, me_ref, got_ref, own_ref, other_ref):
     inner = got_ref.shape[0]
-    outer = len(out_refs)
-    parts = out_refs[0].shape[1] // LANES
-    marks = got_ref[:, parts * LANES :, :].astype(jnp.float32)[:, 0, :].astype(jnp.int32)
-    lane = lax.broadcasted_iota(jnp.int32, (inner, LANES), 1)
-    turn = lax.shift_right_arithmetic(lane, most.bit_length() - 1) - me_ref[0]
-    turn = jnp.where(turn < 0, turn + outer, turn)
-    code = jnp.where(marks > 0, turn * COL_DEV + marks - 1, -1)
+    outer = tiles // inner
+    pool = outer * most
+    group = LANES // pool
+    parts = own_ref.shape[1] // LANES
+    marks = got_ref[:, parts * pool :, :].astype(jnp.float32)[:, 0, :]
     index = lax.broadcasted_iota(jnp.int32, (outer * COL_DEV, LANES), 0)
-    chosen = jnp.concatenate(
-        [as_bf16(index == code[s : s + 1, :]) for s in range(inner)], axis=1
-    )
+    lane = lax.broadcasted_iota(jnp.int32, (1, LANES), 1) & (pool - 1)
+    turn = lax.shift_right_arithmetic(lane, most.bit_length() - 1) ^ (
+        lax.shift_right_arithmetic(me_ref[0], inner.bit_length() - 1)
+    )
+    chosen = []
+    for g in range(inner // group):
+        label = jnp.sum(marks[g * group : (g + 1) * group], axis=0, keepdims=True)
+        label = label.astype(jnp.int32)
+        code = jnp.where(label > 0, turn * COL_DEV + label - 1, -1)
+        chosen.append(as_bf16(index == code))
+    chosen = jnp.concatenate(chosen, axis=1)
     for k in range(parts):
-        block = got_ref[:, k * LANES : (k + 1) * LANES, :].reshape(inner * LANES, LANES)
+        block = got_ref[:, k * pool : (k + 1) * pool, :].reshape(inner * pool, LANES)
         total = jnp.dot(chosen, block, preferred_element_type=jnp.float32)
-        for d in range(outer):
-            out_refs[d][:, k * LANES : (k + 1) * LANES] = total[
-                d * COL_DEV : (d + 1) * COL_DEV
-            ].astype(jnp.bfloat16)
+        own_ref[:, k * LANES : (k + 1) * LANES] = total[:COL_DEV]
+        other_ref[:, k * LANES : (k + 1) * LANES] = total[COL_DEV:].astype(jnp.bfloat16)
 
 
 def per_device(
@@ -165,16 +172,17 @@
     hid = inner_weight.shape[1]
     chan = radiances.shape[1]
     most = max(2, 2 * rows // tiles)
-    inner = INNER
-    outer = tiles // inner
-    high = width + LABEL_ROWS
+    inner = tiles // OUTER
+    pool = OUTER * most
+    high = width // LANES * pool + LABEL_ROWS
+    me = lax.axis_index("tile").astype(jnp.int32).reshape(1)
     vmem = pl.BlockSpec(memory_space=pltpu.VMEM)
     smem = pl.BlockSpec(memory_space=pltpu.SMEM)
     anywhere = pl.BlockSpec(memory_space=pl.ANY)
     bucket = pl.pallas_call(
         functools.partial(rows_kernel, tiles, most),
         out_shape=jax.ShapeDtypeStruct((inner, high, LANES), jnp.bfloat16),
-        in_specs=[smem, vmem, vmem] + [anywhere] * 7,
+        in_specs=[smem, smem, vmem, vmem] + [anywhere] * 7,
         out_specs=vmem,
         scratch_shapes=[
             pltpu.VMEM((rows, width), jnp.bfloat16),
@@ -191,6 +199,7 @@
         compiler_params=pltpu.CompilerParams(vmem_limit_bytes=60 * 1024 * 1024),
         name="rows_kernel",
     )(
+        me,
         counts,
         owner.reshape(1, rows),
         column.reshape(1, rows),
@@ -202,24 +211,23 @@
         outer_bias.reshape(1, chan),
         channel_weight.reshape(1, chan),
     )
-    planes = [[o * inner + i for i in range(inner)] for o in range(outer)]
+    halves = [[o * inner + i for i in range(inner)] for o in range(OUTER)]
     got = lax.all_to_all(
-        bucket, "tile", split_axis=0, concat_axis=0, axis_index_groups=planes, tiled=True
-    )
-    me = lax.div(lax.axis_index("tile"), inner).astype(jnp.int32).reshape(1)
-    blocks = pl.pallas_call(
-        functools.partial(blocks_kernel, most),
-        out_shape=[jax.ShapeDtypeStruct((COL_DEV, width), jnp.bfloat16)] * outer,
+        bucket, "tile", split_axis=0, concat_axis=0, axis_index_groups=halves, tiled=True
+    )
+    own, other = pl.pallas_call(
+        functools.partial(blocks_kernel, tiles, most),
+        out_shape=[
+            jax.ShapeDtypeStruct((COL_DEV, width), jnp.float32),
+            jax.ShapeDtypeStruct((COL_DEV, width), jnp.bfloat16),
+        ],
         in_specs=[smem, vmem],
-        out_specs=[vmem] * outer,
+        out_specs=[vmem, vmem],
         compiler_params=pltpu.CompilerParams(vmem_limit_bytes=24 * 1024 * 1024),
         name="blocks_kernel",
     )(me, got)
-    total = blocks[0].astype(jnp.float32)
-    for d in range(1, outer):
-        pairs = [(t, (t + d * inner) % tiles) for t in range(tiles)]
-        total = total + lax.ppermute(blocks[d], "tile", pairs).astype(jnp.float32)
-    return total
+    pairs = [(t, (t + inner) % tiles) for t in range(tiles)]
+    return own + lax.ppermute(other, "tile", pairs).astype(jnp.float32)
 
 
 def solution(mesh):

time: 44.1 us -> 43.1 us (0.977)
  blocking collectives: 0 us -> 20 us
  waiting for transfers between devices: 16.7 us -> 4.46 us
  starting transfers between devices: 10.7 us -> 2.65 us
    all_to_all x0 -> x1, blocking collectives: none -> 20 us  [per_device(): lax.all_to_all(bucket, 'tile', split_axis=0, concat_axis=0, axis_index_gr...]
    all_to_all x1 -> x0, waiting for transfers between devices: 12.8 us -> none  [per_device(): lax.all_to_all(bucket, 'tile', split_axis=0, concat_axis=0, axis_index_gr...]
    all_to_all x1 -> x0, starting transfers between devices: 5.19 us -> none  [per_device(): lax.all_to_all(bucket, 'tile', split_axis=0, concat_axis=0, axis_index_gr...]
    ppermute x3 -> x1, starting transfers between devices: 5.56 us -> 2.65 us  [per_device(): return own + lax.ppermute(other, 'tile', pairs).astype(jnp.float32)]
    ppermute x3 -> x1, waiting for transfers between devices: 3.95 us -> 4.46 us  [per_device(): return own + lax.ppermute(other, 'tile', pairs).astype(jnp.float32)]
  transfers between devices with their start and end apart: 4 -> 1, of which waited for: 4 -> 1; matrix products, arithmetic and copies ran while one was open for 0% -> 0% of each run, Pallas kernels for 0% -> 0%
where the time goes in v4:
time: 43.1 us; the launch traced here: 42.9 us
  blocking collectives  20 us (46%)
  Pallas kernels  14.4 us (33%)
  waiting for transfers between devices  4.46 us (10%)
  starting transfers between devices  2.65 us (6%)
  other arithmetic  0.7 us (2%)
  between operations  0.67 us (2%)
    all_to_all x1, blocking collectives, per_device(): lax.all_to_all(bucket, 'tile', split_axis=0, concat_axis=0, axis_index_gr...  20 us
    pallas_call x1, Pallas kernels, per_device(): pl.pallas_call(functools.partial(rows_kernel, tiles, most), out_shape=jax...  13.8 us
    ppermute x1, waiting for transfers between devices, per_device(): return own + lax.ppermute(other, 'tile', pairs).astype(jnp.float32)  4.46 us
    ppermute x1, starting transfers between devices, per_device(): return own + lax.ppermute(other, 'tile', pairs).astype(jnp.float32)  2.65 us
  transfers between devices with their start and end apart: 1, of which 1 were waited for; matrix products, arithmetic and copies ran while one was open for 0% of the time, Pallas kernels for 0%

profile of v4, /device:TPU:0, one launch (start us, length us, event | category | flops | bytes accessed | tf_op | source)
XLA Modules:
  0.0 42.9 jit_solution(2219789546748736386)
XLA Ops:
  0.7 13.8 %rows_kernel.1 = bf16[16,200,128]{2,1,0:T(8,128)(2,1)} custom-call(s32[1]{0:T(128)} %bitcast.me_ref, s32[1]{0:T(128)S(6)} %copy.11.count_ref, s32[1,512]{1,0:T(1,128)} %bitcast.7, s32[1,512]{1,0:T(1,128)} %bitcast.8, bf16[512,384]{1,0:T(8,128)(2,1)} %prof_hbm.1, bf16[512,512]{1,0:T(8,128)(2,1)} %rad_hbm.1, bf16[384,4096]{1,0:T(8,128)(2,1)} %w1_hbm.1, ...), custom_call_target="tpu_custom_call" | custom-call | tf_op jit(solution)/shard_map/rows_kernel/pallas_call | solution.py:182
  14.4 20.0 %all_to_all.5.got_ref = bf16[16,200,128]{2,1,0:T(8,128)(2,1)S(1)} all-to-all(bf16[16,200,128]{2,1,0:T(8,128)(2,1)} %rows_kernel.1), channel_id=1, replica_groups={{0,1,2,3,4,5,6,7,8,9,10,11,12,13,14,15},{16,17,18,19,20,21,22,23,24,25,..., dimensions={0} | all-to-all | bytes 1638400 | tf_op jit(solution)/shard_map/all_to_all | solution.py:215
  34.5 0.6 %blocks_kernel.1 = (f32[128,384]{1,0:T(8,128)S(1)}, bf16[128,384]{1,0:T(8,128)(2,1)S(1)}) custom-call(s32[1]{0:T(128)} %bitcast.me_ref, bf16[16,200,128]{2,1,0:T(8,128)(2,1)S(1)} %all_to_all.5.got_ref), custom_call_target="tpu_custom_call" | custom-call | tf_op jit(solution)/shard_map/blocks_kernel/pallas_call | solution.py:218
  35.1 2.6 %collective-permute-start = (bf16[128,384]{1,0:T(8,128)(2,1)S(1)}, bf16[128,384]{1,0:T(8,128)(2,1)S(1)}, u32[]{:S(2)}, u32[]{:S(2)}) collective-permute-start(bf16[128,384]{1,0:T(8,128)(2,1)S(1)} %get-tuple-element.8), channel_id=1, source_target_pairs={{0,16},{1,17},{2,18},{3,19},{4,20},{5,21},{6,22},{7,23},{8,24},{9,... | collective-permute-start | bytes 294920 | tf_op jit(solution)/shard_map/ppermute | solution.py:230
  37.7 4.5 %collective-permute-done = bf16[128,384]{1,0:T(8,128)(2,1)S(1)} collective-permute-done((bf16[128,384]{1,0:T(8,128)(2,1)S(1)}, bf16[128,384]{1,0:T(8,128)(2,1)S(1)}, u32[]{:S(2)}, u32[]{:S(2)}) %collective-permute-start) | collective-permute-done | bytes 98336 | tf_op jit(solution)/shard_map/ppermute | solution.py:230
  42.2 0.7 %convert_add_fusion = f32[128,384]{1,0:T(8,128)} fusion(f32[128,384]{1,0:T(8,128)S(1)} %get-tuple-element.7, bf16[128,384]{1,0:T(8,128)(2,1)S(1)} %collective-permute-done), kind=kLoop, calls=%fused_computation | loop fusion | flops 98304 | bytes 491520 | tf_op jit(solution)/shard_map/add | solution.py:230
Async XLA Ops:
  35.1 7.1 %collective-permute-start = (bf16[128,384]{1,0:T(8,128)(2,1)S(1)}, bf16[128,384]{1,0:T(8,128)(2,1)S(1)}, u32[]{:S(2)}, u32[]{:S(2)}) collective-permute-start(bf16[128,384]{1,0:T(8,128)(2,1)S(1)} %get-tuple-element.8), channel_id=1, source_target_pairs={{0,16},{1,17},{2,18},{3,19},{4,20},{5,21},{6,22},{7,23},{8,24},{9,... | collective-permute-start | bytes 294920 | tf_op jit(solution)/shard_map/ppermute | solution.py:230

commit v5 on v4

--- a/solution.py
+++ b/solution.py
@@ -41,21 +41,20 @@
     w2_ref,
     b2_ref,
     cw_ref,
-    hidden_ref,
     factor_ref,
+    even_ref,
+    odd_ref,
+    output_ref,
+    grads_ref,
     sems,
+    sems1,
+    sems2,
 ):
     rows, width = prof_ref.shape
-    hid = w1_ref.shape[1]
-    chan = rad_ref.shape[1]
-    half = hid // 2
-    low, high = pl.ds(0, half), pl.ds(half, half)
+    chunks = w1_ref.shape[0]
     pairs = (
         (prof_hbm, prof_ref),
         (b1_hbm, b1_ref),
-        (w1_hbm.at[:, low], w1_ref.at[:, low]),
-        (w1_hbm.at[:, high], w1_ref.at[:, high]),
-        (w2_hbm, w2_ref),
         (rad_hbm, rad_ref),
         (b2_hbm, b2_ref),
         (cw_hbm, cw_ref),
@@ -63,7 +62,29 @@
     copies = [
         pltpu.make_async_copy(src, dst, sems.at[i]) for i, (src, dst) in enumerate(pairs)
     ]
-    for copy in copies:
+
+    def copy1(i):
+        part = pl.ds(pl.multiple_of(i * CHUNK, CHUNK), CHUNK)
+        return pltpu.make_async_copy(w1_hbm.at[:, part], w1_ref.at[i], sems1.at[i])
+
+    def copy2(i):
+        part = pl.ds(pl.multiple_of(i * CHUNK, CHUNK), CHUNK)
+        return pltpu.make_async_copy(w2_hbm.at[part, :], w2_ref.at[i], sems2.at[i])
+
+    copies[0].start()
+    copies[1].start()
+    copy1(0).start()
+    copy1(1).start()
+    copy2(0).start()
+
+    def start_rest(i, carry):
+        copy1(i + 1).start()
+        copy2(i).start()
+        return carry
+
+    lax.fori_loop(1, chunks - 1, start_rest, 0)
+    copy2(chunks - 1).start()
+    for copy in copies[2:]:
         copy.start()
 
     inner = out_ref.shape[0]
@@ -92,32 +113,76 @@
 
     copies[0].wait()
     copies[1].wait()
-    prof = (prof_ref[...].astype(jnp.float32) * 0.5).astype(jnp.bfloat16)
-    for i in range(hid // CHUNK):
-        part = pl.ds(i * CHUNK, CHUNK)
-        if i == 0:
-            copies[2].wait()
-        if i == hid // CHUNK // 2:
-            copies[3].wait()
-        u = jnp.dot(prof, w1_ref[:, part], preferred_element_type=jnp.float32)
-        u = u + 0.5 * b1_ref[:, part]
+    prof_ref[...] = (prof_ref[...].astype(jnp.float32) * 0.5).astype(jnp.bfloat16)
+
+    def enter(i, half_ref):
+        half_ref[...] = jnp.dot(prof_ref[...], w1_ref[i], preferred_element_type=jnp.float32)
+
+    def leave(i, half_ref):
+        u = half_ref[...] + 0.5 * b1_ref[i]
         p = jnp.tanh(u) + 1.0
         hidden = u * p
-        hidden_ref[:, part] = hidden.astype(jnp.bfloat16)
-        factor_ref[:, part] = p + hidden * (2.0 - p)
-    for copy in copies[4:]:
+        factor_ref[i] = p + hidden * (2.0 - p)
+        output_ref[...] += jnp.dot(
+            hidden.astype(jnp.bfloat16), w2_ref[i], preferred_element_type=jnp.float32
+        )
+
+    def forward_pair(j, carry):
+        i = 2 * j
+        copy1(i + 1).wait()
+        copy2(i).wait()
+        enter(i + 1, odd_ref)
+        leave(i, even_ref)
+        copy1(i + 2).wait()
+        copy2(i + 1).wait()
+        enter(i + 2, even_ref)
+        leave(i + 1, odd_ref)
+        return carry
+
+    output_ref[...] = jnp.zeros_like(output_ref)
+    copy1(0).wait()
+    enter(0, even_ref)
+    lax.fori_loop(0, chunks // 2 - 1, forward_pair, 0)
+    copy1(chunks - 1).wait()
+    copy2(chunks - 2).wait()
+    enter(chunks - 1, odd_ref)
+    leave(chunks - 2, even_ref)
+    copy2(chunks - 1).wait()
+    for copy in copies[2:]:
         copy.wait()
-    output = jnp.dot(hidden_ref[...], w2_ref[...], preferred_element_type=jnp.float32)
-    misfit = (0.5 * cw_ref[...]) * (output + b2_ref[...] - rad_ref[...].astype(jnp.float32))
+    leave(chunks - 1, odd_ref)
+
+    misfit = output_ref[...] + b2_ref[...] - rad_ref[...].astype(jnp.float32)
+    misfit = (0.5 * cw_ref[...]) * misfit
     alive = lax.broadcasted_iota(jnp.int32, (rows, 1), 0) < count_ref[0]
-    misfit = jnp.where(alive, misfit, 0.0).astype(jnp.bfloat16)
-    for i in range(hid // CHUNK):
-        part = pl.ds(i * CHUNK, CHUNK)
-        back = lax.dot_general(misfit, w2_ref[part, :], NT, preferred_element_type=jnp.float32)
-        hidden_ref[:, part] = (back * factor_ref[:, part]).astype(jnp.bfloat16)
-    grads = lax.dot_general(
-        hidden_ref[...], w1_ref[...], NT, preferred_element_type=jnp.float32
-    ).astype(jnp.bfloat16)
+    rad_ref[...] = jnp.where(alive, misfit, 0.0).astype(jnp.bfloat16)
+
+    def enter_back(i, half_ref):
+        half_ref[...] = lax.dot_general(
+            rad_ref[...], w2_ref[i], NT, preferred_element_type=jnp.float32
+        )
+
+    def leave_back(i, half_ref):
+        slope = (half_ref[...] * factor_ref[i]).astype(jnp.bfloat16)
+        grads_ref[...] += lax.dot_general(
+            slope, w1_ref[i], NT, preferred_element_type=jnp.float32
+        )
+
+    def backward_pair(j, carry):
+        i = 2 * j
+        enter_back(i + 1, odd_ref)
+        leave_back(i, even_ref)
+        enter_back(i + 2, even_ref)
+        leave_back(i + 1, odd_ref)
+        return carry
+
+    grads_ref[...] = jnp.zeros_like(grads_ref)
+    enter_back(0, even_ref)
+    lax.fori_loop(0, chunks // 2 - 1, backward_pair, 0)
+    enter_back(chunks - 1, odd_ref)
+    leave_back(chunks - 2, even_ref)
+    leave_back(chunks - 1, odd_ref)
+    grads = grads_ref[...].astype(jnp.bfloat16)
     placed = jnp.dot(placing, grads, preferred_element_type=jnp.float32).astype(jnp.bfloat16)
     parts = width // LANES
     for k in range(parts):
@@ -172,6 +237,7 @@
     hid = inner_weight.shape[1]
     chan = radiances.shape[1]
     most = max(2, 2 * rows // tiles)
+    chunks = hid // CHUNK
     inner = tiles // OUTER
     pool = OUTER * most
     high = width // LANES * pool + LABEL_ROWS
@@ -187,14 +253,19 @@
         scratch_shapes=[
             pltpu.VMEM((rows, width), jnp.bfloat16),
             pltpu.VMEM((rows, chan), jnp.bfloat16),
-            pltpu.VMEM((width, hid), jnp.bfloat16),
-            pltpu.VMEM((1, hid), jnp.float32),
-            pltpu.VMEM((hid, chan), jnp.bfloat16),
+            pltpu.VMEM((chunks, width, CHUNK), jnp.bfloat16),
+            pltpu.VMEM((chunks, 1, CHUNK), jnp.float32),
+            pltpu.VMEM((chunks, CHUNK, chan), jnp.bfloat16),
             pltpu.VMEM((1, chan), jnp.float32),
             pltpu.VMEM((1, chan), jnp.float32),
-            pltpu.VMEM((rows, hid), jnp.bfloat16),
-            pltpu.VMEM((rows, hid), jnp.float32),
-            pltpu.SemaphoreType.DMA((8,)),
+            pltpu.VMEM((chunks, rows, CHUNK), jnp.float32),
+            pltpu.VMEM((rows, CHUNK), jnp.float32),
+            pltpu.VMEM((rows, CHUNK), jnp.float32),
+            pltpu.VMEM((rows, chan), jnp.float32),
+            pltpu.VMEM((rows, width), jnp.float32),
+            pltpu.SemaphoreType.DMA((5,)),
+            pltpu.SemaphoreType.DMA((chunks,)),
+            pltpu.SemaphoreType.DMA((chunks,)),
         ],
         compiler_params=pltpu.CompilerParams(vmem_limit_bytes=60 * 1024 * 1024),
         name="rows_kernel",
@@ -206,7 +277,7 @@
         profiles,
         radiances,
         inner_weight,
-        inner_bias.reshape(1, hid),
+        inner_bias.reshape(chunks, 1, CHUNK),
         outer_weight,
         outer_bias.reshape(1, chan),
         channel_weight.reshape(1, chan),

time: 43.1 us -> 43.9 us (1.019)
  Pallas kernels: 14.4 us -> 15.1 us
    pallas_call x1, Pallas kernels: 13.8 us -> 14.5 us  [per_device(): pl.pallas_call(functools.partial(rows_kernel, tiles, most), out_shape=jax...]
where the time goes in v5:
time: 43.9 us; the launch traced here: 43.6 us
  blocking collectives  20 us (46%)
  Pallas kernels  15.1 us (34%)
  waiting for transfers between devices  4.46 us (10%)
  starting transfers between devices  2.65 us (6%)
  other arithmetic  0.7 us (2%)
  between operations  0.67 us (2%)
    all_to_all x1, blocking collectives, per_device(): lax.all_to_all(bucket, 'tile', split_axis=0, concat_axis=0, axis_index_gr...  20 us
    pallas_call x1, Pallas kernels, per_device(): pl.pallas_call(functools.partial(rows_kernel, tiles, most), out_shape=jax...  14.5 us
    ppermute x1, waiting for transfers between devices, per_device(): return own + lax.ppermute(other, 'tile', pairs).astype(jnp.float32)  4.46 us
    ppermute x1, starting transfers between devices, per_device(): return own + lax.ppermute(other, 'tile', pairs).astype(jnp.float32)  2.65 us
  transfers between devices with their start and end apart: 1, of which 1 were waited for; matrix products, arithmetic and copies ran while one was open for 0% of the time, Pallas kernels for 0%

profile of v5, /device:TPU:0, one launch (start us, length us, event | category | flops | bytes accessed | tf_op | source)
XLA Modules:
  0.0 43.6 jit_solution(4212525071437567197)
XLA Ops:
  0.7 14.5 %rows_kernel.1 = bf16[16,200,128]{2,1,0:T(8,128)(2,1)} custom-call(s32[1]{0:T(128)} %bitcast.me_ref, s32[1]{0:T(128)S(6)} %copy.11.count_ref, s32[1,512]{1,0:T(1,128)} %bitcast.7, s32[1,512]{1,0:T(1,128)} %bitcast.8, bf16[512,384]{1,0:T(8,128)(2,1)} %prof_hbm.1, bf16[512,512]{1,0:T(8,128)(2,1)} %rad_hbm.1, bf16[384,4096]{1,0:T(8,128)(2,1)} %w1_hbm.1, ...), custom_call_target="tpu_custom_call" | custom-call | tf_op jit(solution)/shard_map/rows_kernel/pallas_call | solution.py:248
  15.2 20.0 %all_to_all.5.got_ref = bf16[16,200,128]{2,1,0:T(8,128)(2,1)S(1)} all-to-all(bf16[16,200,128]{2,1,0:T(8,128)(2,1)} %rows_kernel.1), channel_id=1, replica_groups={{0,1,2,3,4,5,6,7,8,9,10,11,12,13,14,15},{16,17,18,19,20,21,22,23,24,25,..., dimensions={0} | all-to-all | bytes 1638400 | tf_op jit(solution)/shard_map/all_to_all | solution.py:286
  35.2 0.6 %blocks_kernel.1 = (f32[128,384]{1,0:T(8,128)S(1)}, bf16[128,384]{1,0:T(8,128)(2,1)S(1)}) custom-call(s32[1]{0:T(128)} %bitcast.me_ref, bf16[16,200,128]{2,1,0:T(8,128)(2,1)S(1)} %all_to_all.5.got_ref), custom_call_target="tpu_custom_call" | custom-call | tf_op jit(solution)/shard_map/blocks_kernel/pallas_call | solution.py:289
  35.8 2.6 %collective-permute-start = (bf16[128,384]{1,0:T(8,128)(2,1)S(1)}, bf16[128,384]{1,0:T(8,128)(2,1)S(1)}, u32[]{:S(2)}, u32[]{:S(2)}) collective-permute-start(bf16[128,384]{1,0:T(8,128)(2,1)S(1)} %get-tuple-element.8), channel_id=1, source_target_pairs={{0,16},{1,17},{2,18},{3,19},{4,20},{5,21},{6,22},{7,23},{8,24},{9,... | collective-permute-start | bytes 294920 | tf_op jit(solution)/shard_map/ppermute | solution.py:301
  38.5 4.5 %collective-permute-done = bf16[128,384]{1,0:T(8,128)(2,1)S(1)} collective-permute-done((bf16[128,384]{1,0:T(8,128)(2,1)S(1)}, bf16[128,384]{1,0:T(8,128)(2,1)S(1)}, u32[]{:S(2)}, u32[]{:S(2)}) %collective-permute-start) | collective-permute-done | bytes 98336 | tf_op jit(solution)/shard_map/ppermute | solution.py:301
  42.9 0.7 %convert_add_fusion = f32[128,384]{1,0:T(8,128)} fusion(f32[128,384]{1,0:T(8,128)S(1)} %get-tuple-element.7, bf16[128,384]{1,0:T(8,128)(2,1)S(1)} %collective-permute-done), kind=kLoop, calls=%fused_computation | loop fusion | flops 98304 | bytes 491520 | tf_op jit(solution)/shard_map/add | solution.py:301
Async XLA Ops:
  35.8 7.1 %collective-permute-start = (bf16[128,384]{1,0:T(8,128)(2,1)S(1)}, bf16[128,384]{1,0:T(8,128)(2,1)S(1)}, u32[]{:S(2)}, u32[]{:S(2)}) collective-permute-start(bf16[128,384]{1,0:T(8,128)(2,1)S(1)} %get-tuple-element.8), channel_id=1, source_target_pairs={{0,16},{1,17},{2,18},{3,19},{4,20},{5,21},{6,22},{7,23},{8,24},{9,... | collective-permute-start | bytes 294920 | tf_op jit(solution)/shard_map/ppermute | solution.py:301

commit v6 on v4

--- a/solution.py
+++ b/solution.py
@@ -12,6 +12,8 @@
 LANES = 128
 LABEL_ROWS = 8
 OUTER = 2
+FIRST = 256
+QUARTERS = 4
 NT = (((1,), (1,)), ((), ()))
 
 
@@ -34,6 +36,8 @@
     b2_hbm,
     cw_hbm,
     out_ref,
+    slot_ref,
+    slope_hbm,
     prof_ref,
     rad_ref,
     w1_ref,
@@ -44,21 +48,16 @@
     hidden_ref,
     factor_ref,
     sems,
+    out_sems,
 ):
     rows, width = prof_ref.shape
     hid = w1_ref.shape[1]
-    chan = rad_ref.shape[1]
-    half = hid // 2
-    low, high = pl.ds(0, half), pl.ds(half, half)
+    quarter = hid // QUARTERS
+    pieces = [pl.ds(i * quarter, quarter) for i in range(QUARTERS)]
     pairs = (
-        (prof_hbm, prof_ref),
-        (b1_hbm, b1_ref),
-        (w1_hbm.at[:, low], w1_ref.at[:, low]),
-        (w1_hbm.at[:, high], w1_ref.at[:, high]),
-        (w2_hbm, w2_ref),
-        (rad_hbm, rad_ref),
-        (b2_hbm, b2_ref),
-        (cw_hbm, cw_ref),
+        [(prof_hbm, prof_ref), (b1_hbm, b1_ref)]
+        + [(w1_hbm.at[:, piece], w1_ref.at[:, piece]) for piece in pieces]
+        + [(w2_hbm, w2_ref), (rad_hbm, rad_ref), (b2_hbm, b2_ref), (cw_hbm, cw_ref)]
     )
     copies = [
         pltpu.make_async_copy(src, dst, sems.at[i]) for i, (src, dst) in enumerate(pairs)
@@ -81,6 +80,7 @@
     place = owner & (inner - 1)
     order = lax.shift_right_arithmetic(owner, inner.bit_length() - 1) * most + rank
     slot = jnp.where(live, place * pool + order, -1)
+    slot_ref[...] = slot
     placing = as_bf16(lax.broadcasted_iota(jnp.int32, (inner * pool, rows), 0) == slot)
     lane = order + lax.rem(me_ref[0], LANES // pool) * pool
     lane_hot = as_bf16(lax.broadcasted_iota(jnp.int32, (LANES, rows), 0) == lane)
@@ -95,31 +95,34 @@
     prof = (prof_ref[...].astype(jnp.float32) * 0.5).astype(jnp.bfloat16)
     for i in range(hid // CHUNK):
         part = pl.ds(i * CHUNK, CHUNK)
-        if i == 0:
-            copies[2].wait()
-        if i == hid // CHUNK // 2:
-            copies[3].wait()
+        if i * CHUNK % quarter == 0:
+            copies[2 + i * CHUNK // quarter].wait()
         u = jnp.dot(prof, w1_ref[:, part], preferred_element_type=jnp.float32)
         u = u + 0.5 * b1_ref[:, part]
         p = jnp.tanh(u) + 1.0
         hidden = u * p
         hidden_ref[:, part] = hidden.astype(jnp.bfloat16)
         factor_ref[:, part] = p + hidden * (2.0 - p)
-    for copy in copies[4:]:
+    for copy in copies[2 + QUARTERS :]:
         copy.wait()
     output = jnp.dot(hidden_ref[...], w2_ref[...], preferred_element_type=jnp.float32)
     misfit = (0.5 * cw_ref[...]) * (output + b2_ref[...] - rad_ref[...].astype(jnp.float32))
     alive = lax.broadcasted_iota(jnp.int32, (rows, 1), 0) < count_ref[0]
     misfit = jnp.where(alive, misfit, 0.0).astype(jnp.bfloat16)
+    sent = []
     for i in range(hid // CHUNK):
         part = pl.ds(i * CHUNK, CHUNK)
         back = lax.dot_general(misfit, w2_ref[part, :], NT, preferred_element_type=jnp.float32)
         hidden_ref[:, part] = (back * factor_ref[:, part]).astype(jnp.bfloat16)
+        sent.append(
+            pltpu.make_async_copy(hidden_ref.at[:, part], slope_hbm.at[:, part], out_sems.at[i])
+        )
+        sent[-1].start()
+    parts = FIRST // LANES
     grads = lax.dot_general(
-        hidden_ref[...], w1_ref[...], NT, preferred_element_type=jnp.float32
+        hidden_ref[...], w1_ref[:FIRST, :], NT, preferred_element_type=jnp.float32
     ).astype(jnp.bfloat16)
     placed = jnp.dot(placing, grads, preferred_element_type=jnp.float32).astype(jnp.bfloat16)
-    parts = width // LANES
     for k in range(parts):
         out_ref[:, k * pool : (k + 1) * pool, :] = placed[
             :, k * LANES : (k + 1) * LANES
@@ -127,15 +130,46 @@
     out_ref[:, parts * pool :, :] = jnp.broadcast_to(
         labels.reshape(inner, 1, LANES), (inner, LABEL_ROWS, LANES)
     ).astype(jnp.bfloat16)
-
-
-def blocks_kernel(tiles, most, me_ref, got_ref, own_ref, other_ref):
+    for copy in sent:
+        copy.wait()
+
+
+def rest_kernel(pool, slot_ref, slope_hbm, w1_hbm, out_ref, slope_ref, w1_ref, sems):
+    inner = out_ref.shape[0]
+    rows, hid = slope_ref.shape
+    quarter = hid // QUARTERS
+    pieces = [pl.ds(i * quarter, quarter) for i in range(QUARTERS)]
+    pairs = [(w1_hbm.at[pl.ds(FIRST, w1_ref.shape[0]), :], w1_ref)]
+    pairs += [(slope_hbm.at[:, piece], slope_ref.at[:, piece]) for piece in pieces]
+    copies = [
+        pltpu.make_async_copy(src, dst, sems.at[i]) for i, (src, dst) in enumerate(pairs)
+    ]
+    for copy in copies:
+        copy.start()
+    slots = inner * pool
+    placing = as_bf16(lax.broadcasted_iota(jnp.int32, (slots, rows), 0) == slot_ref[...])
+    copies[0].wait()
+    grads = jnp.zeros((rows, w1_ref.shape[0]), jnp.float32)
+    for i, piece in enumerate(pieces):
+        copies[1 + i].wait()
+        grads += lax.dot_general(
+            slope_ref[:, piece], w1_ref[:, piece], NT, preferred_element_type=jnp.float32
+        )
+    placed = jnp.dot(placing, grads.astype(jnp.bfloat16), preferred_element_type=jnp.float32)
+    placed = placed.astype(jnp.bfloat16)
+    for k in range(w1_ref.shape[0] // LANES):
+        out_ref[:, k * pool : (k + 1) * pool, :] = placed[
+            :, k * LANES : (k + 1) * LANES
+        ].reshape(inner, pool, LANES)
+
+
+def blocks_kernel(tiles, most, marks_row, me_ref, got_ref, first_ref, own_ref, other_ref):
     inner = got_ref.shape[0]
     outer = tiles // inner
     pool = outer * most
     group = LANES // pool
     parts = own_ref.shape[1] // LANES
-    marks = got_ref[:, parts * pool :, :].astype(jnp.float32)[:, 0, :]
+    marks = first_ref[:, marks_row:, :].astype(jnp.float32)[:, 0, :]
     index = lax.broadcasted_iota(jnp.int32, (outer * COL_DEV, LANES), 0)
     lane = lax.broadcasted_iota(jnp.int32, (1, LANES), 1) & (pool - 1)
     turn = lax.shift_right_arithmetic(lane, most.bit_length() - 1) ^ (
@@ -153,6 +187,11 @@
         total = jnp.dot(chosen, block, preferred_element_type=jnp.float32)
         own_ref[:, k * LANES : (k + 1) * LANES] = total[:COL_DEV]
         other_ref[:, k * LANES : (k + 1) * LANES] = total[COL_DEV:].astype(jnp.bfloat16)
+
+
+def add_kernel(own_ref, came_ref, own_rest_ref, came_rest_ref, out_ref):
+    out_ref[:, :FIRST] = own_ref[...] + came_ref[...].astype(jnp.float32)
+    out_ref[:, FIRST:] = own_rest_ref[...] + came_rest_ref[...].astype(jnp.float32)
 
 
 def per_device(
@@ -174,16 +213,22 @@
     most = max(2, 2 * rows // tiles)
     inner = tiles // OUTER
     pool = OUTER * most
-    high = width // LANES * pool + LABEL_ROWS
+    marks_row = FIRST // LANES * pool
+    high = marks_row + LABEL_ROWS
     me = lax.axis_index("tile").astype(jnp.int32).reshape(1)
+    halves = [[o * inner + i for i in range(inner)] for o in range(OUTER)]
     vmem = pl.BlockSpec(memory_space=pltpu.VMEM)
     smem = pl.BlockSpec(memory_space=pltpu.SMEM)
     anywhere = pl.BlockSpec(memory_space=pl.ANY)
-    bucket = pl.pallas_call(
+    bucket, slot, slope = pl.pallas_call(
         functools.partial(rows_kernel, tiles, most),
-        out_shape=jax.ShapeDtypeStruct((inner, high, LANES), jnp.bfloat16),
+        out_shape=[
+            jax.ShapeDtypeStruct((inner, high, LANES), jnp.bfloat16),
+            jax.ShapeDtypeStruct((1, rows), jnp.int32),
+            jax.ShapeDtypeStruct((rows, hid), jnp.bfloat16),
+        ],
         in_specs=[smem, smem, vmem, vmem] + [anywhere] * 7,
-        out_specs=vmem,
+        out_specs=[vmem, vmem, anywhere],
         scratch_shapes=[
             pltpu.VMEM((rows, width), jnp.bfloat16),
             pltpu.VMEM((rows, chan), jnp.bfloat16),
@@ -194,7 +239,8 @@
             pltpu.VMEM((1, chan), jnp.float32),
             pltpu.VMEM((rows, hid), jnp.bfloat16),
             pltpu.VMEM((rows, hid), jnp.float32),
-            pltpu.SemaphoreType.DMA((8,)),
+            pltpu.SemaphoreType.DMA((QUARTERS + 6,)),
+            pltpu.SemaphoreType.DMA((hid // CHUNK,)),
         ],
         compiler_params=pltpu.CompilerParams(vmem_limit_bytes=60 * 1024 * 1024),
         name="rows_kernel",
@@ -211,23 +257,57 @@
         outer_bias.reshape(1, chan),
         channel_weight.reshape(1, chan),
     )
-    halves = [[o * inner + i for i in range(inner)] for o in range(OUTER)]
-    got = lax.all_to_all(
-        bucket, "tile", split_axis=0, concat_axis=0, axis_index_groups=halves, tiled=True
-    )
-    own, other = pl.pallas_call(
-        functools.partial(blocks_kernel, tiles, most),
-        out_shape=[
-            jax.ShapeDtypeStruct((COL_DEV, width), jnp.float32),
-            jax.ShapeDtypeStruct((COL_DEV, width), jnp.bfloat16),
+    rest = width - FIRST
+    bucket_rest = pl.pallas_call(
+        functools.partial(rest_kernel, pool),
+        out_shape=jax.ShapeDtypeStruct((inner, rest // LANES * pool, LANES), jnp.bfloat16),
+        in_specs=[vmem, anywhere, anywhere],
+        out_specs=vmem,
+        scratch_shapes=[
+            pltpu.VMEM((rows, hid), jnp.bfloat16),
+            pltpu.VMEM((rest, hid), jnp.bfloat16),
+            pltpu.SemaphoreType.DMA((QUARTERS + 1,)),
         ],
-        in_specs=[smem, vmem],
-        out_specs=[vmem, vmem],
-        compiler_params=pltpu.CompilerParams(vmem_limit_bytes=24 * 1024 * 1024),
-        name="blocks_kernel",
-    )(me, got)
+        compiler_params=pltpu.CompilerParams(vmem_limit_bytes=60 * 1024 * 1024),
+        cost_estimate=pl.CostEstimate(flops=3 << 30, bytes_accessed=7 << 20, transcendentals=0),
+        name="rest_kernel",
+    )(slot, slope, inner_weight)
+
+    def exchange(block):
+        return lax.all_to_all(
+            block, "tile", split_axis=0, concat_axis=0, axis_index_groups=halves, tiled=True
+        )
+
+    def blocks(block, first, features):
+        return pl.pallas_call(
+            functools.partial(blocks_kernel, tiles, most, marks_row),
+            out_shape=[
+                jax.ShapeDtypeStruct((COL_DEV, features), jnp.float32),
+                jax.ShapeDtypeStruct((COL_DEV, features), jnp.bfloat16),
+            ],
+            in_specs=[smem, vmem, vmem],
+            out_specs=[vmem, vmem],
+            compiler_params=pltpu.CompilerParams(vmem_limit_bytes=24 * 1024 * 1024),
+            cost_estimate=pl.CostEstimate(
+                flops=1 << 28, bytes_accessed=1 << 20, transcendentals=0
+            ),
+            name="blocks_kernel",
+        )(me, block, first)
+
     pairs = [(t, (t + inner) % tiles) for t in range(tiles)]
-    return own + lax.ppermute(other, "tile", pairs).astype(jnp.float32)
+    got = exchange(bucket)
+    got_rest = exchange(bucket_rest)
+    own, other = blocks(got, got, FIRST)
+    came = lax.ppermute(other, "tile", pairs)
+    own_rest, other_rest = blocks(got_rest, got, rest)
+    came_rest = lax.ppermute(other_rest, "tile", pairs)
+    return pl.pallas_call(
+        add_kernel,
+        out_shape=jax.ShapeDtypeStruct((COL_DEV, width), jnp.float32),
+        in_specs=[vmem] * 4,
+        out_specs=vmem,
+        name="add_kernel",
+    )(own, came, own_rest, came_rest)
 
 
 def solution(mesh):

time: 43.1 us -> 53.4 us (1.24)
  blocking collectives: 20 us -> 0 us
  starting transfers between devices: 2.65 us -> 14.1 us
  waiting for transfers between devices: 4.46 us -> 13.3 us
  Pallas kernels: 14.4 us -> 23 us
  local copies, waits for them, and re-layouts: 0 us -> 1.89 us
  other arithmetic: 0.7 us -> 0 us
    all_to_all x1 -> x0, blocking collectives: 20 us -> none  [per_device(): lax.all_to_all(bucket, 'tile', split_axis=0, concat_axis=0, axis_index_gr...]
    all_to_all x0 -> x2, waiting for transfers between devices: none -> 10.1 us  [exchange(): lax.all_to_all(block, 'tile', split_axis=0, concat_axis=0, axis_index_gro...]
    all_to_all x0 -> x2, starting transfers between devices: none -> 9.83 us  [exchange(): lax.all_to_all(block, 'tile', split_axis=0, concat_axis=0, axis_index_gro...]
    pallas_call x2 -> x5, Pallas kernels: 14.4 us -> 23 us  [the longest x1 14.4 us: per_device(): pl.pallas_call(functools.partial(rows_kernel, tiles, most), out_shape=[ja...]
    unnamed x0 -> x8, local copies, waits for them, and re-layouts: none -> 1.89 us
    ppermute x1 -> x2, starting transfers between devices: 2.65 us -> 4.25 us  [the longest x1 2.59 us: per_device(): came = lax.ppermute(other, 'tile', pairs)]
    ppermute x1 -> x2, waiting for transfers between devices: 4.46 us -> 3.16 us  [the longest x1 3.15 us: per_device(): came_rest = lax.ppermute(other_rest, 'tile', pairs)]
    add x1 -> x0, other arithmetic: 0.7 us -> none  [per_device(): return own + lax.ppermute(other, 'tile', pairs).astype(jnp.float32)]
  transfers between devices with their start and end apart: 1 -> 4, of which waited for: 1 -> 3; matrix products, arithmetic and copies ran while one was open for 0% -> 0% of each run, Pallas kernels for 0% -> 13%
where the time goes in v6:
time: 53.4 us; the launch traced here: 53 us
  Pallas kernels  23 us (43%)
  starting transfers between devices  14.1 us (26%)
  waiting for transfers between devices  13.3 us (25%)
  local copies, waits for them, and re-layouts  1.89 us (4%)
  between operations  0.72 us (1%)
    pallas_call x1, Pallas kernels, per_device(): pl.pallas_call(functools.partial(rows_kernel, tiles, most), out_shape=[ja...  14.4 us
    all_to_all x2, waiting for transfers between devices, exchange(): lax.all_to_all(block, 'tile', split_axis=0, concat_axis=0, axis_index_gro...  10.1 us
    all_to_all x2, starting transfers between devices, exchange(): lax.all_to_all(block, 'tile', split_axis=0, concat_axis=0, axis_index_gro...  9.83 us
    pallas_call x1, Pallas kernels, per_device(): pl.pallas_call(functools.partial(rest_kernel, pool), out_shape=jax.ShapeD...  6.12 us
    ppermute x1, waiting for transfers between devices, per_device(): came_rest = lax.ppermute(other_rest, 'tile', pairs)  3.15 us
    ppermute x1, starting transfers between devices, per_device(): came = lax.ppermute(other, 'tile', pairs)  2.59 us
    unnamed x8, local copies, waits for them, and re-layouts  1.89 us
    ppermute x1, starting transfers between devices, per_device(): came_rest = lax.ppermute(other_rest, 'tile', pairs)  1.66 us
  transfers between devices with their start and end apart: 4, of which 3 were waited for; matrix products, arithmetic and copies ran while one was open for 0% of the time, Pallas kernels for 13%

profile of v6, /device:TPU:0, one launch (start us, length us, event | category | flops | bytes accessed | tf_op | source)
XLA Modules:
  0.0 53.0 jit_solution(14101511465822448939)
XLA Ops:
  0.7 14.4 %rows_kernel.1 = (bf16[16,136,128]{2,1,0:T(8,128)(2,1)}, s32[1,512]{1,0:T(1,128)}, bf16[512,4096]{1,0:T(8,128)(2,1)}) custom-call(s32[1]{0:T(128)} %bitcast.me_ref, s32[1]{0:T(128)S(6)} %copy.11.count_ref, s32[1,512]{1,0:T(1,128)} %bitcast.7, s32[1,512]{1,0:T(1,128)} %bitcast.8, bf16[512,384]{1,0:T(8,128)(2,1)} %prof_hbm.1, bf16[512,512]{1,0:T(8,128)(2,1)} %rad_hbm.1, ...), custom_call_target="tpu_custom_call" | custom-call | tf_op jit(solution)/shard_map/rows_kernel/pallas_call | solution.py:223
  15.1 6.3 %all-to-all-start = ((bf16[16,136,128]{2,1,0:T(8,128)(2,1)}), bf16[16,136,128]{2,1,0:T(8,128)(2,1)S(1)}, u32[]{:S(2)}, u32[]{:S(2)}) async-start(bf16[16,136,128]{2,1,0:T(8,128)(2,1)} %get-tuple-element.12), calls=%async_computation | async-start | bytes 1114112 | tf_op jit(solution)/shard_map/all_to_all | solution.py:277
  21.4 6.1 %rest_kernel.1 = bf16[16,64,128]{2,1,0:T(8,128)(2,1)} custom-call(s32[1,512]{1,0:T(1,128)} %get-tuple-element.15.slot_ref, bf16[512,4096]{1,0:T(8,128)(2,1)} %get-tuple-element.16.slope_hbm, bf16[384,4096]{1,0:T(8,128)(2,1)} %w1_hbm.3), custom_call_target="tpu_custom_call" | custom-call | flops 3221225472 | bytes 7340032 | tf_op jit(solution)/shard_map/rest_kernel/pallas_call | solution.py:261
  27.5 4.8 %all-to-all-done.got_ref.first_ref = bf16[16,136,128]{2,1,0:T(8,128)(2,1)S(1)} async-done(((bf16[16,136,128]{2,1,0:T(8,128)(2,1)}), bf16[16,136,128]{2,1,0:T(8,128)(2,1)S(1)}, u32[]{:S(2)}, u32[]{:S(2)}) %all-to-all-start) | async-done | bytes 557088 | tf_op jit(solution)/shard_map/all_to_all | solution.py:277
  32.3 3.5 %all-to-all-start.1 = ((bf16[16,64,128]{2,1,0:T(8,128)(2,1)}), bf16[16,64,128]{2,1,0:T(8,128)(2,1)S(1)}, u32[]{:S(2)}, u32[]{:S(2)}) async-start(bf16[16,64,128]{2,1,0:T(8,128)(2,1)} %rest_kernel.1), calls=%async_computation.1 | async-start | bytes 524288 | tf_op jit(solution)/shard_map/all_to_all | solution.py:277
  35.8 0.5 blocks_kernel.2
  36.3 0.0 copy-start
  36.3 0.6 %copy-done = f32[128,256]{1,0:T(8,128)} copy-done((f32[128,256]{1,0:T(8,128)}, f32[128,256]{1,0:T(8,128)S(1)}, u32[]{:S(2)}) %copy-start) | copy-done | bytes 131096
  37.0 2.6 %collective-permute-start = (bf16[128,256]{1,0:T(8,128)(2,1)S(1)}, bf16[128,256]{1,0:T(8,128)(2,1)S(1)}, u32[]{:S(2)}, u32[]{:S(2)}) collective-permute-start(bf16[128,256]{1,0:T(8,128)(2,1)S(1)} %get-tuple-element.14), channel_id=1, source_target_pairs={{0,16},{1,17},{2,18},{3,19},{4,20},{5,21},{6,22},{7,23},{8,24},{9,... | collective-permute-start | bytes 196616 | tf_op jit(solution)/shard_map/ppermute | solution.py:301
  39.6 5.4 %all-to-all-done.1.got_ref = bf16[16,64,128]{2,1,0:T(8,128)(2,1)S(1)} async-done(((bf16[16,64,128]{2,1,0:T(8,128)(2,1)}), bf16[16,64,128]{2,1,0:T(8,128)(2,1)S(1)}, u32[]{:S(2)}, u32[]{:S(2)}) %all-to-all-start.1) | async-done | bytes 262176 | tf_op jit(solution)/shard_map/all_to_all | solution.py:277
  44.9 0.3 blocks_kernel.3
  45.3 0.0 copy-start.1
  45.3 0.6 %copy-done.1 = f32[128,128]{1,0:T(8,128)} copy-done((f32[128,128]{1,0:T(8,128)}, f32[128,128]{1,0:T(8,128)S(1)}, u32[]{:S(2)}) %copy-start.1) | copy-done | bytes 65560
  45.9 1.7 %collective-permute-start.1 = (bf16[128,128]{1,0:T(8,128)(2,1)S(1)}, bf16[128,128]{1,0:T(8,128)(2,1)S(1)}, u32[]{:S(2)}, u32[]{:S(2)}) collective-permute-start(bf16[128,128]{1,0:T(8,128)(2,1)S(1)} %get-tuple-element.18), channel_id=1, source_target_pairs={{0,16},{1,17},{2,18},{3,19},{4,20},{5,21},{6,22},{7,23},{8,24},{9,... | collective-permute-start | bytes 98312 | tf_op jit(solution)/shard_map/ppermute | solution.py:303
  47.6 3.2 %collective-permute-done.1.came_rest_ref = bf16[128,128]{1,0:T(8,128)(2,1)S(1)} collective-permute-done((bf16[128,128]{1,0:T(8,128)(2,1)S(1)}, bf16[128,128]{1,0:T(8,128)(2,1)S(1)}, u32[]{:S(2)}, u32[]{:S(2)}) %collective-permute-start.1) | collective-permute-done | bytes 32800 | tf_op jit(solution)/shard_map/ppermute | solution.py:303
  50.7 0.0 copy-start.3
  50.7 0.0 collective-permute-done.came_ref
  50.7 0.0 copy-start.2
  50.7 0.6 %copy-done.3 = bf16[128,128]{1,0:T(8,128)(2,1)} copy-done((bf16[128,128]{1,0:T(8,128)(2,1)}, bf16[128,128]{1,0:T(8,128)(2,1)S(1)}, u32[]{:S(2)}) %copy-start.3) | copy-done | bytes 32792
  51.3 0.0 copy-done.2
  51.3 1.6 %add_kernel.1 = f32[128,384]{1,0:T(8,128)} custom-call(f32[128,256]{1,0:T(8,128)} %copy-done, bf16[128,256]{1,0:T(8,128)(2,1)} %copy-done.2, f32[128,128]{1,0:T(8,128)} %copy-done.1, bf16[128,128]{1,0:T(8,128)(2,1)} %copy-done.3), custom_call_target="tpu_custom_call" | custom-call | tf_op jit(solution)/shard_map/add_kernel/pallas_call | solution.py:304
Async XLA Ops:
  15.1 17.2 %all-to-all-start = ((bf16[16,136,128]{2,1,0:T(8,128)(2,1)}), bf16[16,136,128]{2,1,0:T(8,128)(2,1)S(1)}, u32[]{:S(2)}, u32[]{:S(2)}) async-start(bf16[16,136,128]{2,1,0:T(8,128)(2,1)} %get-tuple-element.12), calls=%async_computation | async-start | bytes 1114112 | tf_op jit(solution)/shard_map/all_to_all | solution.py:277
  32.3 12.6 %all-to-all-start.1 = ((bf16[16,64,128]{2,1,0:T(8,128)(2,1)}), bf16[16,64,128]{2,1,0:T(8,128)(2,1)S(1)}, u32[]{:S(2)}, u32[]{:S(2)}) async-start(bf16[16,64,128]{2,1,0:T(8,128)(2,1)} %rest_kernel.1), calls=%async_computation.1 | async-start | bytes 524288 | tf_op jit(solution)/shard_map/all_to_all | solution.py:277
  36.3 0.7 %copy-start = (f32[128,256]{1,0:T(8,128)}, f32[128,256]{1,0:T(8,128)S(1)}, u32[]{:S(2)}) copy-start(f32[128,256]{1,0:T(8,128)S(1)} %get-tuple-element.13.own_ref) | copy-start | bytes 393220
  37.0 13.7 %collective-permute-start = (bf16[128,256]{1,0:T(8,128)(2,1)S(1)}, bf16[128,256]{1,0:T(8,128)(2,1)S(1)}, u32[]{:S(2)}, u32[]{:S(2)}) collective-permute-start(bf16[128,256]{1,0:T(8,128)(2,1)S(1)} %get-tuple-element.14), channel_id=1, source_target_pairs={{0,16},{1,17},{2,18},{3,19},{4,20},{5,21},{6,22},{7,23},{8,24},{9,... | collective-permute-start | bytes 196616 | tf_op jit(solution)/shard_map/ppermute | solution.py:301
  45.3 0.6 %copy-start.1 = (f32[128,128]{1,0:T(8,128)}, f32[128,128]{1,0:T(8,128)S(1)}, u32[]{:S(2)}) copy-start(f32[128,128]{1,0:T(8,128)S(1)} %get-tuple-element.17.own_rest_ref) | copy-start | bytes 196612
  45.9 4.8 %collective-permute-start.1 = (bf16[128,128]{1,0:T(8,128)(2,1)S(1)}, bf16[128,128]{1,0:T(8,128)(2,1)S(1)}, u32[]{:S(2)}, u32[]{:S(2)}) collective-permute-start(bf16[128,128]{1,0:T(8,128)(2,1)S(1)} %get-tuple-element.18), channel_id=1, source_target_pairs={{0,16},{1,17},{2,18},{3,19},{4,20},{5,21},{6,22},{7,23},{8,24},{9,... | collective-permute-start | bytes 98312 | tf_op jit(solution)/shard_map/ppermute | solution.py:303
  50.7 0.6 %copy-start.3 = (bf16[128,128]{1,0:T(8,128)(2,1)}, bf16[128,128]{1,0:T(8,128)(2,1)S(1)}, u32[]{:S(2)}) copy-start(bf16[128,128]{1,0:T(8,128)(2,1)S(1)} %collective-permute-done.1.came_rest_ref) | copy-start | bytes 98308
  50.7 0.6 %copy-start.2 = (bf16[128,256]{1,0:T(8,128)(2,1)}, bf16[128,256]{1,0:T(8,128)(2,1)S(1)}, u32[]{:S(2)}) copy-start(bf16[128,256]{1,0:T(8,128)(2,1)S(1)} %collective-permute-done.came_ref) | copy-start | bytes 196612

commit v7 on v4

--- a/solution.py
+++ b/solution.py
@@ -12,6 +12,7 @@
 LANES = 128
 LABEL_ROWS = 8
 OUTER = 2
+QUARTERS = 4
 NT = (((1,), (1,)), ((), ()))
 
 
@@ -41,24 +42,21 @@
     w2_ref,
     b2_ref,
     cw_ref,
+    w1t_ref,
+    w2t_ref,
     hidden_ref,
     factor_ref,
     sems,
 ):
     rows, width = prof_ref.shape
     hid = w1_ref.shape[1]
-    chan = rad_ref.shape[1]
-    half = hid // 2
-    low, high = pl.ds(0, half), pl.ds(half, half)
+    quarter = hid // QUARTERS
+    pieces = [pl.ds(i * quarter, quarter) for i in range(QUARTERS)]
     pairs = (
-        (prof_hbm, prof_ref),
-        (b1_hbm, b1_ref),
-        (w1_hbm.at[:, low], w1_ref.at[:, low]),
-        (w1_hbm.at[:, high], w1_ref.at[:, high]),
-        (w2_hbm, w2_ref),
-        (rad_hbm, rad_ref),
-        (b2_hbm, b2_ref),
-        (cw_hbm, cw_ref),
+        [(prof_hbm, prof_ref), (b1_hbm, b1_ref)]
+        + [(w1_hbm.at[:, piece], w1_ref.at[:, piece]) for piece in pieces]
+        + [(w2_hbm.at[piece, :], w2_ref.at[piece, :]) for piece in pieces]
+        + [(rad_hbm, rad_ref), (b2_hbm, b2_ref), (cw_hbm, cw_ref)]
     )
     copies = [
         pltpu.make_async_copy(src, dst, sems.at[i]) for i, (src, dst) in enumerate(pairs)
@@ -95,28 +93,30 @@
     prof = (prof_ref[...].astype(jnp.float32) * 0.5).astype(jnp.bfloat16)
     for i in range(hid // CHUNK):
         part = pl.ds(i * CHUNK, CHUNK)
-        if i == 0:
-            copies[2].wait()
-        if i == hid // CHUNK // 2:
-            copies[3].wait()
+        if i * CHUNK % quarter == 0:
+            copies[2 + i * CHUNK // quarter].wait()
         u = jnp.dot(prof, w1_ref[:, part], preferred_element_type=jnp.float32)
         u = u + 0.5 * b1_ref[:, part]
         p = jnp.tanh(u) + 1.0
         hidden = u * p
         hidden_ref[:, part] = hidden.astype(jnp.bfloat16)
         factor_ref[:, part] = p + hidden * (2.0 - p)
-    for copy in copies[4:]:
+        w1t_ref[part, :] = w1_ref[:, part].T
+    for copy in copies[2 + QUARTERS :]:
         copy.wait()
+    for i in range(hid // CHUNK):
+        part = pl.ds(i * CHUNK, CHUNK)
+        w2t_ref[:, part] = w2_ref[part, :].T
     output = jnp.dot(hidden_ref[...], w2_ref[...], preferred_element_type=jnp.float32)
     misfit = (0.5 * cw_ref[...]) * (output + b2_ref[...] - rad_ref[...].astype(jnp.float32))
     alive = lax.broadcasted_iota(jnp.int32, (rows, 1), 0) < count_ref[0]
     misfit = jnp.where(alive, misfit, 0.0).astype(jnp.bfloat16)
     for i in range(hid // CHUNK):
         part = pl.ds(i * CHUNK, CHUNK)
-        back = lax.dot_general(misfit, w2_ref[part, :], NT, preferred_element_type=jnp.float32)
+        back = jnp.dot(misfit, w2t_ref[:, part], preferred_element_type=jnp.float32)
         hidden_ref[:, part] = (back * factor_ref[:, part]).astype(jnp.bfloat16)
-    grads = lax.dot_general(
-        hidden_ref[...], w1_ref[...], NT, preferred_element_type=jnp.float32
+    grads = jnp.dot(
+        hidden_ref[...], w1t_ref[...], preferred_element_type=jnp.float32
     ).astype(jnp.bfloat16)
     placed = jnp.dot(placing, grads, preferred_element_type=jnp.float32).astype(jnp.bfloat16)
     parts = width // LANES
@@ -192,9 +192,11 @@
             pltpu.VMEM((hid, chan), jnp.bfloat16),
             pltpu.VMEM((1, chan), jnp.float32),
             pltpu.VMEM((1, chan), jnp.float32),
+            pltpu.VMEM((hid, width), jnp.bfloat16),
+            pltpu.VMEM((chan, hid), jnp.bfloat16),
             pltpu.VMEM((rows, hid), jnp.bfloat16),
             pltpu.VMEM((rows, hid), jnp.float32),
-            pltpu.SemaphoreType.DMA((8,)),
+            pltpu.SemaphoreType.DMA((2 * QUARTERS + 5,)),
         ],
         compiler_params=pltpu.CompilerParams(vmem_limit_bytes=60 * 1024 * 1024),
         name="rows_kernel",

time: 43.1 us -> 43.4 us (level)
  no operation moved by 1% of the time
where the time goes in v7:
time: 43.4 us; the launch traced here: 43.2 us
  blocking collectives  20 us (46%)
  Pallas kernels  14.7 us (34%)
  waiting for transfers between devices  4.46 us (10%)
  starting transfers between devices  2.66 us (6%)
  other arithmetic  0.7 us (2%)
  between operations  0.67 us (2%)
    all_to_all x1, blocking collectives, per_device(): lax.all_to_all(bucket, 'tile', split_axis=0, concat_axis=0, axis_index_gr...  20 us
    pallas_call x1, Pallas kernels, per_device(): pl.pallas_call(functools.partial(rows_kernel, tiles, most), out_shape=jax...  14.1 us
    ppermute x1, waiting for transfers between devices, per_device(): return own + lax.ppermute(other, 'tile', pairs).astype(jnp.float32)  4.46 us
    ppermute x1, starting transfers between devices, per_device(): return own + lax.ppermute(other, 'tile', pairs).astype(jnp.float32)  2.66 us
  transfers between devices with their start and end apart: 1, of which 1 were waited for; matrix products, arithmetic and copies ran while one was open for 0% of the time, Pallas kernels for 0%

profile of v7, /device:TPU:0, one launch (start us, length us, event | category | flops | bytes accessed | tf_op | source)
XLA Modules:
  0.0 43.2 jit_solution(8194754636741422023)
XLA Ops:
  0.7 14.1 %rows_kernel.1 = bf16[16,200,128]{2,1,0:T(8,128)(2,1)} custom-call(s32[1]{0:T(128)} %bitcast.me_ref, s32[1]{0:T(128)S(6)} %copy.11.count_ref, s32[1,512]{1,0:T(1,128)} %bitcast.7, s32[1,512]{1,0:T(1,128)} %bitcast.8, bf16[512,384]{1,0:T(8,128)(2,1)} %prof_hbm.1, bf16[512,512]{1,0:T(8,128)(2,1)} %rad_hbm.1, bf16[384,4096]{1,0:T(8,128)(2,1)} %w1_hbm.1, ...), custom_call_target="tpu_custom_call" | custom-call | tf_op jit(solution)/shard_map/rows_kernel/pallas_call | solution.py:182
  14.8 20.0 %all_to_all.5.got_ref = bf16[16,200,128]{2,1,0:T(8,128)(2,1)S(1)} all-to-all(bf16[16,200,128]{2,1,0:T(8,128)(2,1)} %rows_kernel.1), channel_id=1, replica_groups={{0,1,2,3,4,5,6,7,8,9,10,11,12,13,14,15},{16,17,18,19,20,21,22,23,24,25,..., dimensions={0} | all-to-all | bytes 1638400 | tf_op jit(solution)/shard_map/all_to_all | solution.py:217
  34.8 0.6 %blocks_kernel.1 = (f32[128,384]{1,0:T(8,128)S(1)}, bf16[128,384]{1,0:T(8,128)(2,1)S(1)}) custom-call(s32[1]{0:T(128)} %bitcast.me_ref, bf16[16,200,128]{2,1,0:T(8,128)(2,1)S(1)} %all_to_all.5.got_ref), custom_call_target="tpu_custom_call" | custom-call | tf_op jit(solution)/shard_map/blocks_kernel/pallas_call | solution.py:220
  35.4 2.7 %collective-permute-start = (bf16[128,384]{1,0:T(8,128)(2,1)S(1)}, bf16[128,384]{1,0:T(8,128)(2,1)S(1)}, u32[]{:S(2)}, u32[]{:S(2)}) collective-permute-start(bf16[128,384]{1,0:T(8,128)(2,1)S(1)} %get-tuple-element.8), channel_id=1, source_target_pairs={{0,16},{1,17},{2,18},{3,19},{4,20},{5,21},{6,22},{7,23},{8,24},{9,... | collective-permute-start | bytes 294920 | tf_op jit(solution)/shard_map/ppermute | solution.py:232
  38.0 4.5 %collective-permute-done = bf16[128,384]{1,0:T(8,128)(2,1)S(1)} collective-permute-done((bf16[128,384]{1,0:T(8,128)(2,1)S(1)}, bf16[128,384]{1,0:T(8,128)(2,1)S(1)}, u32[]{:S(2)}, u32[]{:S(2)}) %collective-permute-start) | collective-permute-done | bytes 98336 | tf_op jit(solution)/shard_map/ppermute | solution.py:232
  42.5 0.7 %convert_add_fusion = f32[128,384]{1,0:T(8,128)} fusion(f32[128,384]{1,0:T(8,128)S(1)} %get-tuple-element.7, bf16[128,384]{1,0:T(8,128)(2,1)S(1)} %collective-permute-done), kind=kLoop, calls=%fused_computation | loop fusion | flops 98304 | bytes 491520 | tf_op jit(solution)/shard_map/add | solution.py:232
Async XLA Ops:
  35.4 7.1 %collective-permute-start = (bf16[128,384]{1,0:T(8,128)(2,1)S(1)}, bf16[128,384]{1,0:T(8,128)(2,1)S(1)}, u32[]{:S(2)}, u32[]{:S(2)}) collective-permute-start(bf16[128,384]{1,0:T(8,128)(2,1)S(1)} %get-tuple-element.8), channel_id=1, source_target_pairs={{0,16},{1,17},{2,18},{3,19},{4,20},{5,21},{6,22},{7,23},{8,24},{9,... | collective-permute-start | bytes 294920 | tf_op jit(solution)/shard_map/ppermute | solution.py:232

commit v8 on v7

--- a/solution.py
+++ b/solution.py
@@ -42,14 +42,13 @@
     w2_ref,
     b2_ref,
     cw_ref,
-    w1t_ref,
-    w2t_ref,
     hidden_ref,
     factor_ref,
     sems,
 ):
     rows, width = prof_ref.shape
     hid = w1_ref.shape[1]
+    chan = rad_ref.shape[1]
     quarter = hid // QUARTERS
     pieces = [pl.ds(i * quarter, quarter) for i in range(QUARTERS)]
     pairs = (
@@ -61,8 +60,10 @@
     copies = [
         pltpu.make_async_copy(src, dst, sems.at[i]) for i, (src, dst) in enumerate(pairs)
     ]
-    for copy in copies:
-        copy.start()
+    for i in range(2 + QUARTERS):
+        copies[i].start(priority=0)
+    for i in range(2 + QUARTERS, len(copies)):
+        copies[i].start(priority=1)
 
     inner = out_ref.shape[0]
     live = lax.broadcasted_iota(jnp.int32, (1, rows), 1) < count_ref[0]
@@ -91,32 +92,32 @@
     copies[0].wait()
     copies[1].wait()
     prof = (prof_ref[...].astype(jnp.float32) * 0.5).astype(jnp.bfloat16)
-    for i in range(hid // CHUNK):
-        part = pl.ds(i * CHUNK, CHUNK)
-        if i * CHUNK % quarter == 0:
-            copies[2 + i * CHUNK // quarter].wait()
-        u = jnp.dot(prof, w1_ref[:, part], preferred_element_type=jnp.float32)
-        u = u + 0.5 * b1_ref[:, part]
-        p = jnp.tanh(u) + 1.0
-        hidden = u * p
-        hidden_ref[:, part] = hidden.astype(jnp.bfloat16)
-        factor_ref[:, part] = p + hidden * (2.0 - p)
-        w1t_ref[part, :] = w1_ref[:, part].T
-    for copy in copies[2 + QUARTERS :]:
+    output = jnp.zeros((rows, chan), jnp.float32)
+    for q in range(QUARTERS):
+        copies[2 + q].wait()
+        for i in range(quarter // CHUNK):
+            part = pl.ds(q * quarter + i * CHUNK, CHUNK)
+            u = jnp.dot(prof, w1_ref[:, part], preferred_element_type=jnp.float32)
+            u = u + 0.5 * b1_ref[:, part]
+            p = jnp.tanh(u) + 1.0
+            hidden = u * p
+            hidden_ref[:, part] = hidden.astype(jnp.bfloat16)
+            factor_ref[:, part] = p + hidden * (2.0 - p)
+        copies[2 + QUARTERS + q].wait()
+        output += jnp.dot(
+            hidden_ref[:, pieces[q]], w2_ref[pieces[q], :], preferred_element_type=jnp.float32
+        )
+    for copy in copies[2 + 2 * QUARTERS :]:
         copy.wait()
-    for i in range(hid // CHUNK):
-        part = pl.ds(i * CHUNK, CHUNK)
-        w2t_ref[:, part] = w2_ref[part, :].T
-    output = jnp.dot(hidden_ref[...], w2_ref[...], preferred_element_type=jnp.float32)
     misfit = (0.5 * cw_ref[...]) * (output + b2_ref[...] - rad_ref[...].astype(jnp.float32))
     alive = lax.broadcasted_iota(jnp.int32, (rows, 1), 0) < count_ref[0]
     misfit = jnp.where(alive, misfit, 0.0).astype(jnp.bfloat16)
     for i in range(hid // CHUNK):
         part = pl.ds(i * CHUNK, CHUNK)
-        back = jnp.dot(misfit, w2t_ref[:, part], preferred_element_type=jnp.float32)
+        back = lax.dot_general(misfit, w2_ref[part, :], NT, preferred_element_type=jnp.float32)
         hidden_ref[:, part] = (back * factor_ref[:, part]).astype(jnp.bfloat16)
-    grads = jnp.dot(
-        hidden_ref[...], w1t_ref[...], preferred_element_type=jnp.float32
+    grads = lax.dot_general(
+        hidden_ref[...], w1_ref[...], NT, preferred_element_type=jnp.float32
     ).astype(jnp.bfloat16)
     placed = jnp.dot(placing, grads, preferred_element_type=jnp.float32).astype(jnp.bfloat16)
     parts = width // LANES
@@ -192,8 +193,6 @@
             pltpu.VMEM((hid, chan), jnp.bfloat16),
             pltpu.VMEM((1, chan), jnp.float32),
             pltpu.VMEM((1, chan), jnp.float32),
-            pltpu.VMEM((hid, width), jnp.bfloat16),
-            pltpu.VMEM((chan, hid), jnp.bfloat16),
             pltpu.VMEM((rows, hid), jnp.bfloat16),
             pltpu.VMEM((rows, hid), jnp.float32),
             pltpu.SemaphoreType.DMA((2 * QUARTERS + 5,)),

time: 43.4 us -> 43.8 us (level)
  no operation moved by 1% of the time
where the time goes in v8:
time: 43.8 us; the launch traced here: 43.6 us
  blocking collectives  20 us (46%)
  Pallas kernels  15.1 us (34%)
  waiting for transfers between devices  4.45 us (10%)
  starting transfers between devices  2.66 us (6%)
  other arithmetic  0.7 us (2%)
  between operations  0.67 us (2%)
    all_to_all x1, blocking collectives, per_device(): lax.all_to_all(bucket, 'tile', split_axis=0, concat_axis=0, axis_index_gr...  20 us
    pallas_call x1, Pallas kernels, per_device(): pl.pallas_call(functools.partial(rows_kernel, tiles, most), out_shape=jax...  14.5 us
    ppermute x1, waiting for transfers between devices, per_device(): return own + lax.ppermute(other, 'tile', pairs).astype(jnp.float32)  4.45 us
    ppermute x1, starting transfers between devices, per_device(): return own + lax.ppermute(other, 'tile', pairs).astype(jnp.float32)  2.66 us
  transfers between devices with their start and end apart: 1, of which 1 were waited for; matrix products, arithmetic and copies ran while one was open for 0% of the time, Pallas kernels for 0%

profile of v8, /device:TPU:0, one launch (start us, length us, event | category | flops | bytes accessed | tf_op | source)
XLA Modules:
  0.0 43.6 jit_solution(14371209406018447623)
XLA Ops:
  0.7 14.5 %rows_kernel.1 = bf16[16,200,128]{2,1,0:T(8,128)(2,1)} custom-call(s32[1]{0:T(128)} %bitcast.me_ref, s32[1]{0:T(128)S(6)} %copy.11.count_ref, s32[1,512]{1,0:T(1,128)} %bitcast.7, s32[1,512]{1,0:T(1,128)} %bitcast.8, bf16[512,384]{1,0:T(8,128)(2,1)} %prof_hbm.1, bf16[512,512]{1,0:T(8,128)(2,1)} %rad_hbm.1, bf16[384,4096]{1,0:T(8,128)(2,1)} %w1_hbm.1, ...), custom_call_target="tpu_custom_call" | custom-call | tf_op jit(solution)/shard_map/rows_kernel/pallas_call | solution.py:183
  15.1 20.0 %all_to_all.5.got_ref = bf16[16,200,128]{2,1,0:T(8,128)(2,1)S(1)} all-to-all(bf16[16,200,128]{2,1,0:T(8,128)(2,1)} %rows_kernel.1), channel_id=1, replica_groups={{0,1,2,3,4,5,6,7,8,9,10,11,12,13,14,15},{16,17,18,19,20,21,22,23,24,25,..., dimensions={0} | all-to-all | bytes 1638400 | tf_op jit(solution)/shard_map/all_to_all | solution.py:216
  35.1 0.6 %blocks_kernel.1 = (f32[128,384]{1,0:T(8,128)S(1)}, bf16[128,384]{1,0:T(8,128)(2,1)S(1)}) custom-call(s32[1]{0:T(128)} %bitcast.me_ref, bf16[16,200,128]{2,1,0:T(8,128)(2,1)S(1)} %all_to_all.5.got_ref), custom_call_target="tpu_custom_call" | custom-call | tf_op jit(solution)/shard_map/blocks_kernel/pallas_call | solution.py:219
  35.8 2.7 %collective-permute-start = (bf16[128,384]{1,0:T(8,128)(2,1)S(1)}, bf16[128,384]{1,0:T(8,128)(2,1)S(1)}, u32[]{:S(2)}, u32[]{:S(2)}) collective-permute-start(bf16[128,384]{1,0:T(8,128)(2,1)S(1)} %get-tuple-element.8), channel_id=1, source_target_pairs={{0,16},{1,17},{2,18},{3,19},{4,20},{5,21},{6,22},{7,23},{8,24},{9,... | collective-permute-start | bytes 294920 | tf_op jit(solution)/shard_map/ppermute | solution.py:231
  38.4 4.4 %collective-permute-done = bf16[128,384]{1,0:T(8,128)(2,1)S(1)} collective-permute-done((bf16[128,384]{1,0:T(8,128)(2,1)S(1)}, bf16[128,384]{1,0:T(8,128)(2,1)S(1)}, u32[]{:S(2)}, u32[]{:S(2)}) %collective-permute-start) | collective-permute-done | bytes 98336 | tf_op jit(solution)/shard_map/ppermute | solution.py:231
  42.9 0.7 %convert_add_fusion = f32[128,384]{1,0:T(8,128)} fusion(f32[128,384]{1,0:T(8,128)S(1)} %get-tuple-element.7, bf16[128,384]{1,0:T(8,128)(2,1)S(1)} %collective-permute-done), kind=kLoop, calls=%fused_computation | loop fusion | flops 98304 | bytes 491520 | tf_op jit(solution)/shard_map/add | solution.py:231
Async XLA Ops:
  35.8 7.1 %collective-permute-start = (bf16[128,384]{1,0:T(8,128)(2,1)S(1)}, bf16[128,384]{1,0:T(8,128)(2,1)S(1)}, u32[]{:S(2)}, u32[]{:S(2)}) collective-permute-start(bf16[128,384]{1,0:T(8,128)(2,1)S(1)} %get-tuple-element.8), channel_id=1, source_target_pairs={{0,16},{1,17},{2,18},{3,19},{4,20},{5,21},{6,22},{7,23},{8,24},{9,... | collective-permute-start | bytes 294920 | tf_op jit(solution)/shard_map/ppermute | solution.py:231

commit v9 on v4

--- a/solution.py
+++ b/solution.py
@@ -12,6 +12,7 @@
 LANES = 128
 LABEL_ROWS = 8
 OUTER = 2
+ROWS = 256
 NT = (((1,), (1,)), ((), ()))
 
 
@@ -92,32 +93,42 @@
 
     copies[0].wait()
     copies[1].wait()
-    prof = (prof_ref[...].astype(jnp.float32) * 0.5).astype(jnp.bfloat16)
+    prof_ref[...] = (prof_ref[...].astype(jnp.float32) * 0.5).astype(jnp.bfloat16)
+    blocks = [pl.ds(i, ROWS) for i in range(0, rows, ROWS)]
     for i in range(hid // CHUNK):
         part = pl.ds(i * CHUNK, CHUNK)
         if i == 0:
             copies[2].wait()
         if i == hid // CHUNK // 2:
             copies[3].wait()
-        u = jnp.dot(prof, w1_ref[:, part], preferred_element_type=jnp.float32)
-        u = u + 0.5 * b1_ref[:, part]
-        p = jnp.tanh(u) + 1.0
-        hidden = u * p
-        hidden_ref[:, part] = hidden.astype(jnp.bfloat16)
-        factor_ref[:, part] = p + hidden * (2.0 - p)
+        for m in blocks:
+            u = jnp.dot(prof_ref[m, :], w1_ref[:, part], preferred_element_type=jnp.float32)
+            u = u + 0.5 * b1_ref[:, part]
+            p = jnp.tanh(u) + 1.0
+            hidden = u * p
+            hidden_ref[m, part] = hidden.astype(jnp.bfloat16)
+            factor_ref[m, part] = p + hidden * (2.0 - p)
     for copy in copies[4:]:
         copy.wait()
-    output = jnp.dot(hidden_ref[...], w2_ref[...], preferred_element_type=jnp.float32)
-    misfit = (0.5 * cw_ref[...]) * (output + b2_ref[...] - rad_ref[...].astype(jnp.float32))
-    alive = lax.broadcasted_iota(jnp.int32, (rows, 1), 0) < count_ref[0]
-    misfit = jnp.where(alive, misfit, 0.0).astype(jnp.bfloat16)
+    scale = 0.5 * cw_ref[...]
+    for n, m in enumerate(blocks):
+        output = jnp.dot(hidden_ref[m, :], w2_ref[...], preferred_element_type=jnp.float32)
+        misfit = scale * (output + b2_ref[...] - rad_ref[m, :].astype(jnp.float32))
+        alive = lax.broadcasted_iota(jnp.int32, (ROWS, 1), 0) + n * ROWS < count_ref[0]
+        rad_ref[m, :] = jnp.where(alive, misfit, 0.0).astype(jnp.bfloat16)
     for i in range(hid // CHUNK):
         part = pl.ds(i * CHUNK, CHUNK)
-        back = lax.dot_general(misfit, w2_ref[part, :], NT, preferred_element_type=jnp.float32)
-        hidden_ref[:, part] = (back * factor_ref[:, part]).astype(jnp.bfloat16)
-    grads = lax.dot_general(
-        hidden_ref[...], w1_ref[...], NT, preferred_element_type=jnp.float32
-    ).astype(jnp.bfloat16)
+        for m in blocks:
+            back = lax.dot_general(
+                rad_ref[m, :], w2_ref[part, :], NT, preferred_element_type=jnp.float32
+            )
+            hidden_ref[m, part] = (back * factor_ref[m, part]).astype(jnp.bfloat16)
+    for m in blocks:
+        grads = lax.dot_general(
+            hidden_ref[m, :], w1_ref[...], NT, preferred_element_type=jnp.float32
+        )
+        prof_ref[m, :] = grads.astype(jnp.bfloat16)
+    grads = prof_ref[...]
     placed = jnp.dot(placing, grads, preferred_element_type=jnp.float32).astype(jnp.bfloat16)
     parts = width // LANES
     for k in range(parts):

time: 43.1 us -> 42.9 us (level)
  no operation moved by 1% of the time
where the time goes in v9:
time: 42.9 us; the launch traced here: 42.7 us
  blocking collectives  20 us (47%)
  Pallas kernels  14.2 us (33%)
  waiting for transfers between devices  4.46 us (10%)
  starting transfers between devices  2.65 us (6%)
  other arithmetic  0.7 us (2%)
  between operations  0.67 us (2%)
    all_to_all x1, blocking collectives, per_device(): lax.all_to_all(bucket, 'tile', split_axis=0, concat_axis=0, axis_index_gr...  20 us
    pallas_call x1, Pallas kernels, per_device(): pl.pallas_call(functools.partial(rows_kernel, tiles, most), out_shape=jax...  13.6 us
    ppermute x1, waiting for transfers between devices, per_device(): return own + lax.ppermute(other, 'tile', pairs).astype(jnp.float32)  4.46 us
    ppermute x1, starting transfers between devices, per_device(): return own + lax.ppermute(other, 'tile', pairs).astype(jnp.float32)  2.65 us
  transfers between devices with their start and end apart: 1, of which 1 were waited for; matrix products, arithmetic and copies ran while one was open for 0% of the time, Pallas kernels for 0%

profile of v9, /device:TPU:0, one launch (start us, length us, event | category | flops | bytes accessed | tf_op | source)
XLA Modules:
  0.0 42.7 jit_solution(8699579148913179647)
XLA Ops:
  0.7 13.6 %rows_kernel.1 = bf16[16,200,128]{2,1,0:T(8,128)(2,1)} custom-call(s32[1]{0:T(128)} %bitcast.me_ref, s32[1]{0:T(128)S(6)} %copy.11.count_ref, s32[1,512]{1,0:T(1,128)} %bitcast.7, s32[1,512]{1,0:T(1,128)} %bitcast.8, bf16[512,384]{1,0:T(8,128)(2,1)} %prof_hbm.1, bf16[512,512]{1,0:T(8,128)(2,1)} %rad_hbm.1, bf16[384,4096]{1,0:T(8,128)(2,1)} %w1_hbm.1, ...), custom_call_target="tpu_custom_call" | custom-call | tf_op jit(solution)/shard_map/rows_kernel/pallas_call | solution.py:193
  14.2 20.0 %all_to_all.5.got_ref = bf16[16,200,128]{2,1,0:T(8,128)(2,1)S(1)} all-to-all(bf16[16,200,128]{2,1,0:T(8,128)(2,1)} %rows_kernel.1), channel_id=1, replica_groups={{0,1,2,3,4,5,6,7,8,9,10,11,12,13,14,15},{16,17,18,19,20,21,22,23,24,25,..., dimensions={0} | all-to-all | bytes 1638400 | tf_op jit(solution)/shard_map/all_to_all | solution.py:226
  34.3 0.6 %blocks_kernel.1 = (f32[128,384]{1,0:T(8,128)S(1)}, bf16[128,384]{1,0:T(8,128)(2,1)S(1)}) custom-call(s32[1]{0:T(128)} %bitcast.me_ref, bf16[16,200,128]{2,1,0:T(8,128)(2,1)S(1)} %all_to_all.5.got_ref), custom_call_target="tpu_custom_call" | custom-call | tf_op jit(solution)/shard_map/blocks_kernel/pallas_call | solution.py:229
  34.9 2.6 %collective-permute-start = (bf16[128,384]{1,0:T(8,128)(2,1)S(1)}, bf16[128,384]{1,0:T(8,128)(2,1)S(1)}, u32[]{:S(2)}, u32[]{:S(2)}) collective-permute-start(bf16[128,384]{1,0:T(8,128)(2,1)S(1)} %get-tuple-element.8), channel_id=1, source_target_pairs={{0,16},{1,17},{2,18},{3,19},{4,20},{5,21},{6,22},{7,23},{8,24},{9,... | collective-permute-start | bytes 294920 | tf_op jit(solution)/shard_map/ppermute | solution.py:241
  37.5 4.5 %collective-permute-done = bf16[128,384]{1,0:T(8,128)(2,1)S(1)} collective-permute-done((bf16[128,384]{1,0:T(8,128)(2,1)S(1)}, bf16[128,384]{1,0:T(8,128)(2,1)S(1)}, u32[]{:S(2)}, u32[]{:S(2)}) %collective-permute-start) | collective-permute-done | bytes 98336 | tf_op jit(solution)/shard_map/ppermute | solution.py:241
  42.0 0.7 %convert_add_fusion = f32[128,384]{1,0:T(8,128)} fusion(f32[128,384]{1,0:T(8,128)S(1)} %get-tuple-element.7, bf16[128,384]{1,0:T(8,128)(2,1)S(1)} %collective-permute-done), kind=kLoop, calls=%fused_computation | loop fusion | flops 98304 | bytes 491520 | tf_op jit(solution)/shard_map/add | solution.py:241
Async XLA Ops:
  34.9 7.1 %collective-permute-start = (bf16[128,384]{1,0:T(8,128)(2,1)S(1)}, bf16[128,384]{1,0:T(8,128)(2,1)S(1)}, u32[]{:S(2)}, u32[]{:S(2)}) collective-permute-start(bf16[128,384]{1,0:T(8,128)(2,1)S(1)} %get-tuple-element.8), channel_id=1, source_target_pairs={{0,16},{1,17},{2,18},{3,19},{4,20},{5,21},{6,22},{7,23},{8,24},{9,... | collective-permute-start | bytes 294920 | tf_op jit(solution)/shard_map/ppermute | solution.py:241

commit v10 on v9

--- a/solution.py
+++ b/solution.py
@@ -34,7 +34,7 @@
     w2_hbm,
     b2_hbm,
     cw_hbm,
-    out_ref,
+    out_hbm,
     prof_ref,
     rad_ref,
     w1_ref,
@@ -44,22 +44,19 @@
     cw_ref,
     hidden_ref,
     factor_ref,
+    out_ref,
     sems,
+    out_sems,
 ):
     rows, width = prof_ref.shape
     hid = w1_ref.shape[1]
     chan = rad_ref.shape[1]
-    half = hid // 2
-    low, high = pl.ds(0, half), pl.ds(half, half)
+    starts = [0, CHUNK, 2 * CHUNK, 4 * CHUNK, hid]
+    pieces = [pl.ds(lo, hi - lo) for lo, hi in zip(starts[:-1], starts[1:])]
     pairs = (
-        (prof_hbm, prof_ref),
-        (b1_hbm, b1_ref),
-        (w1_hbm.at[:, low], w1_ref.at[:, low]),
-        (w1_hbm.at[:, high], w1_ref.at[:, high]),
-        (w2_hbm, w2_ref),
-        (rad_hbm, rad_ref),
-        (b2_hbm, b2_ref),
-        (cw_hbm, cw_ref),
+        [(prof_hbm, prof_ref), (b1_hbm, b1_ref)]
+        + [(w1_hbm.at[:, piece], w1_ref.at[:, piece]) for piece in pieces]
+        + [(w2_hbm, w2_ref), (rad_hbm, rad_ref), (b2_hbm, b2_ref), (cw_hbm, cw_ref)]
     )
     copies = [
         pltpu.make_async_copy(src, dst, sems.at[i]) for i, (src, dst) in enumerate(pairs)
@@ -67,6 +64,29 @@
     for copy in copies:
         copy.start()
 
+    copies[0].wait()
+    copies[1].wait()
+    prof_ref[...] = (prof_ref[...].astype(jnp.float32) * 0.5).astype(jnp.bfloat16)
+    blocks = [pl.ds(i, ROWS) for i in range(0, rows, ROWS)]
+    for i in range(hid // CHUNK):
+        part = pl.ds(i * CHUNK, CHUNK)
+        if i * CHUNK in starts:
+            copies[2 + starts.index(i * CHUNK)].wait()
+        for m in blocks:
+            u = jnp.dot(prof_ref[m, :], w1_ref[:, part], preferred_element_type=jnp.float32)
+            u = u + 0.5 * b1_ref[:, part]
+            p = jnp.tanh(u) + 1.0
+            hidden = u * p
+            hidden_ref[m, part] = hidden.astype(jnp.bfloat16)
+            factor_ref[m, part] = p + hidden * (2.0 - p)
+    for copy in copies[2 + len(pieces) :]:
+        copy.wait()
+    scale = 0.5 * cw_ref[...]
+    for n, m in enumerate(blocks):
+        output = jnp.dot(hidden_ref[m, :], w2_ref[...], preferred_element_type=jnp.float32)
+        misfit = scale * (output + b2_ref[...] - rad_ref[m, :].astype(jnp.float32))
+        alive = lax.broadcasted_iota(jnp.int32, (ROWS, 1), 0) + n * ROWS < count_ref[0]
+        rad_ref[m, :] = jnp.where(alive, misfit, 0.0).astype(jnp.bfloat16)
     inner = out_ref.shape[0]
     live = lax.broadcasted_iota(jnp.int32, (1, rows), 1) < count_ref[0]
     owner = jnp.where(live, owner_ref[...], -1)
@@ -91,31 +111,6 @@
         marked.astype(jnp.bfloat16), lane_hot, NT, preferred_element_type=jnp.float32
     )
 
-    copies[0].wait()
-    copies[1].wait()
-    prof_ref[...] = (prof_ref[...].astype(jnp.float32) * 0.5).astype(jnp.bfloat16)
-    blocks = [pl.ds(i, ROWS) for i in range(0, rows, ROWS)]
-    for i in range(hid // CHUNK):
-        part = pl.ds(i * CHUNK, CHUNK)
-        if i == 0:
-            copies[2].wait()
-        if i == hid // CHUNK // 2:
-            copies[3].wait()
-        for m in blocks:
-            u = jnp.dot(prof_ref[m, :], w1_ref[:, part], preferred_element_type=jnp.float32)
-            u = u + 0.5 * b1_ref[:, part]
-            p = jnp.tanh(u) + 1.0
-            hidden = u * p
-            hidden_ref[m, part] = hidden.astype(jnp.bfloat16)
-            factor_ref[m, part] = p + hidden * (2.0 - p)
-    for copy in copies[4:]:
-        copy.wait()
-    scale = 0.5 * cw_ref[...]
-    for n, m in enumerate(blocks):
-        output = jnp.dot(hidden_ref[m, :], w2_ref[...], preferred_element_type=jnp.float32)
-        misfit = scale * (output + b2_ref[...] - rad_ref[m, :].astype(jnp.float32))
-        alive = lax.broadcasted_iota(jnp.int32, (ROWS, 1), 0) + n * ROWS < count_ref[0]
-        rad_ref[m, :] = jnp.where(alive, misfit, 0.0).astype(jnp.bfloat16)
     for i in range(hid // CHUNK):
         part = pl.ds(i * CHUNK, CHUNK)
         for m in blocks:
@@ -129,15 +124,25 @@
         )
         prof_ref[m, :] = grads.astype(jnp.bfloat16)
     grads = prof_ref[...]
-    placed = jnp.dot(placing, grads, preferred_element_type=jnp.float32).astype(jnp.bfloat16)
     parts = width // LANES
-    for k in range(parts):
-        out_ref[:, k * pool : (k + 1) * pool, :] = placed[
-            :, k * LANES : (k + 1) * LANES
-        ].reshape(inner, pool, LANES)
+    wide = ROWS // pool
     out_ref[:, parts * pool :, :] = jnp.broadcast_to(
         labels.reshape(inner, 1, LANES), (inner, LABEL_ROWS, LANES)
     ).astype(jnp.bfloat16)
+    sent = []
+    for n in range(inner // wide):
+        placed = jnp.dot(
+            placing[n * ROWS : (n + 1) * ROWS], grads, preferred_element_type=jnp.float32
+        ).astype(jnp.bfloat16)
+        some = pl.ds(n * wide, wide)
+        for k in range(parts):
+            out_ref[some, k * pool : (k + 1) * pool, :] = placed[
+                :, k * LANES : (k + 1) * LANES
+            ].reshape(wide, pool, LANES)
+        sent.append(pltpu.make_async_copy(out_ref.at[some], out_hbm.at[some], out_sems.at[n]))
+        sent[-1].start()
+    for copy in sent:
+        copy.wait()
 
 
 def blocks_kernel(tiles, most, me_ref, got_ref, own_ref, other_ref):
@@ -194,7 +199,7 @@
         functools.partial(rows_kernel, tiles, most),
         out_shape=jax.ShapeDtypeStruct((inner, high, LANES), jnp.bfloat16),
         in_specs=[smem, smem, vmem, vmem] + [anywhere] * 7,
-        out_specs=vmem,
+        out_specs=anywhere,
         scratch_shapes=[
             pltpu.VMEM((rows, width), jnp.bfloat16),
             pltpu.VMEM((rows, chan), jnp.bfloat16),
@@ -205,7 +210,9 @@
             pltpu.VMEM((1, chan), jnp.float32),
             pltpu.VMEM((rows, hid), jnp.bfloat16),
             pltpu.VMEM((rows, hid), jnp.float32),
-            pltpu.SemaphoreType.DMA((8,)),
+            pltpu.VMEM((inner, high, LANES), jnp.bfloat16),
+            pltpu.SemaphoreType.DMA((10,)),
+            pltpu.SemaphoreType.DMA((inner * pool // ROWS,)),
         ],
         compiler_params=pltpu.CompilerParams(vmem_limit_bytes=60 * 1024 * 1024),
         name="rows_kernel",

time: 42.9 us -> 43 us (level)
  no operation moved by 1% of the time
where the time goes in v10:
time: 43 us; the launch traced here: 42.8 us
  blocking collectives  20 us (47%)
  Pallas kernels  14.3 us (33%)
  waiting for transfers between devices  4.45 us (10%)
  starting transfers between devices  2.66 us (6%)
  other arithmetic  0.7 us (2%)
  between operations  0.67 us (2%)
    all_to_all x1, blocking collectives, per_device(): lax.all_to_all(bucket, 'tile', split_axis=0, concat_axis=0, axis_index_gr...  20 us
    pallas_call x1, Pallas kernels, per_device(): pl.pallas_call(functools.partial(rows_kernel, tiles, most), out_shape=jax...  13.7 us
    ppermute x1, waiting for transfers between devices, per_device(): return own + lax.ppermute(other, 'tile', pairs).astype(jnp.float32)  4.45 us
    ppermute x1, starting transfers between devices, per_device(): return own + lax.ppermute(other, 'tile', pairs).astype(jnp.float32)  2.66 us
  transfers between devices with their start and end apart: 1, of which 1 were waited for; matrix products, arithmetic and copies ran while one was open for 0% of the time, Pallas kernels for 0%

profile of v10, /device:TPU:0, one launch (start us, length us, event | category | flops | bytes accessed | tf_op | source)
XLA Modules:
  0.0 42.8 jit_solution(9136488033412819015)
XLA Ops:
  0.7 13.7 %rows_kernel.1 = bf16[16,200,128]{2,1,0:T(8,128)(2,1)} custom-call(s32[1]{0:T(128)} %bitcast.me_ref, s32[1]{0:T(128)S(6)} %copy.11.count_ref, s32[1,512]{1,0:T(1,128)} %bitcast.7, s32[1,512]{1,0:T(1,128)} %bitcast.8, bf16[512,384]{1,0:T(8,128)(2,1)} %prof_hbm.1, bf16[512,512]{1,0:T(8,128)(2,1)} %rad_hbm.1, bf16[384,4096]{1,0:T(8,128)(2,1)} %w1_hbm.1, ...), custom_call_target="tpu_custom_call" | custom-call | tf_op jit(solution)/shard_map/rows_kernel/pallas_call | solution.py:198
  14.3 20.0 %all_to_all.5.got_ref = bf16[16,200,128]{2,1,0:T(8,128)(2,1)S(1)} all-to-all(bf16[16,200,128]{2,1,0:T(8,128)(2,1)} %rows_kernel.1), channel_id=1, replica_groups={{0,1,2,3,4,5,6,7,8,9,10,11,12,13,14,15},{16,17,18,19,20,21,22,23,24,25,..., dimensions={0} | all-to-all | bytes 1638400 | tf_op jit(solution)/shard_map/all_to_all | solution.py:233
  34.3 0.6 %blocks_kernel.1 = (f32[128,384]{1,0:T(8,128)S(1)}, bf16[128,384]{1,0:T(8,128)(2,1)S(1)}) custom-call(s32[1]{0:T(128)} %bitcast.me_ref, bf16[16,200,128]{2,1,0:T(8,128)(2,1)S(1)} %all_to_all.5.got_ref), custom_call_target="tpu_custom_call" | custom-call | tf_op jit(solution)/shard_map/blocks_kernel/pallas_call | solution.py:236
  35.0 2.7 %collective-permute-start = (bf16[128,384]{1,0:T(8,128)(2,1)S(1)}, bf16[128,384]{1,0:T(8,128)(2,1)S(1)}, u32[]{:S(2)}, u32[]{:S(2)}) collective-permute-start(bf16[128,384]{1,0:T(8,128)(2,1)S(1)} %get-tuple-element.8), channel_id=1, source_target_pairs={{0,16},{1,17},{2,18},{3,19},{4,20},{5,21},{6,22},{7,23},{8,24},{9,... | collective-permute-start | bytes 294920 | tf_op jit(solution)/shard_map/ppermute | solution.py:248
  37.6 4.5 %collective-permute-done = bf16[128,384]{1,0:T(8,128)(2,1)S(1)} collective-permute-done((bf16[128,384]{1,0:T(8,128)(2,1)S(1)}, bf16[128,384]{1,0:T(8,128)(2,1)S(1)}, u32[]{:S(2)}, u32[]{:S(2)}) %collective-permute-start) | collective-permute-done | bytes 98336 | tf_op jit(solution)/shard_map/ppermute | solution.py:248
  42.1 0.7 %convert_add_fusion = f32[128,384]{1,0:T(8,128)} fusion(f32[128,384]{1,0:T(8,128)S(1)} %get-tuple-element.7, bf16[128,384]{1,0:T(8,128)(2,1)S(1)} %collective-permute-done), kind=kLoop, calls=%fused_computation | loop fusion | flops 98304 | bytes 491520 | tf_op jit(solution)/shard_map/add | solution.py:248
Async XLA Ops:
  35.0 7.1 %collective-permute-start = (bf16[128,384]{1,0:T(8,128)(2,1)S(1)}, bf16[128,384]{1,0:T(8,128)(2,1)S(1)}, u32[]{:S(2)}, u32[]{:S(2)}) collective-permute-start(bf16[128,384]{1,0:T(8,128)(2,1)S(1)} %get-tuple-element.8), channel_id=1, source_target_pairs={{0,16},{1,17},{2,18},{3,19},{4,20},{5,21},{6,22},{7,23},{8,24},{9,... | collective-permute-start | bytes 294920 | tf_op jit(solution)/shard_map/ppermute | solution.py:248

commit v11 on v10

--- a/solution.py
+++ b/solution.py
@@ -11,6 +11,7 @@
 CHUNK = 512
 LANES = 128
 LABEL_ROWS = 8
+LOG2E = 1.4426950408889634
 OUTER = 2
 ROWS = 256
 NT = (((1,), (1,)), ((), ()))
@@ -66,22 +67,21 @@
 
     copies[0].wait()
     copies[1].wait()
-    prof_ref[...] = (prof_ref[...].astype(jnp.float32) * 0.5).astype(jnp.bfloat16)
     blocks = [pl.ds(i, ROWS) for i in range(0, rows, ROWS)]
     for i in range(hid // CHUNK):
         part = pl.ds(i * CHUNK, CHUNK)
         if i * CHUNK in starts:
             copies[2 + starts.index(i * CHUNK)].wait()
         for m in blocks:
-            u = jnp.dot(prof_ref[m, :], w1_ref[:, part], preferred_element_type=jnp.float32)
-            u = u + 0.5 * b1_ref[:, part]
-            p = jnp.tanh(u) + 1.0
-            hidden = u * p
+            x = jnp.dot(prof_ref[m, :], w1_ref[:, part], preferred_element_type=jnp.float32)
+            x = x + b1_ref[:, part]
+            sigma = pl.reciprocal(1.0 + jnp.exp2(x * -LOG2E), approx=True)
+            hidden = x * sigma
             hidden_ref[m, part] = hidden.astype(jnp.bfloat16)
-            factor_ref[m, part] = p + hidden * (2.0 - p)
+            factor_ref[m, part] = sigma + hidden * (1.0 - sigma)
     for copy in copies[2 + len(pieces) :]:
         copy.wait()
-    scale = 0.5 * cw_ref[...]
+    scale = cw_ref[...]
     for n, m in enumerate(blocks):
         output = jnp.dot(hidden_ref[m, :], w2_ref[...], preferred_element_type=jnp.float32)
         misfit = scale * (output + b2_ref[...] - rad_ref[m, :].astype(jnp.float32))

time: 43 us -> 43.7 us (1.016)
  Pallas kernels: 14.3 us -> 15 us
    pallas_call x1, Pallas kernels: 13.7 us -> 14.3 us  [per_device(): pl.pallas_call(functools.partial(rows_kernel, tiles, most), out_shape=jax...]
where the time goes in v11:
time: 43.7 us; the launch traced here: 43.5 us
  blocking collectives  20 us (46%)
  Pallas kernels  15 us (34%)
  waiting for transfers between devices  4.46 us (10%)
  starting transfers between devices  2.65 us (6%)
  other arithmetic  0.7 us (2%)
  between operations  0.67 us (2%)
    all_to_all x1, blocking collectives, per_device(): lax.all_to_all(bucket, 'tile', split_axis=0, concat_axis=0, axis_index_gr...  20 us
    pallas_call x1, Pallas kernels, per_device(): pl.pallas_call(functools.partial(rows_kernel, tiles, most), out_shape=jax...  14.3 us
    ppermute x1, waiting for transfers between devices, per_device(): return own + lax.ppermute(other, 'tile', pairs).astype(jnp.float32)  4.46 us
    ppermute x1, starting transfers between devices, per_device(): return own + lax.ppermute(other, 'tile', pairs).astype(jnp.float32)  2.65 us
  transfers between devices with their start and end apart: 1, of which 1 were waited for; matrix products, arithmetic and copies ran while one was open for 0% of the time, Pallas kernels for 0%

profile of v11, /device:TPU:0, one launch (start us, length us, event | category | flops | bytes accessed | tf_op | source)
XLA Modules:
  0.0 43.5 jit_solution(6846464880127631310)
XLA Ops:
  0.7 14.3 %rows_kernel.1 = bf16[16,200,128]{2,1,0:T(8,128)(2,1)} custom-call(s32[1]{0:T(128)} %bitcast.me_ref, s32[1]{0:T(128)S(6)} %copy.11.count_ref, s32[1,512]{1,0:T(1,128)} %bitcast.7, s32[1,512]{1,0:T(1,128)} %bitcast.8, bf16[512,384]{1,0:T(8,128)(2,1)} %prof_hbm.1, bf16[512,512]{1,0:T(8,128)(2,1)} %rad_hbm.1, bf16[384,4096]{1,0:T(8,128)(2,1)} %w1_hbm.1, ...), custom_call_target="tpu_custom_call" | custom-call | tf_op jit(solution)/shard_map/rows_kernel/pallas_call | solution.py:198
  15.0 20.0 %all_to_all.5.got_ref = bf16[16,200,128]{2,1,0:T(8,128)(2,1)S(1)} all-to-all(bf16[16,200,128]{2,1,0:T(8,128)(2,1)} %rows_kernel.1), channel_id=1, replica_groups={{0,1,2,3,4,5,6,7,8,9,10,11,12,13,14,15},{16,17,18,19,20,21,22,23,24,25,..., dimensions={0} | all-to-all | bytes 1638400 | tf_op jit(solution)/shard_map/all_to_all | solution.py:233
  35.0 0.6 %blocks_kernel.1 = (f32[128,384]{1,0:T(8,128)S(1)}, bf16[128,384]{1,0:T(8,128)(2,1)S(1)}) custom-call(s32[1]{0:T(128)} %bitcast.me_ref, bf16[16,200,128]{2,1,0:T(8,128)(2,1)S(1)} %all_to_all.5.got_ref), custom_call_target="tpu_custom_call" | custom-call | tf_op jit(solution)/shard_map/blocks_kernel/pallas_call | solution.py:236
  35.6 2.6 %collective-permute-start = (bf16[128,384]{1,0:T(8,128)(2,1)S(1)}, bf16[128,384]{1,0:T(8,128)(2,1)S(1)}, u32[]{:S(2)}, u32[]{:S(2)}) collective-permute-start(bf16[128,384]{1,0:T(8,128)(2,1)S(1)} %get-tuple-element.8), channel_id=1, source_target_pairs={{0,16},{1,17},{2,18},{3,19},{4,20},{5,21},{6,22},{7,23},{8,24},{9,... | collective-permute-start | bytes 294920 | tf_op jit(solution)/shard_map/ppermute | solution.py:248
  38.3 4.5 %collective-permute-done = bf16[128,384]{1,0:T(8,128)(2,1)S(1)} collective-permute-done((bf16[128,384]{1,0:T(8,128)(2,1)S(1)}, bf16[128,384]{1,0:T(8,128)(2,1)S(1)}, u32[]{:S(2)}, u32[]{:S(2)}) %collective-permute-start) | collective-permute-done | bytes 98336 | tf_op jit(solution)/shard_map/ppermute | solution.py:248
  42.8 0.7 %convert_add_fusion = f32[128,384]{1,0:T(8,128)} fusion(f32[128,384]{1,0:T(8,128)S(1)} %get-tuple-element.7, bf16[128,384]{1,0:T(8,128)(2,1)S(1)} %collective-permute-done), kind=kLoop, calls=%fused_computation | loop fusion | flops 98304 | bytes 491520 | tf_op jit(solution)/shard_map/add | solution.py:248
Async XLA Ops:
  35.6 7.1 %collective-permute-start = (bf16[128,384]{1,0:T(8,128)(2,1)S(1)}, bf16[128,384]{1,0:T(8,128)(2,1)S(1)}, u32[]{:S(2)}, u32[]{:S(2)}) collective-permute-start(bf16[128,384]{1,0:T(8,128)(2,1)S(1)} %get-tuple-element.8), channel_id=1, source_target_pairs={{0,16},{1,17},{2,18},{3,19},{4,20},{5,21},{6,22},{7,23},{8,24},{9,... | collective-permute-start | bytes 294920 | tf_op jit(solution)/shard_map/ppermute | solution.py:248

commit v12 on v10

--- a/solution.py
+++ b/solution.py
@@ -8,7 +8,7 @@
 from jax.sharding import PartitionSpec as P
 
 COL_DEV = 128
-CHUNK = 512
+CHUNK = 256
 LANES = 128
 LABEL_ROWS = 8
 OUTER = 2
@@ -51,7 +51,7 @@
     rows, width = prof_ref.shape
     hid = w1_ref.shape[1]
     chan = rad_ref.shape[1]
-    starts = [0, CHUNK, 2 * CHUNK, 4 * CHUNK, hid]
+    starts = [0, 2 * CHUNK, 4 * CHUNK, 8 * CHUNK, hid]
     pieces = [pl.ds(lo, hi - lo) for lo, hi in zip(starts[:-1], starts[1:])]
     pairs = (
         [(prof_hbm, prof_ref), (b1_hbm, b1_ref)]

time: 43 us -> 42.9 us (level)
  no operation moved by 1% of the time
where the time goes in v12:
time: 42.9 us; the launch traced here: 42.7 us
  blocking collectives  20 us (47%)
  Pallas kernels  14.2 us (33%)
  waiting for transfers between devices  4.46 us (10%)
  starting transfers between devices  2.66 us (6%)
  other arithmetic  0.7 us (2%)
  between operations  0.67 us (2%)
    all_to_all x1, blocking collectives, per_device(): lax.all_to_all(bucket, 'tile', split_axis=0, concat_axis=0, axis_index_gr...  20 us
    pallas_call x1, Pallas kernels, per_device(): pl.pallas_call(functools.partial(rows_kernel, tiles, most), out_shape=jax...  13.6 us
    ppermute x1, waiting for transfers between devices, per_device(): return own + lax.ppermute(other, 'tile', pairs).astype(jnp.float32)  4.46 us
    ppermute x1, starting transfers between devices, per_device(): return own + lax.ppermute(other, 'tile', pairs).astype(jnp.float32)  2.66 us
  transfers between devices with their start and end apart: 1, of which 1 were waited for; matrix products, arithmetic and copies ran while one was open for 0% of the time, Pallas kernels for 0%

profile of v12, /device:TPU:0, one launch (start us, length us, event | category | flops | bytes accessed | tf_op | source)
XLA Modules:
  0.0 42.7 jit_solution(18409561265428903290)
XLA Ops:
  0.7 13.6 %rows_kernel.1 = bf16[16,200,128]{2,1,0:T(8,128)(2,1)} custom-call(s32[1]{0:T(128)} %bitcast.me_ref, s32[1]{0:T(128)S(6)} %copy.11.count_ref, s32[1,512]{1,0:T(1,128)} %bitcast.7, s32[1,512]{1,0:T(1,128)} %bitcast.8, bf16[512,384]{1,0:T(8,128)(2,1)} %prof_hbm.1, bf16[512,512]{1,0:T(8,128)(2,1)} %rad_hbm.1, bf16[384,4096]{1,0:T(8,128)(2,1)} %w1_hbm.1, ...), custom_call_target="tpu_custom_call" | custom-call | tf_op jit(solution)/shard_map/rows_kernel/pallas_call | solution.py:198
  14.3 20.0 %all_to_all.5.got_ref = bf16[16,200,128]{2,1,0:T(8,128)(2,1)S(1)} all-to-all(bf16[16,200,128]{2,1,0:T(8,128)(2,1)} %rows_kernel.1), channel_id=1, replica_groups={{0,1,2,3,4,5,6,7,8,9,10,11,12,13,14,15},{16,17,18,19,20,21,22,23,24,25,..., dimensions={0} | all-to-all | bytes 1638400 | tf_op jit(solution)/shard_map/all_to_all | solution.py:233
  34.3 0.6 %blocks_kernel.1 = (f32[128,384]{1,0:T(8,128)S(1)}, bf16[128,384]{1,0:T(8,128)(2,1)S(1)}) custom-call(s32[1]{0:T(128)} %bitcast.me_ref, bf16[16,200,128]{2,1,0:T(8,128)(2,1)S(1)} %all_to_all.5.got_ref), custom_call_target="tpu_custom_call" | custom-call | tf_op jit(solution)/shard_map/blocks_kernel/pallas_call | solution.py:236
  34.9 2.7 %collective-permute-start = (bf16[128,384]{1,0:T(8,128)(2,1)S(1)}, bf16[128,384]{1,0:T(8,128)(2,1)S(1)}, u32[]{:S(2)}, u32[]{:S(2)}) collective-permute-start(bf16[128,384]{1,0:T(8,128)(2,1)S(1)} %get-tuple-element.8), channel_id=1, source_target_pairs={{0,16},{1,17},{2,18},{3,19},{4,20},{5,21},{6,22},{7,23},{8,24},{9,... | collective-permute-start | bytes 294920 | tf_op jit(solution)/shard_map/ppermute | solution.py:248
  37.5 4.5 %collective-permute-done = bf16[128,384]{1,0:T(8,128)(2,1)S(1)} collective-permute-done((bf16[128,384]{1,0:T(8,128)(2,1)S(1)}, bf16[128,384]{1,0:T(8,128)(2,1)S(1)}, u32[]{:S(2)}, u32[]{:S(2)}) %collective-permute-start) | collective-permute-done | bytes 98336 | tf_op jit(solution)/shard_map/ppermute | solution.py:248
  42.0 0.7 %convert_add_fusion = f32[128,384]{1,0:T(8,128)} fusion(f32[128,384]{1,0:T(8,128)S(1)} %get-tuple-element.7, bf16[128,384]{1,0:T(8,128)(2,1)S(1)} %collective-permute-done), kind=kLoop, calls=%fused_computation | loop fusion | flops 98304 | bytes 491520 | tf_op jit(solution)/shard_map/add | solution.py:248
Async XLA Ops:
  34.9 7.1 %collective-permute-start = (bf16[128,384]{1,0:T(8,128)(2,1)S(1)}, bf16[128,384]{1,0:T(8,128)(2,1)S(1)}, u32[]{:S(2)}, u32[]{:S(2)}) collective-permute-start(bf16[128,384]{1,0:T(8,128)(2,1)S(1)} %get-tuple-element.8), channel_id=1, source_target_pairs={{0,16},{1,17},{2,18},{3,19},{4,20},{5,21},{6,22},{7,23},{8,24},{9,... | collective-permute-start | bytes 294920 | tf_op jit(solution)/shard_map/ppermute | solution.py:248

commit v13 on v12

--- a/solution.py
+++ b/solution.py
@@ -51,7 +51,7 @@
     rows, width = prof_ref.shape
     hid = w1_ref.shape[1]
     chan = rad_ref.shape[1]
-    starts = [0, 2 * CHUNK, 4 * CHUNK, 8 * CHUNK, hid]
+    starts = [0, hid // 4, hid]
     pieces = [pl.ds(lo, hi - lo) for lo, hi in zip(starts[:-1], starts[1:])]
     pairs = (
         [(prof_hbm, prof_ref), (b1_hbm, b1_ref)]
@@ -63,6 +63,35 @@
     ]
     for copy in copies:
         copy.start()
+
+    inner = out_ref.shape[0]
+    live = lax.broadcasted_iota(jnp.int32, (1, rows), 1) < count_ref[0]
+    owner = jnp.where(live, owner_ref[...], -1)
+    mine = lax.broadcasted_iota(jnp.int32, (tiles, rows), 0) == owner
+    one_hot = mine.astype(jnp.float32)
+    upper = as_bf16(
+        lax.broadcasted_iota(jnp.int32, (rows, rows), 0)
+        <= lax.broadcasted_iota(jnp.int32, (rows, rows), 1)
+    )
+    running = jnp.dot(one_hot.astype(jnp.bfloat16), upper, preferred_element_type=jnp.float32)
+    rank = jnp.sum(running * one_hot, axis=0, keepdims=True).astype(jnp.int32) - 1
+    pool = tiles // inner * most
+    place = owner & (inner - 1)
+    order = lax.shift_right_arithmetic(owner, inner.bit_length() - 1) * most + rank
+    slot = jnp.where(live, place * pool + order, -1)
+    placing = as_bf16(lax.broadcasted_iota(jnp.int32, (inner * pool, rows), 0) == slot)
+    lane = order + lax.rem(me_ref[0], LANES // pool) * pool
+    lane_hot = as_bf16(lax.broadcasted_iota(jnp.int32, (LANES, rows), 0) == lane)
+    here = live & (lax.broadcasted_iota(jnp.int32, (inner, rows), 0) == place)
+    marked = jnp.where(here, (column_ref[...] + 1).astype(jnp.float32), 0.0)
+    labels = lax.dot_general(
+        marked.astype(jnp.bfloat16), lane_hot, NT, preferred_element_type=jnp.float32
+    )
+
+    parts = width // LANES
+    out_ref[:, parts * pool :, :] = jnp.broadcast_to(
+        labels.reshape(inner, 1, LANES), (inner, LABEL_ROWS, LANES)
+    ).astype(jnp.bfloat16)
 
     copies[0].wait()
     copies[1].wait()
@@ -87,30 +116,6 @@
         misfit = scale * (output + b2_ref[...] - rad_ref[m, :].astype(jnp.float32))
         alive = lax.broadcasted_iota(jnp.int32, (ROWS, 1), 0) + n * ROWS < count_ref[0]
         rad_ref[m, :] = jnp.where(alive, misfit, 0.0).astype(jnp.bfloat16)
-    inner = out_ref.shape[0]
-    live = lax.broadcasted_iota(jnp.int32, (1, rows), 1) < count_ref[0]
-    owner = jnp.where(live, owner_ref[...], -1)
-    mine = lax.broadcasted_iota(jnp.int32, (tiles, rows), 0) == owner
-    one_hot = mine.astype(jnp.float32)
-    upper = as_bf16(
-        lax.broadcasted_iota(jnp.int32, (rows, rows), 0)
-        <= lax.broadcasted_iota(jnp.int32, (rows, rows), 1)
-    )
-    running = jnp.dot(one_hot.astype(jnp.bfloat16), upper, preferred_element_type=jnp.float32)
-    rank = jnp.sum(running * one_hot, axis=0, keepdims=True).astype(jnp.int32) - 1
-    pool = tiles // inner * most
-    place = owner & (inner - 1)
-    order = lax.shift_right_arithmetic(owner, inner.bit_length() - 1) * most + rank
-    slot = jnp.where(live, place * pool + order, -1)
-    placing = as_bf16(lax.broadcasted_iota(jnp.int32, (inner * pool, rows), 0) == slot)
-    lane = order + lax.rem(me_ref[0], LANES // pool) * pool
-    lane_hot = as_bf16(lax.broadcasted_iota(jnp.int32, (LANES, rows), 0) == lane)
-    here = live & (lax.broadcasted_iota(jnp.int32, (inner, rows), 0) == place)
-    marked = jnp.where(here, (column_ref[...] + 1).astype(jnp.float32), 0.0)
-    labels = lax.dot_general(
-        marked.astype(jnp.bfloat16), lane_hot, NT, preferred_element_type=jnp.float32
-    )
-
     for i in range(hid // CHUNK):
         part = pl.ds(i * CHUNK, CHUNK)
         for m in blocks:
@@ -124,11 +129,7 @@
         )
         prof_ref[m, :] = grads.astype(jnp.bfloat16)
     grads = prof_ref[...]
-    parts = width // LANES
     wide = ROWS // pool
-    out_ref[:, parts * pool :, :] = jnp.broadcast_to(
-        labels.reshape(inner, 1, LANES), (inner, LABEL_ROWS, LANES)
-    ).astype(jnp.bfloat16)
     sent = []
     for n in range(inner // wide):
         placed = jnp.dot(
@@ -211,7 +212,7 @@
             pltpu.VMEM((rows, hid), jnp.bfloat16),
             pltpu.VMEM((rows, hid), jnp.float32),
             pltpu.VMEM((inner, high, LANES), jnp.bfloat16),
-            pltpu.SemaphoreType.DMA((10,)),
+            pltpu.SemaphoreType.DMA((8,)),
             pltpu.SemaphoreType.DMA((inner * pool // ROWS,)),
         ],
         compiler_params=pltpu.CompilerParams(vmem_limit_bytes=60 * 1024 * 1024),

time: 42.9 us -> 42.4 us (0.988)
  Pallas kernels: 14.2 us -> 13.6 us
    pallas_call x1, Pallas kernels: 13.6 us -> 13 us  [per_device(): pl.pallas_call(functools.partial(rows_kernel, tiles, most), out_shape=jax...]
where the time goes in v13:
time: 42.4 us; the launch traced here: 42.1 us
  blocking collectives  20 us (47%)
  Pallas kernels  13.6 us (32%)
  waiting for transfers between devices  4.47 us (11%)
  starting transfers between devices  2.65 us (6%)
  other arithmetic  0.7 us (2%)
  between operations  0.67 us (2%)
    all_to_all x1, blocking collectives, per_device(): lax.all_to_all(bucket, 'tile', split_axis=0, concat_axis=0, axis_index_gr...  20 us
    pallas_call x1, Pallas kernels, per_device(): pl.pallas_call(functools.partial(rows_kernel, tiles, most), out_shape=jax...  13 us
    ppermute x1, waiting for transfers between devices, per_device(): return own + lax.ppermute(other, 'tile', pairs).astype(jnp.float32)  4.47 us
    ppermute x1, starting transfers between devices, per_device(): return own + lax.ppermute(other, 'tile', pairs).astype(jnp.float32)  2.65 us
  transfers between devices with their start and end apart: 1, of which 1 were waited for; matrix products, arithmetic and copies ran while one was open for 0% of the time, Pallas kernels for 0%

profile of v13, /device:TPU:0, one launch (start us, length us, event | category | flops | bytes accessed | tf_op | source)
XLA Modules:
  0.0 42.1 jit_solution(11978682363403563464)
XLA Ops:
  0.7 13.0 %rows_kernel.1 = bf16[16,200,128]{2,1,0:T(8,128)(2,1)} custom-call(s32[1]{0:T(128)} %bitcast.me_ref, s32[1]{0:T(128)S(6)} %copy.11.count_ref, s32[1,512]{1,0:T(1,128)} %bitcast.7, s32[1,512]{1,0:T(1,128)} %bitcast.8, bf16[512,384]{1,0:T(8,128)(2,1)} %prof_hbm.1, bf16[512,512]{1,0:T(8,128)(2,1)} %rad_hbm.1, bf16[384,4096]{1,0:T(8,128)(2,1)} %w1_hbm.1, ...), custom_call_target="tpu_custom_call" | custom-call | tf_op jit(solution)/shard_map/rows_kernel/pallas_call | solution.py:199
  13.7 20.0 %all_to_all.5.got_ref = bf16[16,200,128]{2,1,0:T(8,128)(2,1)S(1)} all-to-all(bf16[16,200,128]{2,1,0:T(8,128)(2,1)} %rows_kernel.1), channel_id=1, replica_groups={{0,1,2,3,4,5,6,7,8,9,10,11,12,13,14,15},{16,17,18,19,20,21,22,23,24,25,..., dimensions={0} | all-to-all | bytes 1638400 | tf_op jit(solution)/shard_map/all_to_all | solution.py:234
  33.7 0.6 %blocks_kernel.1 = (f32[128,384]{1,0:T(8,128)S(1)}, bf16[128,384]{1,0:T(8,128)(2,1)S(1)}) custom-call(s32[1]{0:T(128)} %bitcast.me_ref, bf16[16,200,128]{2,1,0:T(8,128)(2,1)S(1)} %all_to_all.5.got_ref), custom_call_target="tpu_custom_call" | custom-call | tf_op jit(solution)/shard_map/blocks_kernel/pallas_call | solution.py:237
  34.3 2.6 %collective-permute-start = (bf16[128,384]{1,0:T(8,128)(2,1)S(1)}, bf16[128,384]{1,0:T(8,128)(2,1)S(1)}, u32[]{:S(2)}, u32[]{:S(2)}) collective-permute-start(bf16[128,384]{1,0:T(8,128)(2,1)S(1)} %get-tuple-element.8), channel_id=1, source_target_pairs={{0,16},{1,17},{2,18},{3,19},{4,20},{5,21},{6,22},{7,23},{8,24},{9,... | collective-permute-start | bytes 294920 | tf_op jit(solution)/shard_map/ppermute | solution.py:249
  37.0 4.5 %collective-permute-done = bf16[128,384]{1,0:T(8,128)(2,1)S(1)} collective-permute-done((bf16[128,384]{1,0:T(8,128)(2,1)S(1)}, bf16[128,384]{1,0:T(8,128)(2,1)S(1)}, u32[]{:S(2)}, u32[]{:S(2)}) %collective-permute-start) | collective-permute-done | bytes 98336 | tf_op jit(solution)/shard_map/ppermute | solution.py:249
  41.4 0.7 %convert_add_fusion = f32[128,384]{1,0:T(8,128)} fusion(f32[128,384]{1,0:T(8,128)S(1)} %get-tuple-element.7, bf16[128,384]{1,0:T(8,128)(2,1)S(1)} %collective-permute-done), kind=kLoop, calls=%fused_computation | loop fusion | flops 98304 | bytes 491520 | tf_op jit(solution)/shard_map/add | solution.py:249
Async XLA Ops:
  34.3 7.1 %collective-permute-start = (bf16[128,384]{1,0:T(8,128)(2,1)S(1)}, bf16[128,384]{1,0:T(8,128)(2,1)S(1)}, u32[]{:S(2)}, u32[]{:S(2)}) collective-permute-start(bf16[128,384]{1,0:T(8,128)(2,1)S(1)} %get-tuple-element.8), channel_id=1, source_target_pairs={{0,16},{1,17},{2,18},{3,19},{4,20},{5,21},{6,22},{7,23},{8,24},{9,... | collective-permute-start | bytes 294920 | tf_op jit(solution)/shard_map/ppermute | solution.py:249

commit v14 on v13

--- a/solution.py
+++ b/solution.py
@@ -36,6 +36,7 @@
     cw_hbm,
     out_hbm,
     prof_ref,
+    half_ref,
     rad_ref,
     w1_ref,
     b1_ref,
@@ -51,7 +52,7 @@
     rows, width = prof_ref.shape
     hid = w1_ref.shape[1]
     chan = rad_ref.shape[1]
-    starts = [0, hid // 4, hid]
+    starts = [0, hid // 2, hid]
     pieces = [pl.ds(lo, hi - lo) for lo, hi in zip(starts[:-1], starts[1:])]
     pairs = (
         [(prof_hbm, prof_ref), (b1_hbm, b1_ref)]
@@ -95,39 +96,67 @@
 
     copies[0].wait()
     copies[1].wait()
-    prof_ref[...] = (prof_ref[...].astype(jnp.float32) * 0.5).astype(jnp.bfloat16)
-    blocks = [pl.ds(i, ROWS) for i in range(0, rows, ROWS)]
-    for i in range(hid // CHUNK):
-        part = pl.ds(i * CHUNK, CHUNK)
-        if i * CHUNK in starts:
-            copies[2 + starts.index(i * CHUNK)].wait()
-        for m in blocks:
-            u = jnp.dot(prof_ref[m, :], w1_ref[:, part], preferred_element_type=jnp.float32)
+    half_ref[...] = (prof_ref[...].astype(jnp.float32) * 0.5).astype(jnp.bfloat16)
+    count = hid // CHUNK
+
+    def rows_of(m):
+        return pl.ds(m * ROWS, ROWS)
+
+    def enter(m, first, last):
+        for i in range(first, last):
+            part = pl.ds(i * CHUNK, CHUNK)
+            u = jnp.dot(
+                half_ref[rows_of(m), :], w1_ref[:, part], preferred_element_type=jnp.float32
+            )
             u = u + 0.5 * b1_ref[:, part]
             p = jnp.tanh(u) + 1.0
             hidden = u * p
-            hidden_ref[m, part] = hidden.astype(jnp.bfloat16)
-            factor_ref[m, part] = p + hidden * (2.0 - p)
+            hidden_ref[rows_of(m), part] = hidden.astype(jnp.bfloat16)
+            factor_ref[rows_of(m), part] = p + hidden * (2.0 - p)
+
+    def leave(m, n):
+        part = pl.ds(n * CHUNK, CHUNK)
+        output = jnp.dot(
+            hidden_ref[rows_of(m), :], w2_ref[:, part], preferred_element_type=jnp.float32
+        )
+        misfit = output + b2_ref[:, part] - rad_ref[rows_of(m), part].astype(jnp.float32)
+        misfit = (0.5 * cw_ref[:, part]) * misfit
+        alive = lax.broadcasted_iota(jnp.int32, (ROWS, 1), 0) + m * ROWS < count_ref[0]
+        rad_ref[rows_of(m), part] = jnp.where(alive, misfit, 0.0).astype(jnp.bfloat16)
+
+    def enter_back(m, first, last):
+        for i in range(first, last):
+            part = pl.ds(i * CHUNK, CHUNK)
+            back = lax.dot_general(
+                rad_ref[rows_of(m), :], w2_ref[part, :], NT, preferred_element_type=jnp.float32
+            )
+            back = back * factor_ref[rows_of(m), part]
+            hidden_ref[rows_of(m), part] = back.astype(jnp.bfloat16)
+
+    def leave_back(m):
+        grads = lax.dot_general(
+            hidden_ref[rows_of(m), :], w1_ref[...], NT, preferred_element_type=jnp.float32
+        )
+        prof_ref[rows_of(m), :] = grads.astype(jnp.bfloat16)
+
+    copies[2].wait()
+    enter(0, 0, count // 2)
+    copies[3].wait()
+    enter(0, count // 2, count)
+    enter(1, 0, count // 4)
     for copy in copies[2 + len(pieces) :]:
         copy.wait()
-    scale = 0.5 * cw_ref[...]
-    for n, m in enumerate(blocks):
-        output = jnp.dot(hidden_ref[m, :], w2_ref[...], preferred_element_type=jnp.float32)
-        misfit = scale * (output + b2_ref[...] - rad_ref[m, :].astype(jnp.float32))
-        alive = lax.broadcasted_iota(jnp.int32, (ROWS, 1), 0) + n * ROWS < count_ref[0]
-        rad_ref[m, :] = jnp.where(alive, misfit, 0.0).astype(jnp.bfloat16)
-    for i in range(hid // CHUNK):
-        part = pl.ds(i * CHUNK, CHUNK)
-        for m in blocks:
-            back = lax.dot_general(
-                rad_ref[m, :], w2_ref[part, :], NT, preferred_element_type=jnp.float32
-            )
-            hidden_ref[m, part] = (back * factor_ref[m, part]).astype(jnp.bfloat16)
-    for m in blocks:
-        grads = lax.dot_general(
-            hidden_ref[m, :], w1_ref[...], NT, preferred_element_type=jnp.float32
-        )
-        prof_ref[m, :] = grads.astype(jnp.bfloat16)
+    leave(0, 0)
+    enter(1, count // 4, count // 2)
+    leave(0, 1)
+    enter(1, count // 2, count)
+    leave(1, 0)
+    enter_back(0, 0, count // 2)
+    leave(1, 1)
+    enter_back(0, count // 2, count)
+    leave_back(0)
+    enter_back(1, 0, count)
+    leave_back(1)
     grads = prof_ref[...]
     wide = ROWS // pool
     sent = []
@@ -203,6 +232,7 @@
         out_specs=anywhere,
         scratch_shapes=[
             pltpu.VMEM((rows, width), jnp.bfloat16),
+            pltpu.VMEM((rows, width), jnp.bfloat16),
             pltpu.VMEM((rows, chan), jnp.bfloat16),
             pltpu.VMEM((width, hid), jnp.bfloat16),
             pltpu.VMEM((1, hid), jnp.float32),

time: 42.4 us -> 42.7 us (level)
  no operation moved by 1% of the time
where the time goes in v14:
time: 42.7 us; the launch traced here: 42.5 us
  blocking collectives  20 us (47%)
  Pallas kernels  14 us (33%)
  waiting for transfers between devices  4.47 us (10%)
  starting transfers between devices  2.65 us (6%)
  other arithmetic  0.7 us (2%)
  between operations  0.67 us (2%)
    all_to_all x1, blocking collectives, per_device(): lax.all_to_all(bucket, 'tile', split_axis=0, concat_axis=0, axis_index_gr...  20 us
    pallas_call x1, Pallas kernels, per_device(): pl.pallas_call(functools.partial(rows_kernel, tiles, most), out_shape=jax...  13.4 us
    ppermute x1, waiting for transfers between devices, per_device(): return own + lax.ppermute(other, 'tile', pairs).astype(jnp.float32)  4.47 us
    ppermute x1, starting transfers between devices, per_device(): return own + lax.ppermute(other, 'tile', pairs).astype(jnp.float32)  2.65 us
  transfers between devices with their start and end apart: 1, of which 1 were waited for; matrix products, arithmetic and copies ran while one was open for 0% of the time, Pallas kernels for 0%

profile of v14, /device:TPU:0, one launch (start us, length us, event | category | flops | bytes accessed | tf_op | source)
XLA Modules:
  0.0 42.5 jit_solution(6053539610348428728)
XLA Ops:
  0.7 13.4 %rows_kernel.1 = bf16[16,200,128]{2,1,0:T(8,128)(2,1)} custom-call(s32[1]{0:T(128)} %bitcast.me_ref, s32[1]{0:T(128)S(6)} %copy.11.count_ref, s32[1,512]{1,0:T(1,128)} %bitcast.7, s32[1,512]{1,0:T(1,128)} %bitcast.8, bf16[512,384]{1,0:T(8,128)(2,1)} %prof_hbm.1, bf16[512,512]{1,0:T(8,128)(2,1)} %rad_hbm.1, bf16[384,4096]{1,0:T(8,128)(2,1)} %w1_hbm.1, ...), custom_call_target="tpu_custom_call" | custom-call | tf_op jit(solution)/shard_map/rows_kernel/pallas_call | solution.py:228
  14.0 20.0 %all_to_all.5.got_ref = bf16[16,200,128]{2,1,0:T(8,128)(2,1)S(1)} all-to-all(bf16[16,200,128]{2,1,0:T(8,128)(2,1)} %rows_kernel.1), channel_id=1, replica_groups={{0,1,2,3,4,5,6,7,8,9,10,11,12,13,14,15},{16,17,18,19,20,21,22,23,24,25,..., dimensions={0} | all-to-all | bytes 1638400 | tf_op jit(solution)/shard_map/all_to_all | solution.py:264
  34.0 0.6 %blocks_kernel.1 = (f32[128,384]{1,0:T(8,128)S(1)}, bf16[128,384]{1,0:T(8,128)(2,1)S(1)}) custom-call(s32[1]{0:T(128)} %bitcast.me_ref, bf16[16,200,128]{2,1,0:T(8,128)(2,1)S(1)} %all_to_all.5.got_ref), custom_call_target="tpu_custom_call" | custom-call | tf_op jit(solution)/shard_map/blocks_kernel/pallas_call | solution.py:267
  34.7 2.6 %collective-permute-start = (bf16[128,384]{1,0:T(8,128)(2,1)S(1)}, bf16[128,384]{1,0:T(8,128)(2,1)S(1)}, u32[]{:S(2)}, u32[]{:S(2)}) collective-permute-start(bf16[128,384]{1,0:T(8,128)(2,1)S(1)} %get-tuple-element.8), channel_id=1, source_target_pairs={{0,16},{1,17},{2,18},{3,19},{4,20},{5,21},{6,22},{7,23},{8,24},{9,... | collective-permute-start | bytes 294920 | tf_op jit(solution)/shard_map/ppermute | solution.py:279
  37.3 4.5 %collective-permute-done = bf16[128,384]{1,0:T(8,128)(2,1)S(1)} collective-permute-done((bf16[128,384]{1,0:T(8,128)(2,1)S(1)}, bf16[128,384]{1,0:T(8,128)(2,1)S(1)}, u32[]{:S(2)}, u32[]{:S(2)}) %collective-permute-start) | collective-permute-done | bytes 98336 | tf_op jit(solution)/shard_map/ppermute | solution.py:279
  41.8 0.7 %convert_add_fusion = f32[128,384]{1,0:T(8,128)} fusion(f32[128,384]{1,0:T(8,128)S(1)} %get-tuple-element.7, bf16[128,384]{1,0:T(8,128)(2,1)S(1)} %collective-permute-done), kind=kLoop, calls=%fused_computation | loop fusion | flops 98304 | bytes 491520 | tf_op jit(solution)/shard_map/add | solution.py:279
Async XLA Ops:
  34.7 7.1 %collective-permute-start = (bf16[128,384]{1,0:T(8,128)(2,1)S(1)}, bf16[128,384]{1,0:T(8,128)(2,1)S(1)}, u32[]{:S(2)}, u32[]{:S(2)}) collective-permute-start(bf16[128,384]{1,0:T(8,128)(2,1)S(1)} %get-tuple-element.8), channel_id=1, source_target_pairs={{0,16},{1,17},{2,18},{3,19},{4,20},{5,21},{6,22},{7,23},{8,24},{9,... | collective-permute-start | bytes 294920 | tf_op jit(solution)/shard_map/ppermute | solution.py:279

commit v15 on v13

--- a/solution.py
+++ b/solution.py
@@ -97,11 +97,12 @@
     copies[1].wait()
     prof_ref[...] = (prof_ref[...].astype(jnp.float32) * 0.5).astype(jnp.bfloat16)
     blocks = [pl.ds(i, ROWS) for i in range(0, rows, ROWS)]
+    small = [pl.ds(i, ROWS // 2) for i in range(0, rows, ROWS // 2)]
     for i in range(hid // CHUNK):
         part = pl.ds(i * CHUNK, CHUNK)
         if i * CHUNK in starts:
             copies[2 + starts.index(i * CHUNK)].wait()
-        for m in blocks:
+        for m in small:
             u = jnp.dot(prof_ref[m, :], w1_ref[:, part], preferred_element_type=jnp.float32)
             u = u + 0.5 * b1_ref[:, part]
             p = jnp.tanh(u) + 1.0
@@ -118,7 +119,7 @@
         rad_ref[m, :] = jnp.where(alive, misfit, 0.0).astype(jnp.bfloat16)
     for i in range(hid // CHUNK):
         part = pl.ds(i * CHUNK, CHUNK)
-        for m in blocks:
+        for m in small:
             back = lax.dot_general(
                 rad_ref[m, :], w2_ref[part, :], NT, preferred_element_type=jnp.float32
             )

time: 42.4 us -> 45.4 us (1.071)
  Pallas kernels: 13.6 us -> 16.6 us
    pallas_call x1, Pallas kernels: 13 us -> 16 us  [per_device(): pl.pallas_call(functools.partial(rows_kernel, tiles, most), out_shape=jax...]
where the time goes in v15:
time: 45.4 us; the launch traced here: 45.1 us
  blocking collectives  20 us (44%)
  Pallas kernels  16.6 us (37%)
  waiting for transfers between devices  4.46 us (10%)
  starting transfers between devices  2.66 us (6%)
  other arithmetic  0.7 us (2%)
  between operations  0.67 us (1%)
    all_to_all x1, blocking collectives, per_device(): lax.all_to_all(bucket, 'tile', split_axis=0, concat_axis=0, axis_index_gr...  20 us
    pallas_call x1, Pallas kernels, per_device(): pl.pallas_call(functools.partial(rows_kernel, tiles, most), out_shape=jax...  16 us
    ppermute x1, waiting for transfers between devices, per_device(): return own + lax.ppermute(other, 'tile', pairs).astype(jnp.float32)  4.46 us
    ppermute x1, starting transfers between devices, per_device(): return own + lax.ppermute(other, 'tile', pairs).astype(jnp.float32)  2.66 us
  transfers between devices with their start and end apart: 1, of which 1 were waited for; matrix products, arithmetic and copies ran while one was open for 0% of the time, Pallas kernels for 0%

profile of v15, /device:TPU:0, one launch (start us, length us, event | category | flops | bytes accessed | tf_op | source)
XLA Modules:
  0.0 45.1 jit_solution(10618479038887314190)
XLA Ops:
  0.7 16.0 %rows_kernel.1 = bf16[16,200,128]{2,1,0:T(8,128)(2,1)} custom-call(s32[1]{0:T(128)} %bitcast.me_ref, s32[1]{0:T(128)S(6)} %copy.11.count_ref, s32[1,512]{1,0:T(1,128)} %bitcast.7, s32[1,512]{1,0:T(1,128)} %bitcast.8, bf16[512,384]{1,0:T(8,128)(2,1)} %prof_hbm.1, bf16[512,512]{1,0:T(8,128)(2,1)} %rad_hbm.1, bf16[384,4096]{1,0:T(8,128)(2,1)} %w1_hbm.1, ...), custom_call_target="tpu_custom_call" | custom-call | tf_op jit(solution)/shard_map/rows_kernel/pallas_call | solution.py:200
  16.6 20.0 %all_to_all.5.got_ref = bf16[16,200,128]{2,1,0:T(8,128)(2,1)S(1)} all-to-all(bf16[16,200,128]{2,1,0:T(8,128)(2,1)} %rows_kernel.1), channel_id=1, replica_groups={{0,1,2,3,4,5,6,7,8,9,10,11,12,13,14,15},{16,17,18,19,20,21,22,23,24,25,..., dimensions={0} | all-to-all | bytes 1638400 | tf_op jit(solution)/shard_map/all_to_all | solution.py:235
  36.7 0.6 %blocks_kernel.1 = (f32[128,384]{1,0:T(8,128)S(1)}, bf16[128,384]{1,0:T(8,128)(2,1)S(1)}) custom-call(s32[1]{0:T(128)} %bitcast.me_ref, bf16[16,200,128]{2,1,0:T(8,128)(2,1)S(1)} %all_to_all.5.got_ref), custom_call_target="tpu_custom_call" | custom-call | tf_op jit(solution)/shard_map/blocks_kernel/pallas_call | solution.py:238
  37.3 2.7 %collective-permute-start = (bf16[128,384]{1,0:T(8,128)(2,1)S(1)}, bf16[128,384]{1,0:T(8,128)(2,1)S(1)}, u32[]{:S(2)}, u32[]{:S(2)}) collective-permute-start(bf16[128,384]{1,0:T(8,128)(2,1)S(1)} %get-tuple-element.8), channel_id=1, source_target_pairs={{0,16},{1,17},{2,18},{3,19},{4,20},{5,21},{6,22},{7,23},{8,24},{9,... | collective-permute-start | bytes 294920 | tf_op jit(solution)/shard_map/ppermute | solution.py:250
  39.9 4.5 %collective-permute-done = bf16[128,384]{1,0:T(8,128)(2,1)S(1)} collective-permute-done((bf16[128,384]{1,0:T(8,128)(2,1)S(1)}, bf16[128,384]{1,0:T(8,128)(2,1)S(1)}, u32[]{:S(2)}, u32[]{:S(2)}) %collective-permute-start) | collective-permute-done | bytes 98336 | tf_op jit(solution)/shard_map/ppermute | solution.py:250
  44.4 0.7 %convert_add_fusion = f32[128,384]{1,0:T(8,128)} fusion(f32[128,384]{1,0:T(8,128)S(1)} %get-tuple-element.7, bf16[128,384]{1,0:T(8,128)(2,1)S(1)} %collective-permute-done), kind=kLoop, calls=%fused_computation | loop fusion | flops 98304 | bytes 491520 | tf_op jit(solution)/shard_map/add | solution.py:250
Async XLA Ops:
  37.3 7.1 %collective-permute-start = (bf16[128,384]{1,0:T(8,128)(2,1)S(1)}, bf16[128,384]{1,0:T(8,128)(2,1)S(1)}, u32[]{:S(2)}, u32[]{:S(2)}) collective-permute-start(bf16[128,384]{1,0:T(8,128)(2,1)S(1)} %get-tuple-element.8), channel_id=1, source_target_pairs={{0,16},{1,17},{2,18},{3,19},{4,20},{5,21},{6,22},{7,23},{8,24},{9,... | collective-permute-start | bytes 294920 | tf_op jit(solution)/shard_map/ppermute | solution.py:250

commit v16 on v13

--- a/solution.py
+++ b/solution.py
@@ -101,7 +101,7 @@
         part = pl.ds(i * CHUNK, CHUNK)
         if i * CHUNK in starts:
             copies[2 + starts.index(i * CHUNK)].wait()
-        for m in blocks:
+        for m in [pl.ds(0, rows)]:
             u = jnp.dot(prof_ref[m, :], w1_ref[:, part], preferred_element_type=jnp.float32)
             u = u + 0.5 * b1_ref[:, part]
             p = jnp.tanh(u) + 1.0
@@ -118,7 +118,7 @@
         rad_ref[m, :] = jnp.where(alive, misfit, 0.0).astype(jnp.bfloat16)
     for i in range(hid // CHUNK):
         part = pl.ds(i * CHUNK, CHUNK)
-        for m in blocks:
+        for m in [pl.ds(0, rows)]:
             back = lax.dot_general(
                 rad_ref[m, :], w2_ref[part, :], NT, preferred_element_type=jnp.float32
             )

time: 42.4 us -> 42.8 us (level)
  Pallas kernels: 13.6 us -> 14.1 us
where the time goes in v16:
time: 42.8 us; the launch traced here: 42.5 us
  blocking collectives  20 us (47%)
  Pallas kernels  14.1 us (33%)
  waiting for transfers between devices  4.47 us (10%)
  starting transfers between devices  2.65 us (6%)
  other arithmetic  0.7 us (2%)
  between operations  0.67 us (2%)
    all_to_all x1, blocking collectives, per_device(): lax.all_to_all(bucket, 'tile', split_axis=0, concat_axis=0, axis_index_gr...  20 us
    pallas_call x1, Pallas kernels, per_device(): pl.pallas_call(functools.partial(rows_kernel, tiles, most), out_shape=jax...  13.4 us
    ppermute x1, waiting for transfers between devices, per_device(): return own + lax.ppermute(other, 'tile', pairs).astype(jnp.float32)  4.47 us
    ppermute x1, starting transfers between devices, per_device(): return own + lax.ppermute(other, 'tile', pairs).astype(jnp.float32)  2.65 us
  transfers between devices with their start and end apart: 1, of which 1 were waited for; matrix products, arithmetic and copies ran while one was open for 0% of the time, Pallas kernels for 0%

profile of v16, /device:TPU:0, one launch (start us, length us, event | category | flops | bytes accessed | tf_op | source)
XLA Modules:
  0.0 42.5 jit_solution(11548217226565950201)
XLA Ops:
  0.7 13.4 %rows_kernel.1 = bf16[16,200,128]{2,1,0:T(8,128)(2,1)} custom-call(s32[1]{0:T(128)} %bitcast.me_ref, s32[1]{0:T(128)S(6)} %copy.11.count_ref, s32[1,512]{1,0:T(1,128)} %bitcast.7, s32[1,512]{1,0:T(1,128)} %bitcast.8, bf16[512,384]{1,0:T(8,128)(2,1)} %prof_hbm.1, bf16[512,512]{1,0:T(8,128)(2,1)} %rad_hbm.1, bf16[384,4096]{1,0:T(8,128)(2,1)} %w1_hbm.1, ...), custom_call_target="tpu_custom_call" | custom-call | tf_op jit(solution)/shard_map/rows_kernel/pallas_call | solution.py:199
  14.1 20.0 %all_to_all.5.got_ref = bf16[16,200,128]{2,1,0:T(8,128)(2,1)S(1)} all-to-all(bf16[16,200,128]{2,1,0:T(8,128)(2,1)} %rows_kernel.1), channel_id=1, replica_groups={{0,1,2,3,4,5,6,7,8,9,10,11,12,13,14,15},{16,17,18,19,20,21,22,23,24,25,..., dimensions={0} | all-to-all | bytes 1638400 | tf_op jit(solution)/shard_map/all_to_all | solution.py:234
  34.1 0.6 %blocks_kernel.1 = (f32[128,384]{1,0:T(8,128)S(1)}, bf16[128,384]{1,0:T(8,128)(2,1)S(1)}) custom-call(s32[1]{0:T(128)} %bitcast.me_ref, bf16[16,200,128]{2,1,0:T(8,128)(2,1)S(1)} %all_to_all.5.got_ref), custom_call_target="tpu_custom_call" | custom-call | tf_op jit(solution)/shard_map/blocks_kernel/pallas_call | solution.py:237
  34.7 2.6 %collective-permute-start = (bf16[128,384]{1,0:T(8,128)(2,1)S(1)}, bf16[128,384]{1,0:T(8,128)(2,1)S(1)}, u32[]{:S(2)}, u32[]{:S(2)}) collective-permute-start(bf16[128,384]{1,0:T(8,128)(2,1)S(1)} %get-tuple-element.8), channel_id=1, source_target_pairs={{0,16},{1,17},{2,18},{3,19},{4,20},{5,21},{6,22},{7,23},{8,24},{9,... | collective-permute-start | bytes 294920 | tf_op jit(solution)/shard_map/ppermute | solution.py:249
  37.4 4.5 %collective-permute-done = bf16[128,384]{1,0:T(8,128)(2,1)S(1)} collective-permute-done((bf16[128,384]{1,0:T(8,128)(2,1)S(1)}, bf16[128,384]{1,0:T(8,128)(2,1)S(1)}, u32[]{:S(2)}, u32[]{:S(2)}) %collective-permute-start) | collective-permute-done | bytes 98336 | tf_op jit(solution)/shard_map/ppermute | solution.py:249
  41.8 0.7 %convert_add_fusion = f32[128,384]{1,0:T(8,128)} fusion(f32[128,384]{1,0:T(8,128)S(1)} %get-tuple-element.7, bf16[128,384]{1,0:T(8,128)(2,1)S(1)} %collective-permute-done), kind=kLoop, calls=%fused_computation | loop fusion | flops 98304 | bytes 491520 | tf_op jit(solution)/shard_map/add | solution.py:249
Async XLA Ops:
  34.7 7.1 %collective-permute-start = (bf16[128,384]{1,0:T(8,128)(2,1)S(1)}, bf16[128,384]{1,0:T(8,128)(2,1)S(1)}, u32[]{:S(2)}, u32[]{:S(2)}) collective-permute-start(bf16[128,384]{1,0:T(8,128)(2,1)S(1)} %get-tuple-element.8), channel_id=1, source_target_pairs={{0,16},{1,17},{2,18},{3,19},{4,20},{5,21},{6,22},{7,23},{8,24},{9,... | collective-permute-start | bytes 294920 | tf_op jit(solution)/shard_map/ppermute | solution.py:249

commit v17 on v13

--- a/solution.py
+++ b/solution.py
@@ -101,6 +101,9 @@
         part = pl.ds(i * CHUNK, CHUNK)
         if i * CHUNK in starts:
             copies[2 + starts.index(i * CHUNK)].wait()
+        if i * CHUNK == hid * 5 // 8:
+            for copy in copies[2 + len(pieces) :]:
+                copy.wait()
         for m in blocks:
             u = jnp.dot(prof_ref[m, :], w1_ref[:, part], preferred_element_type=jnp.float32)
             u = u + 0.5 * b1_ref[:, part]
@@ -108,14 +111,16 @@
             hidden = u * p
             hidden_ref[m, part] = hidden.astype(jnp.bfloat16)
             factor_ref[m, part] = p + hidden * (2.0 - p)
-    for copy in copies[2 + len(pieces) :]:
-        copy.wait()
-    scale = 0.5 * cw_ref[...]
     for n, m in enumerate(blocks):
-        output = jnp.dot(hidden_ref[m, :], w2_ref[...], preferred_element_type=jnp.float32)
-        misfit = scale * (output + b2_ref[...] - rad_ref[m, :].astype(jnp.float32))
         alive = lax.broadcasted_iota(jnp.int32, (ROWS, 1), 0) + n * ROWS < count_ref[0]
-        rad_ref[m, :] = jnp.where(alive, misfit, 0.0).astype(jnp.bfloat16)
+        for lo in range(0, chan, CHUNK):
+            part = pl.ds(lo, CHUNK)
+            output = jnp.dot(
+                hidden_ref[m, :], w2_ref[:, part], preferred_element_type=jnp.float32
+            )
+            misfit = output + b2_ref[:, part] - rad_ref[m, part].astype(jnp.float32)
+            misfit = (0.5 * cw_ref[:, part]) * misfit
+            rad_ref[m, part] = jnp.where(alive, misfit, 0.0).astype(jnp.bfloat16)
     for i in range(hid // CHUNK):
         part = pl.ds(i * CHUNK, CHUNK)
         for m in blocks:
@@ -124,10 +129,12 @@
             )
             hidden_ref[m, part] = (back * factor_ref[m, part]).astype(jnp.bfloat16)
     for m in blocks:
-        grads = lax.dot_general(
-            hidden_ref[m, :], w1_ref[...], NT, preferred_element_type=jnp.float32
-        )
-        prof_ref[m, :] = grads.astype(jnp.bfloat16)
+        for lo in range(0, width, CHUNK):
+            part = pl.ds(lo, min(CHUNK, width - lo))
+            grads = lax.dot_general(
+                hidden_ref[m, :], w1_ref[part, :], NT, preferred_element_type=jnp.float32
+            )
+            prof_ref[m, part] = grads.astype(jnp.bfloat16)
     grads = prof_ref[...]
     wide = ROWS // pool
     sent = []

time: 42.4 us -> 42.5 us (level)
  no operation moved by 1% of the time
where the time goes in v17:
time: 42.5 us; the launch traced here: 42.3 us
  blocking collectives  20 us (47%)
  Pallas kernels  13.8 us (32%)
  waiting for transfers between devices  4.47 us (11%)
  starting transfers between devices  2.65 us (6%)
  other arithmetic  0.7 us (2%)
  between operations  0.67 us (2%)
    all_to_all x1, blocking collectives, per_device(): lax.all_to_all(bucket, 'tile', split_axis=0, concat_axis=0, axis_index_gr...  20 us
    pallas_call x1, Pallas kernels, per_device(): pl.pallas_call(functools.partial(rows_kernel, tiles, most), out_shape=jax...  13.2 us
    ppermute x1, waiting for transfers between devices, per_device(): return own + lax.ppermute(other, 'tile', pairs).astype(jnp.float32)  4.47 us
    ppermute x1, starting transfers between devices, per_device(): return own + lax.ppermute(other, 'tile', pairs).astype(jnp.float32)  2.65 us
  transfers between devices with their start and end apart: 1, of which 1 were waited for; matrix products, arithmetic and copies ran while one was open for 0% of the time, Pallas kernels for 0%

profile of v17, /device:TPU:0, one launch (start us, length us, event | category | flops | bytes accessed | tf_op | source)
XLA Modules:
  0.0 42.3 jit_solution(15145903036103037914)
XLA Ops:
  0.7 13.2 %rows_kernel.1 = bf16[16,200,128]{2,1,0:T(8,128)(2,1)} custom-call(s32[1]{0:T(128)} %bitcast.me_ref, s32[1]{0:T(128)S(6)} %copy.11.count_ref, s32[1,512]{1,0:T(1,128)} %bitcast.7, s32[1,512]{1,0:T(1,128)} %bitcast.8, bf16[512,384]{1,0:T(8,128)(2,1)} %prof_hbm.1, bf16[512,512]{1,0:T(8,128)(2,1)} %rad_hbm.1, bf16[384,4096]{1,0:T(8,128)(2,1)} %w1_hbm.1, ...), custom_call_target="tpu_custom_call" | custom-call | tf_op jit(solution)/shard_map/rows_kernel/pallas_call | solution.py:206
  13.8 20.0 %all_to_all.5.got_ref = bf16[16,200,128]{2,1,0:T(8,128)(2,1)S(1)} all-to-all(bf16[16,200,128]{2,1,0:T(8,128)(2,1)} %rows_kernel.1), channel_id=1, replica_groups={{0,1,2,3,4,5,6,7,8,9,10,11,12,13,14,15},{16,17,18,19,20,21,22,23,24,25,..., dimensions={0} | all-to-all | bytes 1638400 | tf_op jit(solution)/shard_map/all_to_all | solution.py:241
  33.9 0.6 %blocks_kernel.1 = (f32[128,384]{1,0:T(8,128)S(1)}, bf16[128,384]{1,0:T(8,128)(2,1)S(1)}) custom-call(s32[1]{0:T(128)} %bitcast.me_ref, bf16[16,200,128]{2,1,0:T(8,128)(2,1)S(1)} %all_to_all.5.got_ref), custom_call_target="tpu_custom_call" | custom-call | tf_op jit(solution)/shard_map/blocks_kernel/pallas_call | solution.py:244
  34.5 2.6 %collective-permute-start = (bf16[128,384]{1,0:T(8,128)(2,1)S(1)}, bf16[128,384]{1,0:T(8,128)(2,1)S(1)}, u32[]{:S(2)}, u32[]{:S(2)}) collective-permute-start(bf16[128,384]{1,0:T(8,128)(2,1)S(1)} %get-tuple-element.8), channel_id=1, source_target_pairs={{0,16},{1,17},{2,18},{3,19},{4,20},{5,21},{6,22},{7,23},{8,24},{9,... | collective-permute-start | bytes 294920 | tf_op jit(solution)/shard_map/ppermute | solution.py:256
  37.1 4.5 %collective-permute-done = bf16[128,384]{1,0:T(8,128)(2,1)S(1)} collective-permute-done((bf16[128,384]{1,0:T(8,128)(2,1)S(1)}, bf16[128,384]{1,0:T(8,128)(2,1)S(1)}, u32[]{:S(2)}, u32[]{:S(2)}) %collective-permute-start) | collective-permute-done | bytes 98336 | tf_op jit(solution)/shard_map/ppermute | solution.py:256
  41.6 0.7 %convert_add_fusion = f32[128,384]{1,0:T(8,128)} fusion(f32[128,384]{1,0:T(8,128)S(1)} %get-tuple-element.7, bf16[128,384]{1,0:T(8,128)(2,1)S(1)} %collective-permute-done), kind=kLoop, calls=%fused_computation | loop fusion | flops 98304 | bytes 491520 | tf_op jit(solution)/shard_map/add | solution.py:256
Async XLA Ops:
  34.5 7.1 %collective-permute-start = (bf16[128,384]{1,0:T(8,128)(2,1)S(1)}, bf16[128,384]{1,0:T(8,128)(2,1)S(1)}, u32[]{:S(2)}, u32[]{:S(2)}) collective-permute-start(bf16[128,384]{1,0:T(8,128)(2,1)S(1)} %get-tuple-element.8), channel_id=1, source_target_pairs={{0,16},{1,17},{2,18},{3,19},{4,20},{5,21},{6,22},{7,23},{8,24},{9,... | collective-permute-start | bytes 294920 | tf_op jit(solution)/shard_map/ppermute | solution.py:256

commit v18 on v13

--- a/solution.py
+++ b/solution.py
@@ -110,12 +110,13 @@
             factor_ref[m, part] = p + hidden * (2.0 - p)
     for copy in copies[2 + len(pieces) :]:
         copy.wait()
-    scale = 0.5 * cw_ref[...]
-    for n, m in enumerate(blocks):
-        output = jnp.dot(hidden_ref[m, :], w2_ref[...], preferred_element_type=jnp.float32)
-        misfit = scale * (output + b2_ref[...] - rad_ref[m, :].astype(jnp.float32))
-        alive = lax.broadcasted_iota(jnp.int32, (ROWS, 1), 0) + n * ROWS < count_ref[0]
-        rad_ref[m, :] = jnp.where(alive, misfit, 0.0).astype(jnp.bfloat16)
+    alive = lax.broadcasted_iota(jnp.int32, (rows, 1), 0) < count_ref[0]
+    for lo in range(0, chan, CHUNK):
+        part = pl.ds(lo, CHUNK)
+        output = jnp.dot(hidden_ref[...], w2_ref[:, part], preferred_element_type=jnp.float32)
+        misfit = output + b2_ref[:, part] - rad_ref[:, part].astype(jnp.float32)
+        misfit = (0.5 * cw_ref[:, part]) * misfit
+        rad_ref[:, part] = jnp.where(alive, misfit, 0.0).astype(jnp.bfloat16)
     for i in range(hid // CHUNK):
         part = pl.ds(i * CHUNK, CHUNK)
         for m in blocks:
@@ -123,11 +124,12 @@
                 rad_ref[m, :], w2_ref[part, :], NT, preferred_element_type=jnp.float32
             )
             hidden_ref[m, part] = (back * factor_ref[m, part]).astype(jnp.bfloat16)
-    for m in blocks:
+    for lo in range(0, width, CHUNK):
+        part = pl.ds(lo, min(CHUNK, width - lo))
         grads = lax.dot_general(
-            hidden_ref[m, :], w1_ref[...], NT, preferred_element_type=jnp.float32
+            hidden_ref[...], w1_ref[part, :], NT, preferred_element_type=jnp.float32
         )
-        prof_ref[m, :] = grads.astype(jnp.bfloat16)
+        prof_ref[:, part] = grads.astype(jnp.bfloat16)
     grads = prof_ref[...]
     wide = ROWS // pool
     sent = []

time: 42.4 us -> 42.3 us (level)
  no operation moved by 1% of the time
where the time goes in v18:
time: 42.3 us; the launch traced here: 42.1 us
  blocking collectives  20 us (47%)
  Pallas kernels  13.6 us (32%)
  waiting for transfers between devices  4.47 us (11%)
  starting transfers between devices  2.64 us (6%)
  other arithmetic  0.7 us (2%)
  between operations  0.67 us (2%)
    all_to_all x1, blocking collectives, per_device(): lax.all_to_all(bucket, 'tile', split_axis=0, concat_axis=0, axis_index_gr...  20 us
    pallas_call x1, Pallas kernels, per_device(): pl.pallas_call(functools.partial(rows_kernel, tiles, most), out_shape=jax...  13 us
    ppermute x1, waiting for transfers between devices, per_device(): return own + lax.ppermute(other, 'tile', pairs).astype(jnp.float32)  4.47 us
    ppermute x1, starting transfers between devices, per_device(): return own + lax.ppermute(other, 'tile', pairs).astype(jnp.float32)  2.64 us
  transfers between devices with their start and end apart: 1, of which 1 were waited for; matrix products, arithmetic and copies ran while one was open for 0% of the time, Pallas kernels for 0%

profile of v18, /device:TPU:0, one launch (start us, length us, event | category | flops | bytes accessed | tf_op | source)
XLA Modules:
  0.0 42.1 jit_solution(17721803699867420976)
XLA Ops:
  0.7 13.0 %rows_kernel.1 = bf16[16,200,128]{2,1,0:T(8,128)(2,1)} custom-call(s32[1]{0:T(128)} %bitcast.me_ref, s32[1]{0:T(128)S(6)} %copy.11.count_ref, s32[1,512]{1,0:T(1,128)} %bitcast.7, s32[1,512]{1,0:T(1,128)} %bitcast.8, bf16[512,384]{1,0:T(8,128)(2,1)} %prof_hbm.1, bf16[512,512]{1,0:T(8,128)(2,1)} %rad_hbm.1, bf16[384,4096]{1,0:T(8,128)(2,1)} %w1_hbm.1, ...), custom_call_target="tpu_custom_call" | custom-call | tf_op jit(solution)/shard_map/rows_kernel/pallas_call | solution.py:201
  13.6 20.0 %all_to_all.5.got_ref = bf16[16,200,128]{2,1,0:T(8,128)(2,1)S(1)} all-to-all(bf16[16,200,128]{2,1,0:T(8,128)(2,1)} %rows_kernel.1), channel_id=1, replica_groups={{0,1,2,3,4,5,6,7,8,9,10,11,12,13,14,15},{16,17,18,19,20,21,22,23,24,25,..., dimensions={0} | all-to-all | bytes 1638400 | tf_op jit(solution)/shard_map/all_to_all | solution.py:236
  33.7 0.6 %blocks_kernel.1 = (f32[128,384]{1,0:T(8,128)S(1)}, bf16[128,384]{1,0:T(8,128)(2,1)S(1)}) custom-call(s32[1]{0:T(128)} %bitcast.me_ref, bf16[16,200,128]{2,1,0:T(8,128)(2,1)S(1)} %all_to_all.5.got_ref), custom_call_target="tpu_custom_call" | custom-call | tf_op jit(solution)/shard_map/blocks_kernel/pallas_call | solution.py:239
  34.3 2.6 %collective-permute-start = (bf16[128,384]{1,0:T(8,128)(2,1)S(1)}, bf16[128,384]{1,0:T(8,128)(2,1)S(1)}, u32[]{:S(2)}, u32[]{:S(2)}) collective-permute-start(bf16[128,384]{1,0:T(8,128)(2,1)S(1)} %get-tuple-element.8), channel_id=1, source_target_pairs={{0,16},{1,17},{2,18},{3,19},{4,20},{5,21},{6,22},{7,23},{8,24},{9,... | collective-permute-start | bytes 294920 | tf_op jit(solution)/shard_map/ppermute | solution.py:251
  36.9 4.5 %collective-permute-done = bf16[128,384]{1,0:T(8,128)(2,1)S(1)} collective-permute-done((bf16[128,384]{1,0:T(8,128)(2,1)S(1)}, bf16[128,384]{1,0:T(8,128)(2,1)S(1)}, u32[]{:S(2)}, u32[]{:S(2)}) %collective-permute-start) | collective-permute-done | bytes 98336 | tf_op jit(solution)/shard_map/ppermute | solution.py:251
  41.4 0.7 %convert_add_fusion = f32[128,384]{1,0:T(8,128)} fusion(f32[128,384]{1,0:T(8,128)S(1)} %get-tuple-element.7, bf16[128,384]{1,0:T(8,128)(2,1)S(1)} %collective-permute-done), kind=kLoop, calls=%fused_computation | loop fusion | flops 98304 | bytes 491520 | tf_op jit(solution)/shard_map/add | solution.py:251
Async XLA Ops:
  34.3 7.1 %collective-permute-start = (bf16[128,384]{1,0:T(8,128)(2,1)S(1)}, bf16[128,384]{1,0:T(8,128)(2,1)S(1)}, u32[]{:S(2)}, u32[]{:S(2)}) collective-permute-start(bf16[128,384]{1,0:T(8,128)(2,1)S(1)} %get-tuple-element.8), channel_id=1, source_target_pairs={{0,16},{1,17},{2,18},{3,19},{4,20},{5,21},{6,22},{7,23},{8,24},{9,... | collective-permute-start | bytes 294920 | tf_op jit(solution)/shard_map/ppermute | solution.py:251

commit v19 on v18

--- a/solution.py
+++ b/solution.py
@@ -24,9 +24,9 @@
     tiles,
     most,
     me_ref,
-    count_ref,
-    owner_ref,
-    column_ref,
+    count_hbm,
+    owner_hbm,
+    column_hbm,
     prof_hbm,
     rad_hbm,
     w1_hbm,
@@ -35,6 +35,9 @@
     b2_hbm,
     cw_hbm,
     out_hbm,
+    count_ref,
+    owner_ref,
+    column_ref,
     prof_ref,
     rad_ref,
     w1_ref,
@@ -45,6 +48,7 @@
     hidden_ref,
     factor_ref,
     out_ref,
+    early_sems,
     sems,
     out_sems,
 ):
@@ -61,8 +65,16 @@
     copies = [
         pltpu.make_async_copy(src, dst, sems.at[i]) for i, (src, dst) in enumerate(pairs)
     ]
-    for copy in copies:
+    early = [
+        pltpu.make_async_copy(src, dst, early_sems.at[i])
+        for i, (src, dst) in enumerate(
+            ((owner_hbm, owner_ref), (column_hbm, column_ref), (count_hbm, count_ref))
+        )
+    ]
+    for copy in early + copies:
         copy.start()
+    for copy in early:
+        copy.wait()
 
     inner = out_ref.shape[0]
     live = lax.broadcasted_iota(jnp.int32, (1, rows), 1) < count_ref[0]
@@ -201,9 +213,12 @@
     bucket = pl.pallas_call(
         functools.partial(rows_kernel, tiles, most),
         out_shape=jax.ShapeDtypeStruct((inner, high, LANES), jnp.bfloat16),
-        in_specs=[smem, smem, vmem, vmem] + [anywhere] * 7,
+        in_specs=[smem] + [anywhere] * 10,
         out_specs=anywhere,
         scratch_shapes=[
+            pltpu.SMEM((1,), jnp.int32),
+            pltpu.VMEM((1, rows), jnp.int32),
+            pltpu.VMEM((1, rows), jnp.int32),
             pltpu.VMEM((rows, width), jnp.bfloat16),
             pltpu.VMEM((rows, chan), jnp.bfloat16),
             pltpu.VMEM((width, hid), jnp.bfloat16),
@@ -214,6 +229,7 @@
             pltpu.VMEM((rows, hid), jnp.bfloat16),
             pltpu.VMEM((rows, hid), jnp.float32),
             pltpu.VMEM((inner, high, LANES), jnp.bfloat16),
+            pltpu.SemaphoreType.DMA((3,)),
             pltpu.SemaphoreType.DMA((8,)),
             pltpu.SemaphoreType.DMA((inner * pool // ROWS,)),
         ],

time: 42.3 us -> 44.2 us (1.045)
  Pallas kernels: 13.6 us -> 15.5 us
    pallas_call x1, Pallas kernels: 13 us -> 14.9 us  [per_device(): pl.pallas_call(functools.partial(rows_kernel, tiles, most), out_shape=jax...]
where the time goes in v19:
time: 44.2 us; the launch traced here: 44 us
  blocking collectives  20 us (45%)
  Pallas kernels  15.5 us (35%)
  waiting for transfers between devices  4.44 us (10%)
  starting transfers between devices  2.67 us (6%)
  other arithmetic  0.7 us (2%)
  between operations  0.67 us (2%)
    all_to_all x1, blocking collectives, per_device(): lax.all_to_all(bucket, 'tile', split_axis=0, concat_axis=0, axis_index_gr...  20 us
    pallas_call x1, Pallas kernels, per_device(): pl.pallas_call(functools.partial(rows_kernel, tiles, most), out_shape=jax...  14.9 us
    ppermute x1, waiting for transfers between devices, per_device(): return own + lax.ppermute(other, 'tile', pairs).astype(jnp.float32)  4.44 us
    ppermute x1, starting transfers between devices, per_device(): return own + lax.ppermute(other, 'tile', pairs).astype(jnp.float32)  2.67 us
  transfers between devices with their start and end apart: 1, of which 1 were waited for; matrix products, arithmetic and copies ran while one was open for 0% of the time, Pallas kernels for 0%

profile of v19, /device:TPU:0, one launch (start us, length us, event | category | flops | bytes accessed | tf_op | source)
XLA Modules:
  0.0 44.0 jit_solution(1493415924569965846)
XLA Ops:
  0.7 14.9 %rows_kernel.1 = bf16[16,200,128]{2,1,0:T(8,128)(2,1)} custom-call(s32[1]{0:T(128)} %bitcast.me_ref, s32[1]{0:T(128)S(6)} %copy.11.count_hbm, s32[1,512]{1,0:T(1,128)} %bitcast.7, s32[1,512]{1,0:T(1,128)} %bitcast.8, bf16[512,384]{1,0:T(8,128)(2,1)} %prof_hbm.1, bf16[512,512]{1,0:T(8,128)(2,1)} %rad_hbm.1, bf16[384,4096]{1,0:T(8,128)(2,1)} %w1_hbm.1, ...), custom_call_target="tpu_custom_call" | custom-call | tf_op jit(solution)/shard_map/rows_kernel/pallas_call | solution.py:213
  15.5 20.0 %all_to_all.5.got_ref = bf16[16,200,128]{2,1,0:T(8,128)(2,1)S(1)} all-to-all(bf16[16,200,128]{2,1,0:T(8,128)(2,1)} %rows_kernel.1), channel_id=1, replica_groups={{0,1,2,3,4,5,6,7,8,9,10,11,12,13,14,15},{16,17,18,19,20,21,22,23,24,25,..., dimensions={0} | all-to-all | bytes 1638400 | tf_op jit(solution)/shard_map/all_to_all | solution.py:252
  35.5 0.6 %blocks_kernel.1 = (f32[128,384]{1,0:T(8,128)S(1)}, bf16[128,384]{1,0:T(8,128)(2,1)S(1)}) custom-call(s32[1]{0:T(128)} %bitcast.me_ref, bf16[16,200,128]{2,1,0:T(8,128)(2,1)S(1)} %all_to_all.5.got_ref), custom_call_target="tpu_custom_call" | custom-call | tf_op jit(solution)/shard_map/blocks_kernel/pallas_call | solution.py:255
  36.2 2.7 %collective-permute-start = (bf16[128,384]{1,0:T(8,128)(2,1)S(1)}, bf16[128,384]{1,0:T(8,128)(2,1)S(1)}, u32[]{:S(2)}, u32[]{:S(2)}) collective-permute-start(bf16[128,384]{1,0:T(8,128)(2,1)S(1)} %get-tuple-element.8), channel_id=1, source_target_pairs={{0,16},{1,17},{2,18},{3,19},{4,20},{5,21},{6,22},{7,23},{8,24},{9,... | collective-permute-start | bytes 294920 | tf_op jit(solution)/shard_map/ppermute | solution.py:267
  38.8 4.4 %collective-permute-done = bf16[128,384]{1,0:T(8,128)(2,1)S(1)} collective-permute-done((bf16[128,384]{1,0:T(8,128)(2,1)S(1)}, bf16[128,384]{1,0:T(8,128)(2,1)S(1)}, u32[]{:S(2)}, u32[]{:S(2)}) %collective-permute-start) | collective-permute-done | bytes 98336 | tf_op jit(solution)/shard_map/ppermute | solution.py:267
  43.3 0.7 %convert_add_fusion = f32[128,384]{1,0:T(8,128)} fusion(f32[128,384]{1,0:T(8,128)S(1)} %get-tuple-element.7, bf16[128,384]{1,0:T(8,128)(2,1)S(1)} %collective-permute-done), kind=kLoop, calls=%fused_computation | loop fusion | flops 98304 | bytes 491520 | tf_op jit(solution)/shard_map/add | solution.py:267
Async XLA Ops:
  36.2 7.1 %collective-permute-start = (bf16[128,384]{1,0:T(8,128)(2,1)S(1)}, bf16[128,384]{1,0:T(8,128)(2,1)S(1)}, u32[]{:S(2)}, u32[]{:S(2)}) collective-permute-start(bf16[128,384]{1,0:T(8,128)(2,1)S(1)} %get-tuple-element.8), channel_id=1, source_target_pairs={{0,16},{1,17},{2,18},{3,19},{4,20},{5,21},{6,22},{7,23},{8,24},{9,... | collective-permute-start | bytes 294920 | tf_op jit(solution)/shard_map/ppermute | solution.py:267

commit v20 on v13

--- a/solution.py
+++ b/solution.py
@@ -65,7 +65,7 @@
         copy.start()
 
     inner = out_ref.shape[0]
-    live = lax.broadcasted_iota(jnp.int32, (1, rows), 1) < count_ref[0]
+    live = lax.broadcasted_iota(jnp.int32, (1, rows), 1) < count_ref[...]
     owner = jnp.where(live, owner_ref[...], -1)
     mine = lax.broadcasted_iota(jnp.int32, (tiles, rows), 0) == owner
     one_hot = mine.astype(jnp.float32)
@@ -79,7 +79,6 @@
     place = owner & (inner - 1)
     order = lax.shift_right_arithmetic(owner, inner.bit_length() - 1) * most + rank
     slot = jnp.where(live, place * pool + order, -1)
-    placing = as_bf16(lax.broadcasted_iota(jnp.int32, (inner * pool, rows), 0) == slot)
     lane = order + lax.rem(me_ref[0], LANES // pool) * pool
     lane_hot = as_bf16(lax.broadcasted_iota(jnp.int32, (LANES, rows), 0) == lane)
     here = live & (lax.broadcasted_iota(jnp.int32, (inner, rows), 0) == place)
@@ -114,7 +113,7 @@
     for n, m in enumerate(blocks):
         output = jnp.dot(hidden_ref[m, :], w2_ref[...], preferred_element_type=jnp.float32)
         misfit = scale * (output + b2_ref[...] - rad_ref[m, :].astype(jnp.float32))
-        alive = lax.broadcasted_iota(jnp.int32, (ROWS, 1), 0) + n * ROWS < count_ref[0]
+        alive = lax.broadcasted_iota(jnp.int32, (ROWS, 1), 0) + n * ROWS < count_ref[...]
         rad_ref[m, :] = jnp.where(alive, misfit, 0.0).astype(jnp.bfloat16)
     for i in range(hid // CHUNK):
         part = pl.ds(i * CHUNK, CHUNK)
@@ -132,9 +131,10 @@
     wide = ROWS // pool
     sent = []
     for n in range(inner // wide):
-        placed = jnp.dot(
-            placing[n * ROWS : (n + 1) * ROWS], grads, preferred_element_type=jnp.float32
-        ).astype(jnp.bfloat16)
+        placing = as_bf16(
+            lax.broadcasted_iota(jnp.int32, (ROWS, rows), 0) + n * ROWS == slot
+        )
+        placed = jnp.dot(placing, grads, preferred_element_type=jnp.float32).astype(jnp.bfloat16)
         some = pl.ds(n * wide, wide)
         for k in range(parts):
             out_ref[some, k * pool : (k + 1) * pool, :] = placed[
@@ -199,7 +199,7 @@
     bucket = pl.pallas_call(
         functools.partial(rows_kernel, tiles, most),
         out_shape=jax.ShapeDtypeStruct((inner, high, LANES), jnp.bfloat16),
-        in_specs=[smem, smem, vmem, vmem] + [anywhere] * 7,
+        in_specs=[smem, vmem, vmem, vmem] + [anywhere] * 7,
         out_specs=anywhere,
         scratch_shapes=[
             pltpu.VMEM((rows, width), jnp.bfloat16),
@@ -219,7 +219,7 @@
         name="rows_kernel",
     )(
         me,
-        counts,
+        counts.reshape(1, 1),
         owner.reshape(1, rows),
         column.reshape(1, rows),
         profiles,

time: 42.4 us -> 42.3 us (level)
  no operation moved by 1% of the time
where the time goes in v20:
time: 42.3 us; the launch traced here: 42.1 us
  blocking collectives  20 us (47%)
  Pallas kernels  13.6 us (32%)
  waiting for transfers between devices  4.44 us (10%)
  starting transfers between devices  2.67 us (6%)
  other arithmetic  0.7 us (2%)
  between operations  0.67 us (2%)
    all_to_all x1, blocking collectives, per_device(): lax.all_to_all(bucket, 'tile', split_axis=0, concat_axis=0, axis_index_gr...  20 us
    pallas_call x1, Pallas kernels, per_device(): pl.pallas_call(functools.partial(rows_kernel, tiles, most), out_shape=jax...  13 us
    ppermute x1, waiting for transfers between devices, per_device(): return own + lax.ppermute(other, 'tile', pairs).astype(jnp.float32)  4.44 us
    ppermute x1, starting transfers between devices, per_device(): return own + lax.ppermute(other, 'tile', pairs).astype(jnp.float32)  2.67 us
  transfers between devices with their start and end apart: 1, of which 1 were waited for; matrix products, arithmetic and copies ran while one was open for 0% of the time, Pallas kernels for 0%

profile of v20, /device:TPU:0, one launch (start us, length us, event | category | flops | bytes accessed | tf_op | source)
XLA Modules:
  0.0 42.1 jit_solution(11095541588451498710)
XLA Ops:
  0.7 13.0 %rows_kernel.1 = bf16[16,200,128]{2,1,0:T(8,128)(2,1)} custom-call(s32[1]{0:T(128)} %bitcast.me_ref, s32[1,1]{1,0:T(1,128)} %bitcast.7.count_ref, s32[1,512]{1,0:T(1,128)} %bitcast.9, s32[1,512]{1,0:T(1,128)} %bitcast.10, bf16[512,384]{1,0:T(8,128)(2,1)} %prof_hbm.1, bf16[512,512]{1,0:T(8,128)(2,1)} %rad_hbm.1, bf16[384,4096]{1,0:T(8,128)(2,1)} %w1_hbm.1, ...), custom_call_target="tpu_custom_call" | custom-call | tf_op jit(solution)/shard_map/rows_kernel/pallas_call | solution.py:199
  13.6 20.0 %all_to_all.5.got_ref = bf16[16,200,128]{2,1,0:T(8,128)(2,1)S(1)} all-to-all(bf16[16,200,128]{2,1,0:T(8,128)(2,1)} %rows_kernel.1), channel_id=1, replica_groups={{0,1,2,3,4,5,6,7,8,9,10,11,12,13,14,15},{16,17,18,19,20,21,22,23,24,25,..., dimensions={0} | all-to-all | bytes 1638400 | tf_op jit(solution)/shard_map/all_to_all | solution.py:234
  33.7 0.6 %blocks_kernel.1 = (f32[128,384]{1,0:T(8,128)S(1)}, bf16[128,384]{1,0:T(8,128)(2,1)S(1)}) custom-call(s32[1]{0:T(128)} %bitcast.me_ref, bf16[16,200,128]{2,1,0:T(8,128)(2,1)S(1)} %all_to_all.5.got_ref), custom_call_target="tpu_custom_call" | custom-call | tf_op jit(solution)/shard_map/blocks_kernel/pallas_call | solution.py:237
  34.3 2.7 %collective-permute-start = (bf16[128,384]{1,0:T(8,128)(2,1)S(1)}, bf16[128,384]{1,0:T(8,128)(2,1)S(1)}, u32[]{:S(2)}, u32[]{:S(2)}) collective-permute-start(bf16[128,384]{1,0:T(8,128)(2,1)S(1)} %get-tuple-element.8), channel_id=1, source_target_pairs={{0,16},{1,17},{2,18},{3,19},{4,20},{5,21},{6,22},{7,23},{8,24},{9,... | collective-permute-start | bytes 294920 | tf_op jit(solution)/shard_map/ppermute | solution.py:249
  37.0 4.4 %collective-permute-done = bf16[128,384]{1,0:T(8,128)(2,1)S(1)} collective-permute-done((bf16[128,384]{1,0:T(8,128)(2,1)S(1)}, bf16[128,384]{1,0:T(8,128)(2,1)S(1)}, u32[]{:S(2)}, u32[]{:S(2)}) %collective-permute-start) | collective-permute-done | bytes 98336 | tf_op jit(solution)/shard_map/ppermute | solution.py:249
  41.4 0.7 %convert_add_fusion = f32[128,384]{1,0:T(8,128)} fusion(f32[128,384]{1,0:T(8,128)S(1)} %get-tuple-element.7, bf16[128,384]{1,0:T(8,128)(2,1)S(1)} %collective-permute-done), kind=kLoop, calls=%fused_computation | loop fusion | flops 98304 | bytes 491520 | tf_op jit(solution)/shard_map/add | solution.py:249
Async XLA Ops:
  34.3 7.1 %collective-permute-start = (bf16[128,384]{1,0:T(8,128)(2,1)S(1)}, bf16[128,384]{1,0:T(8,128)(2,1)S(1)}, u32[]{:S(2)}, u32[]{:S(2)}) collective-permute-start(bf16[128,384]{1,0:T(8,128)(2,1)S(1)} %get-tuple-element.8), channel_id=1, source_target_pairs={{0,16},{1,17},{2,18},{3,19},{4,20},{5,21},{6,22},{7,23},{8,24},{9,... | collective-permute-start | bytes 294920 | tf_op jit(solution)/shard_map/ppermute | solution.py:249

commit v21 on v13

--- a/solution.py
+++ b/solution.py
@@ -11,7 +11,6 @@
 CHUNK = 256
 LANES = 128
 LABEL_ROWS = 8
-OUTER = 2
 ROWS = 256
 NT = (((1,), (1,)), ((), ()))
 
@@ -34,20 +33,24 @@
     w2_hbm,
     b2_hbm,
     cw_hbm,
-    out_hbm,
-    prof_ref,
-    rad_ref,
-    w1_ref,
-    b1_ref,
-    w2_ref,
-    b2_ref,
-    cw_ref,
-    hidden_ref,
-    factor_ref,
-    out_ref,
-    sems,
-    out_sems,
+    *refs,
 ):
+    (
+        prof_ref,
+        rad_ref,
+        w1_ref,
+        b1_ref,
+        w2_ref,
+        b2_ref,
+        cw_ref,
+        hidden_ref,
+        factor_ref,
+        far_ref,
+        near_ref,
+        sems,
+        out_sems,
+    ) = refs[-13:]
+    far_hbm, near_hbms = refs[0], refs[1:-13]
     rows, width = prof_ref.shape
     hid = w1_ref.shape[1]
     chan = rad_ref.shape[1]
@@ -64,7 +67,8 @@
     for copy in copies:
         copy.start()
 
-    inner = out_ref.shape[0]
+    inner, chips = far_ref.shape[0], near_ref.shape[0]
+    me = me_ref[0]
     live = lax.broadcasted_iota(jnp.int32, (1, rows), 1) < count_ref[0]
     owner = jnp.where(live, owner_ref[...], -1)
     mine = lax.broadcasted_iota(jnp.int32, (tiles, rows), 0) == owner
@@ -75,22 +79,35 @@
     )
     running = jnp.dot(one_hot.astype(jnp.bfloat16), upper, preferred_element_type=jnp.float32)
     rank = jnp.sum(running * one_hot, axis=0, keepdims=True).astype(jnp.int32) - 1
-    pool = tiles // inner * most
+    pool = 2 * most
     place = owner & (inner - 1)
-    order = lax.shift_right_arithmetic(owner, inner.bit_length() - 1) * most + rank
-    slot = jnp.where(live, place * pool + order, -1)
-    placing = as_bf16(lax.broadcasted_iota(jnp.int32, (inner * pool, rows), 0) == slot)
-    lane = order + lax.rem(me_ref[0], LANES // pool) * pool
+    near = (owner & inner) == (me & inner)
+    chip = lax.shift_right_arithmetic(place, 1) ^ (
+        lax.shift_right_arithmetic(me, 1) & (chips - 1)
+    )
+    order = (owner & 1) * most + rank
+    slot = jnp.where(near, inner * most + chip * pool + order, place * most + rank)
+    slot = jnp.where(live, slot, -1)
+    slots = inner * most + chips * pool
+    placing = as_bf16(lax.broadcasted_iota(jnp.int32, (slots, rows), 0) == slot)
+    lane = jnp.where(
+        near,
+        (chip & (LANES // pool - 1)) * pool + order,
+        (me & (LANES // most - 1)) * most + rank,
+    )
     lane_hot = as_bf16(lax.broadcasted_iota(jnp.int32, (LANES, rows), 0) == lane)
-    here = live & (lax.broadcasted_iota(jnp.int32, (inner, rows), 0) == place)
+    block = jnp.where(live, jnp.where(near, inner + chip, place), -1)
+    here = lax.broadcasted_iota(jnp.int32, (inner + chips, rows), 0) == block
     marked = jnp.where(here, (column_ref[...] + 1).astype(jnp.float32), 0.0)
     labels = lax.dot_general(
         marked.astype(jnp.bfloat16), lane_hot, NT, preferred_element_type=jnp.float32
     )
-
     parts = width // LANES
-    out_ref[:, parts * pool :, :] = jnp.broadcast_to(
-        labels.reshape(inner, 1, LANES), (inner, LABEL_ROWS, LANES)
+    far_ref[:, parts * most :, :] = jnp.broadcast_to(
+        labels[:inner].reshape(inner, 1, LANES), (inner, LABEL_ROWS, LANES)
+    ).astype(jnp.bfloat16)
+    near_ref[:, parts * pool :, :] = jnp.broadcast_to(
+        labels[inner:].reshape(chips, 1, LANES), (chips, LABEL_ROWS, LANES)
     ).astype(jnp.bfloat16)
 
     copies[0].wait()
@@ -129,44 +146,67 @@
         )
         prof_ref[m, :] = grads.astype(jnp.bfloat16)
     grads = prof_ref[...]
-    wide = ROWS // pool
     sent = []
-    for n in range(inner // wide):
+    for n in range(slots // ROWS):
         placed = jnp.dot(
             placing[n * ROWS : (n + 1) * ROWS], grads, preferred_element_type=jnp.float32
         ).astype(jnp.bfloat16)
-        some = pl.ds(n * wide, wide)
+        far = n * ROWS < inner * most
+        high, target_ref = (most, far_ref) if far else (pool, near_ref)
+        wide = ROWS // high
+        first = n * wide if far else (n * ROWS - inner * most) // high
         for k in range(parts):
-            out_ref[some, k * pool : (k + 1) * pool, :] = placed[
+            target_ref[first : first + wide, k * high : (k + 1) * high, :] = placed[
                 :, k * LANES : (k + 1) * LANES
-            ].reshape(wide, pool, LANES)
-        sent.append(pltpu.make_async_copy(out_ref.at[some], out_hbm.at[some], out_sems.at[n]))
-        sent[-1].start()
+            ].reshape(wide, high, LANES)
+        some = pl.ds(first, wide)
+        if far:
+            moves = [(far_ref.at[some], far_hbm.at[some])]
+        else:
+            moves = [(near_ref.at[j], near_hbms[j]) for j in range(first, first + wide)]
+        for src, dst in moves:
+            sent.append(pltpu.make_async_copy(src, dst, out_sems.at[len(sent)]))
+            sent[-1].start()
     for copy in sent:
         copy.wait()
 
 
-def blocks_kernel(tiles, most, me_ref, got_ref, own_ref, other_ref):
+def far_kernel(most, got_ref, out_ref):
     inner = got_ref.shape[0]
-    outer = tiles // inner
-    pool = outer * most
-    group = LANES // pool
-    parts = own_ref.shape[1] // LANES
-    marks = got_ref[:, parts * pool :, :].astype(jnp.float32)[:, 0, :]
-    index = lax.broadcasted_iota(jnp.int32, (outer * COL_DEV, LANES), 0)
-    lane = lax.broadcasted_iota(jnp.int32, (1, LANES), 1) & (pool - 1)
-    turn = lax.shift_right_arithmetic(lane, most.bit_length() - 1) ^ (
-        lax.shift_right_arithmetic(me_ref[0], inner.bit_length() - 1)
-    )
+    group = LANES // most
+    parts = out_ref.shape[1] // LANES
+    marks = got_ref[:, parts * most :, :].astype(jnp.float32)[:, 0, :]
+    index = lax.broadcasted_iota(jnp.int32, (COL_DEV, LANES), 0) + 1
     chosen = []
     for g in range(inner // group):
         label = jnp.sum(marks[g * group : (g + 1) * group], axis=0, keepdims=True)
-        label = label.astype(jnp.int32)
+        chosen.append(as_bf16(index == label.astype(jnp.int32)))
+    chosen = jnp.concatenate(chosen, axis=1)
+    for k in range(parts):
+        block = got_ref[:, k * most : (k + 1) * most, :].reshape(inner * most, LANES)
+        total = jnp.dot(chosen, block, preferred_element_type=jnp.float32)
+        out_ref[:, k * LANES : (k + 1) * LANES] = total.astype(jnp.bfloat16)
+
+
+def near_kernel(most, me_ref, *refs):
+    got, (own_ref, other_ref) = refs[:-2], refs[-2:]
+    pool = 2 * most
+    group = LANES // pool
+    parts = own_ref.shape[1] // LANES
+    index = lax.broadcasted_iota(jnp.int32, (2 * COL_DEV, LANES), 0)
+    lane = lax.broadcasted_iota(jnp.int32, (1, LANES), 1) & (pool - 1)
+    turn = lax.shift_right_arithmetic(lane, most.bit_length() - 1) ^ (me_ref[0] & 1)
+    chosen = []
+    for g in range(len(got) // group):
+        label = sum(
+            ref[parts * pool :, :].astype(jnp.float32)[:1]
+            for ref in got[g * group : (g + 1) * group]
+        ).astype(jnp.int32)
         code = jnp.where(label > 0, turn * COL_DEV + label - 1, -1)
         chosen.append(as_bf16(index == code))
     chosen = jnp.concatenate(chosen, axis=1)
     for k in range(parts):
-        block = got_ref[:, k * pool : (k + 1) * pool, :].reshape(inner * pool, LANES)
+        block = jnp.concatenate([ref[k * pool : (k + 1) * pool, :] for ref in got], axis=0)
         total = jnp.dot(chosen, block, preferred_element_type=jnp.float32)
         own_ref[:, k * LANES : (k + 1) * LANES] = total[:COL_DEV]
         other_ref[:, k * LANES : (k + 1) * LANES] = total[COL_DEV:].astype(jnp.bfloat16)
@@ -189,18 +229,20 @@
     hid = inner_weight.shape[1]
     chan = radiances.shape[1]
     most = max(2, 2 * rows // tiles)
-    inner = tiles // OUTER
-    pool = OUTER * most
-    high = width // LANES * pool + LABEL_ROWS
+    inner = tiles // 2
+    chips = inner // 2
+    far_high = width // LANES * most + LABEL_ROWS
+    near_high = width // LANES * 2 * most + LABEL_ROWS
     me = lax.axis_index("tile").astype(jnp.int32).reshape(1)
     vmem = pl.BlockSpec(memory_space=pltpu.VMEM)
     smem = pl.BlockSpec(memory_space=pltpu.SMEM)
     anywhere = pl.BlockSpec(memory_space=pl.ANY)
-    bucket = pl.pallas_call(
+    far, *near = pl.pallas_call(
         functools.partial(rows_kernel, tiles, most),
-        out_shape=jax.ShapeDtypeStruct((inner, high, LANES), jnp.bfloat16),
+        out_shape=[jax.ShapeDtypeStruct((inner, far_high, LANES), jnp.bfloat16)]
+        + [jax.ShapeDtypeStruct((near_high, LANES), jnp.bfloat16)] * chips,
         in_specs=[smem, smem, vmem, vmem] + [anywhere] * 7,
-        out_specs=anywhere,
+        out_specs=[anywhere] * (1 + chips),
         scratch_shapes=[
             pltpu.VMEM((rows, width), jnp.bfloat16),
             pltpu.VMEM((rows, chan), jnp.bfloat16),
@@ -211,9 +253,10 @@
             pltpu.VMEM((1, chan), jnp.float32),
             pltpu.VMEM((rows, hid), jnp.bfloat16),
             pltpu.VMEM((rows, hid), jnp.float32),
-            pltpu.VMEM((inner, high, LANES), jnp.bfloat16),
+            pltpu.VMEM((inner, far_high, LANES), jnp.bfloat16),
+            pltpu.VMEM((chips, near_high, LANES), jnp.bfloat16),
             pltpu.SemaphoreType.DMA((8,)),
-            pltpu.SemaphoreType.DMA((inner * pool // ROWS,)),
+            pltpu.SemaphoreType.DMA((inner * most // ROWS + chips,)),
         ],
         compiler_params=pltpu.CompilerParams(vmem_limit_bytes=60 * 1024 * 1024),
         name="rows_kernel",
@@ -230,23 +273,38 @@
         outer_bias.reshape(1, chan),
         channel_weight.reshape(1, chan),
     )
-    halves = [[o * inner + i for i in range(inner)] for o in range(OUTER)]
+    halves = [[o * inner + i for i in range(inner)] for o in range(2)]
     got = lax.all_to_all(
-        bucket, "tile", split_axis=0, concat_axis=0, axis_index_groups=halves, tiled=True
-    )
+        far, "tile", split_axis=0, concat_axis=0, axis_index_groups=halves, tiled=True
+    )
+
+    def swap(block, bits):
+        pairs = [(t, t ^ bits) for t in range(tiles)]
+        return lax.ppermute(block, "tile", pairs)
+
+    across = pl.pallas_call(
+        functools.partial(far_kernel, most),
+        out_shape=jax.ShapeDtypeStruct((COL_DEV, width), jnp.bfloat16),
+        in_specs=[vmem],
+        out_specs=vmem,
+        compiler_params=pltpu.CompilerParams(vmem_limit_bytes=16 * 1024 * 1024),
+        name="far_kernel",
+    )(got)
+    from_half = swap(across, inner)
+    came = [near[0]] + [swap(near[j], 2 * j) for j in range(1, chips)]
     own, other = pl.pallas_call(
-        functools.partial(blocks_kernel, tiles, most),
+        functools.partial(near_kernel, most),
         out_shape=[
             jax.ShapeDtypeStruct((COL_DEV, width), jnp.float32),
             jax.ShapeDtypeStruct((COL_DEV, width), jnp.bfloat16),
         ],
-        in_specs=[smem, vmem],
+        in_specs=[smem] + [vmem] * chips,
         out_specs=[vmem, vmem],
         compiler_params=pltpu.CompilerParams(vmem_limit_bytes=24 * 1024 * 1024),
-        name="blocks_kernel",
-    )(me, got)
-    pairs = [(t, (t + inner) % tiles) for t in range(tiles)]
-    return own + lax.ppermute(other, "tile", pairs).astype(jnp.float32)
+        name="near_kernel",
+    )(me, *came)
+    from_core = swap(other, 1)
+    return own + from_core.astype(jnp.float32) + from_half.astype(jnp.float32)
 
 
 def solution(mesh):

time: 42.4 us -> 48.7 us (1.15)
  blocking collectives: 20 us -> 0 us
  starting transfers between devices: 2.65 us -> 19.2 us
  waiting for transfers between devices: 4.47 us -> 13.2 us
  local copies, waits for them, and re-layouts: 0 us -> 0.8 us
    all_to_all x1 -> x0, blocking collectives: 20 us -> none  [per_device(): lax.all_to_all(bucket, 'tile', split_axis=0, concat_axis=0, axis_index_gr...]
    ppermute x1 -> x9, starting transfers between devices: 2.65 us -> 12.9 us  [swap(): return lax.ppermute(block, 'tile', pairs)]
    ppermute x1 -> x9, waiting for transfers between devices: 4.47 us -> 13.2 us  [swap(): return lax.ppermute(block, 'tile', pairs)]
    all_to_all x0 -> x1, starting transfers between devices: none -> 6.3 us  [per_device(): lax.all_to_all(far, 'tile', split_axis=0, concat_axis=0, axis_index_group...]
    unnamed x0 -> x2, local copies, waits for them, and re-layouts: none -> 0.8 us
    pallas_call x2 -> x3, Pallas kernels: 13.6 us -> 13.8 us  [the longest x1 13.1 us: per_device(): pl.pallas_call(functools.partial(rows_kernel, tiles, most), out_shape=[ja...]
  transfers between devices with their start and end apart: 1 -> 10, of which waited for: 1 -> 4; matrix products, arithmetic and copies ran while one was open for 0% -> 0% of each run, Pallas kernels for 0% -> 1%
where the time goes in v21:
time: 48.7 us; the launch traced here: 48.4 us
  starting transfers between devices  19.2 us (39%)
  Pallas kernels  13.8 us (28%)
  waiting for transfers between devices  13.2 us (27%)
  local copies, waits for them, and re-layouts  0.8 us (2%)
  between operations  0.72 us (1%)
  other arithmetic  0.71 us (1%)
    ppermute x9, waiting for transfers between devices, swap(): return lax.ppermute(block, 'tile', pairs)  13.2 us
    pallas_call x1, Pallas kernels, per_device(): pl.pallas_call(functools.partial(rows_kernel, tiles, most), out_shape=[ja...  13.1 us
    ppermute x9, starting transfers between devices, swap(): return lax.ppermute(block, 'tile', pairs)  12.9 us
    all_to_all x1, starting transfers between devices, per_device(): lax.all_to_all(far, 'tile', split_axis=0, concat_axis=0, axis_index_group...  6.3 us
  transfers between devices with their start and end apart: 10, of which 4 were waited for; matrix products, arithmetic and copies ran while one was open for 0% of the time, Pallas kernels for 1%

profile of v21, /device:TPU:0, one launch (start us, length us, event | category | flops | bytes accessed | tf_op | source)
XLA Modules:
  0.0 48.4 jit_solution(17884240768681515308)
XLA Ops:
  0.7 13.1 %rows_kernel.1 = (bf16[16,104,128]{2,1,0:T(8,128)(2,1)}, bf16[200,128]{1,0:T(8,128)(2,1)}, bf16[200,128]{1,0:T(8,128)(2,1)}, bf16[200,128]{1,0:T(8,128)(2,1)}, b...) custom-call(s32[1]{0:T(128)} %bitcast.me_ref, ...), custom_call_target="tpu_custom_call" | custom-call | tf_op jit(solution)/shard_map/rows_kernel/pallas_call | solution.py:240
  13.8 6.3 %all-to-all-start = ((bf16[16,104,128]{2,1,0:T(8,128)(2,1)}), bf16[16,104,128]{2,1,0:T(8,128)(2,1)S(1)}, u32[]{:S(2)}, u32[]{:S(2)}) async-start(bf16[16,104,128]{2,1,0:T(8,128)(2,1)} %get-tuple-element.26), calls=%async_computation | async-start | bytes 851968 | tf_op jit(solution)/shard_map/all_to_all | solution.py:277
  20.1 1.9 %collective-permute-start = (bf16[200,128]{1,0:T(8,128)(2,1)}, bf16[200,128]{1,0:T(8,128)(2,1)S(1)}, u32[]{:S(2)}, u32[]{:S(2)}) collective-permute-start(bf16[200,128]{1,0:T(8,128)(2,1)} %get-tuple-element.17), channel_id=1, source_target_pairs={{0,2},{1,3},{2,0},{3,1},{4,6},{5,7},{6,4},{7,5},{8,10},{9,11},{10,... | collective-permute-start | bytes 153608 | tf_op jit(solution)/shard_map/ppermute | solution.py:283
  22.0 1.5 %collective-permute-start.1 = (bf16[200,128]{1,0:T(8,128)(2,1)}, bf16[200,128]{1,0:T(8,128)(2,1)S(1)}, u32[]{:S(2)}, u32[]{:S(2)}) collective-permute-start(bf16[200,128]{1,0:T(8,128)(2,1)} %get-tuple-element.18), channel_id=1, source_target_pairs={{0,4},{1,5},{2,6},{3,7},{4,0},{5,1},{6,2},{7,3},{8,12},{9,13},{10,... | collective-permute-start | bytes 153608 | tf_op jit(solution)/shard_map/ppermute | solution.py:283
  23.5 0.2 collective-permute-start.2
  23.6 1.9 %collective-permute-start.3 = (bf16[200,128]{1,0:T(8,128)(2,1)}, bf16[200,128]{1,0:T(8,128)(2,1)S(1)}, u32[]{:S(2)}, u32[]{:S(2)}) collective-permute-start(bf16[200,128]{1,0:T(8,128)(2,1)} %get-tuple-element.20), channel_id=1, source_target_pairs={{0,8},{1,9},{2,10},{3,11},{4,12},{5,13},{6,14},{7,15},{8,0},{9,1},... | collective-permute-start | bytes 153608 | tf_op jit(solution)/shard_map/ppermute | solution.py:283
  25.5 1.5 %collective-permute-start.4 = (bf16[200,128]{1,0:T(8,128)(2,1)}, bf16[200,128]{1,0:T(8,128)(2,1)S(1)}, u32[]{:S(2)}, u32[]{:S(2)}) collective-permute-start(bf16[200,128]{1,0:T(8,128)(2,1)} %get-tuple-element.21), channel_id=1, source_target_pairs={{0,10},{1,11},{2,8},{3,9},{4,14},{5,15},{6,12},{7,13},{8,2},{9,3},... | collective-permute-start | bytes 153608 | tf_op jit(solution)/shard_map/ppermute | solution.py:283
  27.0 2.4 %collective-permute-done.refs_1_ = bf16[200,128]{1,0:T(8,128)(2,1)S(1)} collective-permute-done((bf16[200,128]{1,0:T(8,128)(2,1)}, bf16[200,128]{1,0:T(8,128)(2,1)S(1)}, u32[]{:S(2)}, u32[]{:S(2)}) %collective-permute-start) | collective-permute-done | bytes 51232 | tf_op jit(solution)/shard_map/ppermute | solution.py:283
  29.4 3.3 %collective-permute-start.5 = (bf16[200,128]{1,0:T(8,128)(2,1)}, bf16[200,128]{1,0:T(8,128)(2,1)S(1)}, u32[]{:S(2)}, u32[]{:S(2)}) collective-permute-start(bf16[200,128]{1,0:T(8,128)(2,1)} %get-tuple-element.22), channel_id=1, source_target_pairs={{0,12},{1,13},{2,14},{3,15},{4,8},{5,9},{6,10},{7,11},{8,4},{9,5},... | collective-permute-start | bytes 153608 | tf_op jit(solution)/shard_map/ppermute | solution.py:283
  32.6 0.0 collective-permute-done.1.refs_2_
  32.6 0.0 collective-permute-start.6
  32.7 0.0 collective-permute-done.2.refs_3_
  32.7 0.0 collective-permute-done.3.refs_4_
  32.7 0.0 collective-permute-done.4.refs_5_
  32.7 2.3 %collective-permute-done.5.refs_6_ = bf16[200,128]{1,0:T(8,128)(2,1)S(1)} collective-permute-done((bf16[200,128]{1,0:T(8,128)(2,1)}, bf16[200,128]{1,0:T(8,128)(2,1)S(1)}, u32[]{:S(2)}, u32[]{:S(2)}) %collective-permute-start.5) | collective-permute-done | bytes 51232 | tf_op jit(solution)/shard_map/ppermute | solution.py:283
  34.9 3.8 %collective-permute-done.6.refs_7_ = bf16[200,128]{1,0:T(8,128)(2,1)S(1)} collective-permute-done((bf16[200,128]{1,0:T(8,128)(2,1)}, bf16[200,128]{1,0:T(8,128)(2,1)S(1)}, u32[]{:S(2)}, u32[]{:S(2)}) %collective-permute-start.6) | collective-permute-done | bytes 51232 | tf_op jit(solution)/shard_map/ppermute | solution.py:283
  38.8 0.8 %copy-done = bf16[200,128]{1,0:T(8,128)(2,1)S(1)} copy-done((bf16[200,128]{1,0:T(8,128)(2,1)S(1)}, bf16[200,128]{1,0:T(8,128)(2,1)}, u32[]{:S(2)}) %copy-start) | copy-done | bytes 51224
  39.6 0.4 near_kernel.1
  40.0 0.1 collective-permute-start.7
  40.0 0.0 all-to-all-done.got_ref
  40.1 0.3 far_kernel.1
  40.3 2.6 %collective-permute-start.8 = (bf16[128,384]{1,0:T(8,128)(2,1)S(1)}, bf16[128,384]{1,0:T(8,128)(2,1)S(1)}, u32[]{:S(2)}, u32[]{:S(2)}) collective-permute-start(bf16[128,384]{1,0:T(8,128)(2,1)S(1)} %far_kernel.1), channel_id=1, source_target_pairs={{0,16},{1,17},{2,18},{3,19},{4,20},{5,21},{6,22},{7,23},{8,24},{9,... | collective-permute-start | bytes 294920 | tf_op jit(solution)/shard_map/ppermute | solution.py:283
  43.0 4.7 %collective-permute-done.8 = bf16[128,384]{1,0:T(8,128)(2,1)S(1)} collective-permute-done((bf16[128,384]{1,0:T(8,128)(2,1)S(1)}, bf16[128,384]{1,0:T(8,128)(2,1)S(1)}, u32[]{:S(2)}, u32[]{:S(2)}) %collective-permute-start.8) | collective-permute-done | bytes 98336 | tf_op jit(solution)/shard_map/ppermute | solution.py:283
  47.7 0.7 %convert_add_fusion = f32[128,384]{1,0:T(8,128)} fusion(bf16[128,384]{1,0:T(8,128)(2,1)S(1)} %collective-permute-done.8, f32[128,384]{1,0:T(8,128)S(1)} %get-tuple-element.24, bf16[128,384]{1,0:T(8,128)(2,1)S(1)} %collective-permute-done.7), kind=kLoop, calls=%fused_computation | loop fusion | flops 196608 | bytes 589824 | tf_op jit(solution)/shard_map/add | solution.py:307
  (2 shorter events, 0.0 us)
Async XLA Ops:
  13.8 26.3 %all-to-all-start = ((bf16[16,104,128]{2,1,0:T(8,128)(2,1)}), bf16[16,104,128]{2,1,0:T(8,128)(2,1)S(1)}, u32[]{:S(2)}, u32[]{:S(2)}) async-start(bf16[16,104,128]{2,1,0:T(8,128)(2,1)} %get-tuple-element.26), calls=%async_computation | async-start | bytes 851968 | tf_op jit(solution)/shard_map/all_to_all | solution.py:277
  20.1 9.3 %collective-permute-start = (bf16[200,128]{1,0:T(8,128)(2,1)}, bf16[200,128]{1,0:T(8,128)(2,1)S(1)}, u32[]{:S(2)}, u32[]{:S(2)}) collective-permute-start(bf16[200,128]{1,0:T(8,128)(2,1)} %get-tuple-element.17), channel_id=1, source_target_pairs={{0,2},{1,3},{2,0},{3,1},{4,6},{5,7},{6,4},{7,5},{8,10},{9,11},{10,... | collective-permute-start | bytes 153608 | tf_op jit(solution)/shard_map/ppermute | solution.py:283
  22.0 10.6 %collective-permute-start.1 = (bf16[200,128]{1,0:T(8,128)(2,1)}, bf16[200,128]{1,0:T(8,128)(2,1)S(1)}, u32[]{:S(2)}, u32[]{:S(2)}) collective-permute-start(bf16[200,128]{1,0:T(8,128)(2,1)} %get-tuple-element.18), channel_id=1, source_target_pairs={{0,4},{1,5},{2,6},{3,7},{4,0},{5,1},{6,2},{7,3},{8,12},{9,13},{10,... | collective-permute-start | bytes 153608 | tf_op jit(solution)/shard_map/ppermute | solution.py:283
  23.5 9.2 %collective-permute-start.2 = (bf16[200,128]{1,0:T(8,128)(2,1)}, bf16[200,128]{1,0:T(8,128)(2,1)S(1)}, u32[]{:S(2)}, u32[]{:S(2)}) collective-permute-start(bf16[200,128]{1,0:T(8,128)(2,1)} %get-tuple-element.19), channel_id=1, source_target_pairs={{0,6},{1,7},{2,4},{3,5},{4,2},{5,3},{6,0},{7,1},{8,14},{9,15},{10,... | collective-permute-start | bytes 153608 | tf_op jit(solution)/shard_map/ppermute | solution.py:283
  23.6 9.0 %collective-permute-start.3 = (bf16[200,128]{1,0:T(8,128)(2,1)}, bf16[200,128]{1,0:T(8,128)(2,1)S(1)}, u32[]{:S(2)}, u32[]{:S(2)}) collective-permute-start(bf16[200,128]{1,0:T(8,128)(2,1)} %get-tuple-element.20), channel_id=1, source_target_pairs={{0,8},{1,9},{2,10},{3,11},{4,12},{5,13},{6,14},{7,15},{8,0},{9,1},... | collective-permute-start | bytes 153608 | tf_op jit(solution)/shard_map/ppermute | solution.py:283
  25.5 7.2 %collective-permute-start.4 = (bf16[200,128]{1,0:T(8,128)(2,1)}, bf16[200,128]{1,0:T(8,128)(2,1)S(1)}, u32[]{:S(2)}, u32[]{:S(2)}) collective-permute-start(bf16[200,128]{1,0:T(8,128)(2,1)} %get-tuple-element.21), channel_id=1, source_target_pairs={{0,10},{1,11},{2,8},{3,9},{4,14},{5,15},{6,12},{7,13},{8,2},{9,3},... | collective-permute-start | bytes 153608 | tf_op jit(solution)/shard_map/ppermute | solution.py:283
  29.4 5.6 %collective-permute-start.5 = (bf16[200,128]{1,0:T(8,128)(2,1)}, bf16[200,128]{1,0:T(8,128)(2,1)S(1)}, u32[]{:S(2)}, u32[]{:S(2)}) collective-permute-start(bf16[200,128]{1,0:T(8,128)(2,1)} %get-tuple-element.22), channel_id=1, source_target_pairs={{0,12},{1,13},{2,14},{3,15},{4,8},{5,9},{6,10},{7,11},{8,4},{9,5},... | collective-permute-start | bytes 153608 | tf_op jit(solution)/shard_map/ppermute | solution.py:283
  32.6 6.1 %collective-permute-start.6 = (bf16[200,128]{1,0:T(8,128)(2,1)}, bf16[200,128]{1,0:T(8,128)(2,1)S(1)}, u32[]{:S(2)}, u32[]{:S(2)}) collective-permute-start(bf16[200,128]{1,0:T(8,128)(2,1)} %get-tuple-element.23), channel_id=1, source_target_pairs={{0,14},{1,15},{2,12},{3,13},{4,10},{5,11},{6,8},{7,9},{8,6},{9,7},... | collective-permute-start | bytes 153608 | tf_op jit(solution)/shard_map/ppermute | solution.py:283
  38.8 0.8 %copy-start = (bf16[200,128]{1,0:T(8,128)(2,1)S(1)}, bf16[200,128]{1,0:T(8,128)(2,1)}, u32[]{:S(2)}) copy-start(bf16[200,128]{1,0:T(8,128)(2,1)} %get-tuple-element.16.refs_0_) | copy-start | bytes 153604
  40.0 3.0 %collective-permute-start.7 = (bf16[128,384]{1,0:T(8,128)(2,1)S(1)}, bf16[128,384]{1,0:T(8,128)(2,1)S(1)}, u32[]{:S(2)}, u32[]{:S(2)}) collective-permute-start(bf16[128,384]{1,0:T(8,128)(2,1)S(1)} %get-tuple-element.25), channel_id=1, source_target_pairs={{0,1},{1,0},{2,3},{3,2},{4,5},{5,4},{6,7},{7,6},{8,9},{9,8},{10,11... | collective-permute-start | bytes 294920 | tf_op jit(solution)/shard_map/ppermute | solution.py:283
  40.3 7.4 %collective-permute-start.8 = (bf16[128,384]{1,0:T(8,128)(2,1)S(1)}, bf16[128,384]{1,0:T(8,128)(2,1)S(1)}, u32[]{:S(2)}, u32[]{:S(2)}) collective-permute-start(bf16[128,384]{1,0:T(8,128)(2,1)S(1)} %far_kernel.1), channel_id=1, source_target_pairs={{0,16},{1,17},{2,18},{3,19},{4,20},{5,21},{6,22},{7,23},{8,24},{9,... | collective-permute-start | bytes 294920 | tf_op jit(solution)/shard_map/ppermute | solution.py:283

commit v22 on v13

--- a/solution.py
+++ b/solution.py
@@ -34,7 +34,7 @@
     w2_hbm,
     b2_hbm,
     cw_hbm,
-    out_hbm,
+    out_ref,
     prof_ref,
     rad_ref,
     w1_ref,
@@ -44,9 +44,7 @@
     cw_ref,
     hidden_ref,
     factor_ref,
-    out_ref,
     sems,
-    out_sems,
 ):
     rows, width = prof_ref.shape
     hid = w1_ref.shape[1]
@@ -130,7 +128,6 @@
         prof_ref[m, :] = grads.astype(jnp.bfloat16)
     grads = prof_ref[...]
     wide = ROWS // pool
-    sent = []
     for n in range(inner // wide):
         placed = jnp.dot(
             placing[n * ROWS : (n + 1) * ROWS], grads, preferred_element_type=jnp.float32
@@ -140,10 +137,6 @@
             out_ref[some, k * pool : (k + 1) * pool, :] = placed[
                 :, k * LANES : (k + 1) * LANES
             ].reshape(wide, pool, LANES)
-        sent.append(pltpu.make_async_copy(out_ref.at[some], out_hbm.at[some], out_sems.at[n]))
-        sent[-1].start()
-    for copy in sent:
-        copy.wait()
 
 
 def blocks_kernel(tiles, most, me_ref, got_ref, own_ref, other_ref):
@@ -200,7 +193,7 @@
         functools.partial(rows_kernel, tiles, most),
         out_shape=jax.ShapeDtypeStruct((inner, high, LANES), jnp.bfloat16),
         in_specs=[smem, smem, vmem, vmem] + [anywhere] * 7,
-        out_specs=anywhere,
+        out_specs=vmem,
         scratch_shapes=[
             pltpu.VMEM((rows, width), jnp.bfloat16),
             pltpu.VMEM((rows, chan), jnp.bfloat16),
@@ -211,24 +204,27 @@
             pltpu.VMEM((1, chan), jnp.float32),
             pltpu.VMEM((rows, hid), jnp.bfloat16),
             pltpu.VMEM((rows, hid), jnp.float32),
-            pltpu.VMEM((inner, high, LANES), jnp.bfloat16),
             pltpu.SemaphoreType.DMA((8,)),
-            pltpu.SemaphoreType.DMA((inner * pool // ROWS,)),
         ],
-        compiler_params=pltpu.CompilerParams(vmem_limit_bytes=60 * 1024 * 1024),
+        compiler_params=pltpu.CompilerParams(vmem_limit_bytes=40 * 1024 * 1024),
         name="rows_kernel",
     )(
         me,
         counts,
-        owner.reshape(1, rows),
-        column.reshape(1, rows),
-        profiles,
-        radiances,
-        inner_weight,
-        inner_bias.reshape(1, hid),
-        outer_weight,
-        outer_bias.reshape(1, chan),
-        channel_weight.reshape(1, chan),
+        *[
+            pltpu.with_memory_space_constraint(operand, pltpu.HBM)
+            for operand in (
+                owner.reshape(1, rows),
+                column.reshape(1, rows),
+                profiles,
+                radiances,
+                inner_weight,
+                inner_bias.reshape(1, hid),
+                outer_weight,
+                outer_bias.reshape(1, chan),
+                channel_weight.reshape(1, chan),
+            )
+        ],
     )
     halves = [[o * inner + i for i in range(inner)] for o in range(OUTER)]
     got = lax.all_to_all(

time: 42.4 us -> 41.4 us (0.976)
  Pallas kernels: 13.6 us -> 12.9 us
    pallas_call x1, Pallas kernels: 13 us -> 12.3 us  [per_device(): pl.pallas_call(functools.partial(rows_kernel, tiles, most), out_shape=jax...]
where the time goes in v22:
time: 41.4 us; the launch traced here: 41.2 us
  blocking collectives  19.8 us (48%)
  Pallas kernels  12.9 us (31%)
  waiting for transfers between devices  4.46 us (11%)
  starting transfers between devices  2.65 us (6%)
  other arithmetic  0.69 us (2%)
  between operations  0.67 us (2%)
    all_to_all x1, blocking collectives, per_device(): lax.all_to_all(bucket, 'tile', split_axis=0, concat_axis=0, axis_index_gr...  19.8 us
    pallas_call x1, Pallas kernels, per_device(): pl.pallas_call(functools.partial(rows_kernel, tiles, most), out_shape=jax...  12.3 us
    ppermute x1, waiting for transfers between devices, per_device(): return own + lax.ppermute(other, 'tile', pairs).astype(jnp.float32)  4.46 us
    ppermute x1, starting transfers between devices, per_device(): return own + lax.ppermute(other, 'tile', pairs).astype(jnp.float32)  2.65 us
  transfers between devices with their start and end apart: 1, of which 1 were waited for; matrix products, arithmetic and copies ran while one was open for 0% of the time, Pallas kernels for 0%

profile of v22, /device:TPU:0, one launch (start us, length us, event | category | flops | bytes accessed | tf_op | source)
XLA Modules:
  0.0 41.2 jit_solution(14017328892627429448)
XLA Ops:
  0.7 12.3 %rows_kernel.1 = bf16[16,200,128]{2,1,0:T(8,128)(2,1)S(1)} custom-call(s32[1]{0:T(128)} %bitcast.me_ref, s32[1]{0:T(128)S(6)} %copy.11.count_ref, s32[1,512]{1,0:T(1,128)} %bitcast.7, s32[1,512]{1,0:T(1,128)} %bitcast.8, bf16[512,384]{1,0:T(8,128)(2,1)} %prof_hbm.1, bf16[512,512]{1,0:T(8,128)(2,1)} %rad_hbm.1, bf16[384,4096]{1,0:T(8,128)(2,1)} %w1_hbm.1, ...), custom_call_target="tpu_custom_call" | custom-call | tf_op jit(solution)/shard_map/rows_kernel/pallas_call | solution.py:192
  13.0 19.8 %all_to_all.5.got_ref = bf16[16,200,128]{2,1,0:T(8,128)(2,1)S(1)} all-to-all(bf16[16,200,128]{2,1,0:T(8,128)(2,1)S(1)} %rows_kernel.1), channel_id=1, replica_groups={{0,1,2,3,4,5,6,7,8,9,10,11,12,13,14,15},{16,17,18,19,20,21,22,23,24,25,..., dimensions={0} | all-to-all | bytes 1638400 | tf_op jit(solution)/shard_map/all_to_all | solution.py:230
  32.8 0.6 %blocks_kernel.1 = (f32[128,384]{1,0:T(8,128)S(1)}, bf16[128,384]{1,0:T(8,128)(2,1)S(1)}) custom-call(s32[1]{0:T(128)} %bitcast.me_ref, bf16[16,200,128]{2,1,0:T(8,128)(2,1)S(1)} %all_to_all.5.got_ref), custom_call_target="tpu_custom_call" | custom-call | tf_op jit(solution)/shard_map/blocks_kernel/pallas_call | solution.py:233
  33.4 2.6 %collective-permute-start = (bf16[128,384]{1,0:T(8,128)(2,1)S(1)}, bf16[128,384]{1,0:T(8,128)(2,1)S(1)}, u32[]{:S(2)}, u32[]{:S(2)}) collective-permute-start(bf16[128,384]{1,0:T(8,128)(2,1)S(1)} %get-tuple-element.8), channel_id=1, source_target_pairs={{0,16},{1,17},{2,18},{3,19},{4,20},{5,21},{6,22},{7,23},{8,24},{9,... | collective-permute-start | bytes 294920 | tf_op jit(solution)/shard_map/ppermute | solution.py:245
  36.1 4.5 %collective-permute-done = bf16[128,384]{1,0:T(8,128)(2,1)S(1)} collective-permute-done((bf16[128,384]{1,0:T(8,128)(2,1)S(1)}, bf16[128,384]{1,0:T(8,128)(2,1)S(1)}, u32[]{:S(2)}, u32[]{:S(2)}) %collective-permute-start) | collective-permute-done | bytes 98336 | tf_op jit(solution)/shard_map/ppermute | solution.py:245
  40.5 0.7 %convert_add_fusion = f32[128,384]{1,0:T(8,128)} fusion(f32[128,384]{1,0:T(8,128)S(1)} %get-tuple-element.7, bf16[128,384]{1,0:T(8,128)(2,1)S(1)} %collective-permute-done), kind=kLoop, calls=%fused_computation | loop fusion | flops 98304 | bytes 491520 | tf_op jit(solution)/shard_map/add | solution.py:245
Async XLA Ops:
  33.4 7.1 %collective-permute-start = (bf16[128,384]{1,0:T(8,128)(2,1)S(1)}, bf16[128,384]{1,0:T(8,128)(2,1)S(1)}, u32[]{:S(2)}, u32[]{:S(2)}) collective-permute-start(bf16[128,384]{1,0:T(8,128)(2,1)S(1)} %get-tuple-element.8), channel_id=1, source_target_pairs={{0,16},{1,17},{2,18},{3,19},{4,20},{5,21},{6,22},{7,23},{8,24},{9,... | collective-permute-start | bytes 294920 | tf_op jit(solution)/shard_map/ppermute | solution.py:245

commit v23 on v22

--- a/solution.py
+++ b/solution.py
@@ -25,8 +25,8 @@
     most,
     me_ref,
     count_ref,
-    owner_ref,
-    column_ref,
+    owner_hbm,
+    column_hbm,
     prof_hbm,
     rad_hbm,
     w1_hbm,
@@ -35,6 +35,8 @@
     b2_hbm,
     cw_hbm,
     out_ref,
+    owner_ref,
+    column_ref,
     prof_ref,
     rad_ref,
     w1_ref,
@@ -55,41 +57,13 @@
         [(prof_hbm, prof_ref), (b1_hbm, b1_ref)]
         + [(w1_hbm.at[:, piece], w1_ref.at[:, piece]) for piece in pieces]
         + [(w2_hbm, w2_ref), (rad_hbm, rad_ref), (b2_hbm, b2_ref), (cw_hbm, cw_ref)]
+        + [(owner_hbm, owner_ref), (column_hbm, column_ref)]
     )
     copies = [
         pltpu.make_async_copy(src, dst, sems.at[i]) for i, (src, dst) in enumerate(pairs)
     ]
     for copy in copies:
         copy.start()
-
-    inner = out_ref.shape[0]
-    live = lax.broadcasted_iota(jnp.int32, (1, rows), 1) < count_ref[0]
-    owner = jnp.where(live, owner_ref[...], -1)
-    mine = lax.broadcasted_iota(jnp.int32, (tiles, rows), 0) == owner
-    one_hot = mine.astype(jnp.float32)
-    upper = as_bf16(
-        lax.broadcasted_iota(jnp.int32, (rows, rows), 0)
-        <= lax.broadcasted_iota(jnp.int32, (rows, rows), 1)
-    )
-    running = jnp.dot(one_hot.astype(jnp.bfloat16), upper, preferred_element_type=jnp.float32)
-    rank = jnp.sum(running * one_hot, axis=0, keepdims=True).astype(jnp.int32) - 1
-    pool = tiles // inner * most
-    place = owner & (inner - 1)
-    order = lax.shift_right_arithmetic(owner, inner.bit_length() - 1) * most + rank
-    slot = jnp.where(live, place * pool + order, -1)
-    placing = as_bf16(lax.broadcasted_iota(jnp.int32, (inner * pool, rows), 0) == slot)
-    lane = order + lax.rem(me_ref[0], LANES // pool) * pool
-    lane_hot = as_bf16(lax.broadcasted_iota(jnp.int32, (LANES, rows), 0) == lane)
-    here = live & (lax.broadcasted_iota(jnp.int32, (inner, rows), 0) == place)
-    marked = jnp.where(here, (column_ref[...] + 1).astype(jnp.float32), 0.0)
-    labels = lax.dot_general(
-        marked.astype(jnp.bfloat16), lane_hot, NT, preferred_element_type=jnp.float32
-    )
-
-    parts = width // LANES
-    out_ref[:, parts * pool :, :] = jnp.broadcast_to(
-        labels.reshape(inner, 1, LANES), (inner, LABEL_ROWS, LANES)
-    ).astype(jnp.bfloat16)
 
     copies[0].wait()
     copies[1].wait()
@@ -108,6 +82,35 @@
             factor_ref[m, part] = p + hidden * (2.0 - p)
     for copy in copies[2 + len(pieces) :]:
         copy.wait()
+    inner = out_ref.shape[0]
+    live = lax.broadcasted_iota(jnp.int32, (1, rows), 1) < count_ref[0]
+    owner = jnp.where(live, owner_ref[...], -1)
+    mine = lax.broadcasted_iota(jnp.int32, (tiles, rows), 0) == owner
+    one_hot = mine.astype(jnp.float32)
+    upper = as_bf16(
+        lax.broadcasted_iota(jnp.int32, (rows, rows), 0)
+        <= lax.broadcasted_iota(jnp.int32, (rows, rows), 1)
+    )
+    running = jnp.dot(one_hot.astype(jnp.bfloat16), upper, preferred_element_type=jnp.float32)
+    rank = jnp.sum(running * one_hot, axis=0, keepdims=True).astype(jnp.int32) - 1
+    pool = tiles // inner * most
+    place = owner & (inner - 1)
+    order = lax.shift_right_arithmetic(owner, inner.bit_length() - 1) * most + rank
+    slot = jnp.where(live, place * pool + order, -1)
+    placing = as_bf16(lax.broadcasted_iota(jnp.int32, (inner * pool, rows), 0) == slot)
+    lane = order + lax.rem(me_ref[0], LANES // pool) * pool
+    lane_hot = as_bf16(lax.broadcasted_iota(jnp.int32, (LANES, rows), 0) == lane)
+    here = live & (lax.broadcasted_iota(jnp.int32, (inner, rows), 0) == place)
+    marked = jnp.where(here, (column_ref[...] + 1).astype(jnp.float32), 0.0)
+    labels = lax.dot_general(
+        marked.astype(jnp.bfloat16), lane_hot, NT, preferred_element_type=jnp.float32
+    )
+
+    parts = width // LANES
+    out_ref[:, parts * pool :, :] = jnp.broadcast_to(
+        labels.reshape(inner, 1, LANES), (inner, LABEL_ROWS, LANES)
+    ).astype(jnp.bfloat16)
+
     scale = 0.5 * cw_ref[...]
     for n, m in enumerate(blocks):
         output = jnp.dot(hidden_ref[m, :], w2_ref[...], preferred_element_type=jnp.float32)
@@ -192,9 +195,11 @@
     bucket = pl.pallas_call(
         functools.partial(rows_kernel, tiles, most),
         out_shape=jax.ShapeDtypeStruct((inner, high, LANES), jnp.bfloat16),
-        in_specs=[smem, smem, vmem, vmem] + [anywhere] * 7,
+        in_specs=[smem, smem] + [anywhere] * 9,
         out_specs=vmem,
         scratch_shapes=[
+            pltpu.VMEM((1, rows), jnp.int32),
+            pltpu.VMEM((1, rows), jnp.int32),
             pltpu.VMEM((rows, width), jnp.bfloat16),
             pltpu.VMEM((rows, chan), jnp.bfloat16),
             pltpu.VMEM((width, hid), jnp.bfloat16),
@@ -204,7 +209,7 @@
             pltpu.VMEM((1, chan), jnp.float32),
             pltpu.VMEM((rows, hid), jnp.bfloat16),
             pltpu.VMEM((rows, hid), jnp.float32),
-            pltpu.SemaphoreType.DMA((8,)),
+            pltpu.SemaphoreType.DMA((10,)),
         ],
         compiler_params=pltpu.CompilerParams(vmem_limit_bytes=40 * 1024 * 1024),
         name="rows_kernel",

time: 41.4 us -> 40.8 us (0.986)
  Pallas kernels: 12.9 us -> 12.3 us
    pallas_call x1, Pallas kernels: 12.3 us -> 11.7 us  [per_device(): pl.pallas_call(functools.partial(rows_kernel, tiles, most), out_shape=jax...]
where the time goes in v23:
time: 40.8 us; the launch traced here: 40.6 us
  blocking collectives  19.8 us (49%)
  Pallas kernels  12.3 us (30%)
  waiting for transfers between devices  4.46 us (11%)
  starting transfers between devices  2.66 us (7%)
  other arithmetic  0.69 us (2%)
  between operations  0.67 us (2%)
    all_to_all x1, blocking collectives, per_device(): lax.all_to_all(bucket, 'tile', split_axis=0, concat_axis=0, axis_index_gr...  19.8 us
    pallas_call x1, Pallas kernels, per_device(): pl.pallas_call(functools.partial(rows_kernel, tiles, most), out_shape=jax...  11.7 us
    ppermute x1, waiting for transfers between devices, per_device(): return own + lax.ppermute(other, 'tile', pairs).astype(jnp.float32)  4.46 us
    ppermute x1, starting transfers between devices, per_device(): return own + lax.ppermute(other, 'tile', pairs).astype(jnp.float32)  2.66 us
  transfers between devices with their start and end apart: 1, of which 1 were waited for; matrix products, arithmetic and copies ran while one was open for 0% of the time, Pallas kernels for 0%

profile of v23, /device:TPU:0, one launch (start us, length us, event | category | flops | bytes accessed | tf_op | source)
XLA Modules:
  0.0 40.6 jit_solution(9246193028646390156)
XLA Ops:
  0.7 11.7 %rows_kernel.1 = bf16[16,200,128]{2,1,0:T(8,128)(2,1)S(1)} custom-call(s32[1]{0:T(128)} %bitcast.me_ref, s32[1]{0:T(128)S(6)} %copy.11.count_ref, s32[1,512]{1,0:T(1,128)} %bitcast.7, s32[1,512]{1,0:T(1,128)} %bitcast.8, bf16[512,384]{1,0:T(8,128)(2,1)} %prof_hbm.1, bf16[512,512]{1,0:T(8,128)(2,1)} %rad_hbm.1, bf16[384,4096]{1,0:T(8,128)(2,1)} %w1_hbm.1, ...), custom_call_target="tpu_custom_call" | custom-call | tf_op jit(solution)/shard_map/rows_kernel/pallas_call | solution.py:195
  12.4 19.8 %all_to_all.5.got_ref = bf16[16,200,128]{2,1,0:T(8,128)(2,1)S(1)} all-to-all(bf16[16,200,128]{2,1,0:T(8,128)(2,1)S(1)} %rows_kernel.1), channel_id=1, replica_groups={{0,1,2,3,4,5,6,7,8,9,10,11,12,13,14,15},{16,17,18,19,20,21,22,23,24,25,..., dimensions={0} | all-to-all | bytes 1638400 | tf_op jit(solution)/shard_map/all_to_all | solution.py:235
  32.2 0.6 %blocks_kernel.1 = (f32[128,384]{1,0:T(8,128)S(1)}, bf16[128,384]{1,0:T(8,128)(2,1)S(1)}) custom-call(s32[1]{0:T(128)} %bitcast.me_ref, bf16[16,200,128]{2,1,0:T(8,128)(2,1)S(1)} %all_to_all.5.got_ref), custom_call_target="tpu_custom_call" | custom-call | tf_op jit(solution)/shard_map/blocks_kernel/pallas_call | solution.py:238
  32.8 2.7 %collective-permute-start = (bf16[128,384]{1,0:T(8,128)(2,1)S(1)}, bf16[128,384]{1,0:T(8,128)(2,1)S(1)}, u32[]{:S(2)}, u32[]{:S(2)}) collective-permute-start(bf16[128,384]{1,0:T(8,128)(2,1)S(1)} %get-tuple-element.8), channel_id=1, source_target_pairs={{0,16},{1,17},{2,18},{3,19},{4,20},{5,21},{6,22},{7,23},{8,24},{9,... | collective-permute-start | bytes 294920 | tf_op jit(solution)/shard_map/ppermute | solution.py:250
  35.5 4.5 %collective-permute-done = bf16[128,384]{1,0:T(8,128)(2,1)S(1)} collective-permute-done((bf16[128,384]{1,0:T(8,128)(2,1)S(1)}, bf16[128,384]{1,0:T(8,128)(2,1)S(1)}, u32[]{:S(2)}, u32[]{:S(2)}) %collective-permute-start) | collective-permute-done | bytes 98336 | tf_op jit(solution)/shard_map/ppermute | solution.py:250
  39.9 0.7 %convert_add_fusion = f32[128,384]{1,0:T(8,128)} fusion(f32[128,384]{1,0:T(8,128)S(1)} %get-tuple-element.7, bf16[128,384]{1,0:T(8,128)(2,1)S(1)} %collective-permute-done), kind=kLoop, calls=%fused_computation | loop fusion | flops 98304 | bytes 491520 | tf_op jit(solution)/shard_map/add | solution.py:250
Async XLA Ops:
  32.8 7.1 %collective-permute-start = (bf16[128,384]{1,0:T(8,128)(2,1)S(1)}, bf16[128,384]{1,0:T(8,128)(2,1)S(1)}, u32[]{:S(2)}, u32[]{:S(2)}) collective-permute-start(bf16[128,384]{1,0:T(8,128)(2,1)S(1)} %get-tuple-element.8), channel_id=1, source_target_pairs={{0,16},{1,17},{2,18},{3,19},{4,20},{5,21},{6,22},{7,23},{8,24},{9,... | collective-permute-start | bytes 294920 | tf_op jit(solution)/shard_map/ppermute | solution.py:250

commit v24 on v23

--- a/solution.py
+++ b/solution.py
@@ -79,7 +79,7 @@
             p = jnp.tanh(u) + 1.0
             hidden = u * p
             hidden_ref[m, part] = hidden.astype(jnp.bfloat16)
-            factor_ref[m, part] = p + hidden * (2.0 - p)
+            factor_ref[m, part] = p
     for copy in copies[2 + len(pieces) :]:
         copy.wait()
     inner = out_ref.shape[0]
@@ -123,7 +123,9 @@
             back = lax.dot_general(
                 rad_ref[m, :], w2_ref[part, :], NT, preferred_element_type=jnp.float32
             )
-            hidden_ref[m, part] = (back * factor_ref[m, part]).astype(jnp.bfloat16)
+            p = factor_ref[m, part]
+            factor = p + hidden_ref[m, part].astype(jnp.float32) * (2.0 - p)
+            hidden_ref[m, part] = (back * factor).astype(jnp.bfloat16)
     for m in blocks:
         grads = lax.dot_general(
             hidden_ref[m, :], w1_ref[...], NT, preferred_element_type=jnp.float32

time: 40.8 us -> 40.8 us (level)
  no operation moved by 1% of the time
where the time goes in v24:
time: 40.8 us; the launch traced here: 40.6 us
  blocking collectives  19.8 us (49%)
  Pallas kernels  12.4 us (30%)
  waiting for transfers between devices  4.46 us (11%)
  starting transfers between devices  2.66 us (7%)
  other arithmetic  0.69 us (2%)
  between operations  0.67 us (2%)
    all_to_all x1, blocking collectives, per_device(): lax.all_to_all(bucket, 'tile', split_axis=0, concat_axis=0, axis_index_gr...  19.8 us
    pallas_call x1, Pallas kernels, per_device(): pl.pallas_call(functools.partial(rows_kernel, tiles, most), out_shape=jax...  11.7 us
    ppermute x1, waiting for transfers between devices, per_device(): return own + lax.ppermute(other, 'tile', pairs).astype(jnp.float32)  4.46 us
    ppermute x1, starting transfers between devices, per_device(): return own + lax.ppermute(other, 'tile', pairs).astype(jnp.float32)  2.66 us
  transfers between devices with their start and end apart: 1, of which 1 were waited for; matrix products, arithmetic and copies ran while one was open for 0% of the time, Pallas kernels for 0%

profile of v24, /device:TPU:0, one launch (start us, length us, event | category | flops | bytes accessed | tf_op | source)
XLA Modules:
  0.0 40.6 jit_solution(10016204263309856568)
XLA Ops:
  0.7 11.7 %rows_kernel.1 = bf16[16,200,128]{2,1,0:T(8,128)(2,1)S(1)} custom-call(s32[1]{0:T(128)} %bitcast.me_ref, s32[1]{0:T(128)S(6)} %copy.11.count_ref, s32[1,512]{1,0:T(1,128)} %bitcast.7, s32[1,512]{1,0:T(1,128)} %bitcast.8, bf16[512,384]{1,0:T(8,128)(2,1)} %prof_hbm.1, bf16[512,512]{1,0:T(8,128)(2,1)} %rad_hbm.1, bf16[384,4096]{1,0:T(8,128)(2,1)} %w1_hbm.1, ...), custom_call_target="tpu_custom_call" | custom-call | tf_op jit(solution)/shard_map/rows_kernel/pallas_call | solution.py:197
  12.4 19.8 %all_to_all.5.got_ref = bf16[16,200,128]{2,1,0:T(8,128)(2,1)S(1)} all-to-all(bf16[16,200,128]{2,1,0:T(8,128)(2,1)S(1)} %rows_kernel.1), channel_id=1, replica_groups={{0,1,2,3,4,5,6,7,8,9,10,11,12,13,14,15},{16,17,18,19,20,21,22,23,24,25,..., dimensions={0} | all-to-all | bytes 1638400 | tf_op jit(solution)/shard_map/all_to_all | solution.py:237
  32.2 0.6 %blocks_kernel.1 = (f32[128,384]{1,0:T(8,128)S(1)}, bf16[128,384]{1,0:T(8,128)(2,1)S(1)}) custom-call(s32[1]{0:T(128)} %bitcast.me_ref, bf16[16,200,128]{2,1,0:T(8,128)(2,1)S(1)} %all_to_all.5.got_ref), custom_call_target="tpu_custom_call" | custom-call | tf_op jit(solution)/shard_map/blocks_kernel/pallas_call | solution.py:240
  32.8 2.7 %collective-permute-start = (bf16[128,384]{1,0:T(8,128)(2,1)S(1)}, bf16[128,384]{1,0:T(8,128)(2,1)S(1)}, u32[]{:S(2)}, u32[]{:S(2)}) collective-permute-start(bf16[128,384]{1,0:T(8,128)(2,1)S(1)} %get-tuple-element.8), channel_id=1, source_target_pairs={{0,16},{1,17},{2,18},{3,19},{4,20},{5,21},{6,22},{7,23},{8,24},{9,... | collective-permute-start | bytes 294920 | tf_op jit(solution)/shard_map/ppermute | solution.py:252
  35.5 4.5 %collective-permute-done = bf16[128,384]{1,0:T(8,128)(2,1)S(1)} collective-permute-done((bf16[128,384]{1,0:T(8,128)(2,1)S(1)}, bf16[128,384]{1,0:T(8,128)(2,1)S(1)}, u32[]{:S(2)}, u32[]{:S(2)}) %collective-permute-start) | collective-permute-done | bytes 98336 | tf_op jit(solution)/shard_map/ppermute | solution.py:252
  39.9 0.7 %convert_add_fusion = f32[128,384]{1,0:T(8,128)} fusion(f32[128,384]{1,0:T(8,128)S(1)} %get-tuple-element.7, bf16[128,384]{1,0:T(8,128)(2,1)S(1)} %collective-permute-done), kind=kLoop, calls=%fused_computation | loop fusion | flops 98304 | bytes 491520 | tf_op jit(solution)/shard_map/add | solution.py:252
Async XLA Ops:
  32.8 7.1 %collective-permute-start = (bf16[128,384]{1,0:T(8,128)(2,1)S(1)}, bf16[128,384]{1,0:T(8,128)(2,1)S(1)}, u32[]{:S(2)}, u32[]{:S(2)}) collective-permute-start(bf16[128,384]{1,0:T(8,128)(2,1)S(1)} %get-tuple-element.8), channel_id=1, source_target_pairs={{0,16},{1,17},{2,18},{3,19},{4,20},{5,21},{6,22},{7,23},{8,24},{9,... | collective-permute-start | bytes 294920 | tf_op jit(solution)/shard_map/ppermute | solution.py:252

commit v25 on v23

--- a/solution.py
+++ b/solution.py
@@ -46,6 +46,7 @@
     cw_ref,
     hidden_ref,
     factor_ref,
+    grads_ref,
     sems,
 ):
     rows, width = prof_ref.shape
@@ -126,14 +127,16 @@
             hidden_ref[m, part] = (back * factor_ref[m, part]).astype(jnp.bfloat16)
     for m in blocks:
         grads = lax.dot_general(
-            hidden_ref[m, :], w1_ref[...], NT, preferred_element_type=jnp.float32
+            w1_ref[...], hidden_ref[m, :], NT, preferred_element_type=jnp.float32
         )
-        prof_ref[m, :] = grads.astype(jnp.bfloat16)
-    grads = prof_ref[...]
+        grads_ref[:, m] = grads.astype(jnp.bfloat16)
     wide = ROWS // pool
     for n in range(inner // wide):
-        placed = jnp.dot(
-            placing[n * ROWS : (n + 1) * ROWS], grads, preferred_element_type=jnp.float32
+        placed = lax.dot_general(
+            placing[n * ROWS : (n + 1) * ROWS],
+            grads_ref[...],
+            NT,
+            preferred_element_type=jnp.float32,
         ).astype(jnp.bfloat16)
         some = pl.ds(n * wide, wide)
         for k in range(parts):
@@ -209,6 +212,7 @@
             pltpu.VMEM((1, chan), jnp.float32),
             pltpu.VMEM((rows, hid), jnp.bfloat16),
             pltpu.VMEM((rows, hid), jnp.float32),
+            pltpu.VMEM((width, rows), jnp.bfloat16),
             pltpu.SemaphoreType.DMA((10,)),
         ],
         compiler_params=pltpu.CompilerParams(vmem_limit_bytes=40 * 1024 * 1024),

time: 40.8 us -> 40.2 us (0.985)
  Pallas kernels: 12.3 us -> 11.8 us
    pallas_call x1, Pallas kernels: 11.7 us -> 11.2 us  [per_device(): pl.pallas_call(functools.partial(rows_kernel, tiles, most), out_shape=jax...]
where the time goes in v25:
time: 40.2 us; the launch traced here: 40.1 us
  blocking collectives  19.8 us (49%)
  Pallas kernels  11.8 us (29%)
  waiting for transfers between devices  4.46 us (11%)
  starting transfers between devices  2.66 us (7%)
  other arithmetic  0.69 us (2%)
  between operations  0.67 us (2%)
    all_to_all x1, blocking collectives, per_device(): lax.all_to_all(bucket, 'tile', split_axis=0, concat_axis=0, axis_index_gr...  19.8 us
    pallas_call x1, Pallas kernels, per_device(): pl.pallas_call(functools.partial(rows_kernel, tiles, most), out_shape=jax...  11.2 us
    ppermute x1, waiting for transfers between devices, per_device(): return own + lax.ppermute(other, 'tile', pairs).astype(jnp.float32)  4.46 us
    ppermute x1, starting transfers between devices, per_device(): return own + lax.ppermute(other, 'tile', pairs).astype(jnp.float32)  2.66 us
  transfers between devices with their start and end apart: 1, of which 1 were waited for; matrix products, arithmetic and copies ran while one was open for 0% of the time, Pallas kernels for 0%

profile of v25, /device:TPU:0, one launch (start us, length us, event | category | flops | bytes accessed | tf_op | source)
XLA Modules:
  0.0 40.1 jit_solution(10179349707598448225)
XLA Ops:
  0.7 11.2 %rows_kernel.1 = bf16[16,200,128]{2,1,0:T(8,128)(2,1)S(1)} custom-call(s32[1]{0:T(128)} %bitcast.me_ref, s32[1]{0:T(128)S(6)} %copy.11.count_ref, s32[1,512]{1,0:T(1,128)} %bitcast.7, s32[1,512]{1,0:T(1,128)} %bitcast.8, bf16[512,384]{1,0:T(8,128)(2,1)} %prof_hbm.1, bf16[512,512]{1,0:T(8,128)(2,1)} %rad_hbm.1, bf16[384,4096]{1,0:T(8,128)(2,1)} %w1_hbm.1, ...), custom_call_target="tpu_custom_call" | custom-call | tf_op jit(solution)/shard_map/rows_kernel/pallas_call | solution.py:198
  11.8 19.8 %all_to_all.5.got_ref = bf16[16,200,128]{2,1,0:T(8,128)(2,1)S(1)} all-to-all(bf16[16,200,128]{2,1,0:T(8,128)(2,1)S(1)} %rows_kernel.1), channel_id=1, replica_groups={{0,1,2,3,4,5,6,7,8,9,10,11,12,13,14,15},{16,17,18,19,20,21,22,23,24,25,..., dimensions={0} | all-to-all | bytes 1638400 | tf_op jit(solution)/shard_map/all_to_all | solution.py:239
  31.6 0.6 %blocks_kernel.1 = (f32[128,384]{1,0:T(8,128)S(1)}, bf16[128,384]{1,0:T(8,128)(2,1)S(1)}) custom-call(s32[1]{0:T(128)} %bitcast.me_ref, bf16[16,200,128]{2,1,0:T(8,128)(2,1)S(1)} %all_to_all.5.got_ref), custom_call_target="tpu_custom_call" | custom-call | tf_op jit(solution)/shard_map/blocks_kernel/pallas_call | solution.py:242
  32.2 2.7 %collective-permute-start = (bf16[128,384]{1,0:T(8,128)(2,1)S(1)}, bf16[128,384]{1,0:T(8,128)(2,1)S(1)}, u32[]{:S(2)}, u32[]{:S(2)}) collective-permute-start(bf16[128,384]{1,0:T(8,128)(2,1)S(1)} %get-tuple-element.8), channel_id=1, source_target_pairs={{0,16},{1,17},{2,18},{3,19},{4,20},{5,21},{6,22},{7,23},{8,24},{9,... | collective-permute-start | bytes 294920 | tf_op jit(solution)/shard_map/ppermute | solution.py:254
  34.9 4.5 %collective-permute-done = bf16[128,384]{1,0:T(8,128)(2,1)S(1)} collective-permute-done((bf16[128,384]{1,0:T(8,128)(2,1)S(1)}, bf16[128,384]{1,0:T(8,128)(2,1)S(1)}, u32[]{:S(2)}, u32[]{:S(2)}) %collective-permute-start) | collective-permute-done | bytes 98336 | tf_op jit(solution)/shard_map/ppermute | solution.py:254
  39.4 0.7 %convert_add_fusion = f32[128,384]{1,0:T(8,128)} fusion(f32[128,384]{1,0:T(8,128)S(1)} %get-tuple-element.7, bf16[128,384]{1,0:T(8,128)(2,1)S(1)} %collective-permute-done), kind=kLoop, calls=%fused_computation | loop fusion | flops 98304 | bytes 491520 | tf_op jit(solution)/shard_map/add | solution.py:254
Async XLA Ops:
  32.2 7.1 %collective-permute-start = (bf16[128,384]{1,0:T(8,128)(2,1)S(1)}, bf16[128,384]{1,0:T(8,128)(2,1)S(1)}, u32[]{:S(2)}, u32[]{:S(2)}) collective-permute-start(bf16[128,384]{1,0:T(8,128)(2,1)S(1)} %get-tuple-element.8), channel_id=1, source_target_pairs={{0,16},{1,17},{2,18},{3,19},{4,20},{5,21},{6,22},{7,23},{8,24},{9,... | collective-permute-start | bytes 294920 | tf_op jit(solution)/shard_map/ppermute | solution.py:254

commit v26 on v25

--- a/solution.py
+++ b/solution.py
@@ -66,6 +66,10 @@
     for copy in copies:
         copy.start()
 
+    upper = as_bf16(
+        lax.broadcasted_iota(jnp.int32, (rows, rows), 0)
+        <= lax.broadcasted_iota(jnp.int32, (rows, rows), 1)
+    )
     copies[0].wait()
     copies[1].wait()
     prof_ref[...] = (prof_ref[...].astype(jnp.float32) * 0.5).astype(jnp.bfloat16)
@@ -74,6 +78,9 @@
         part = pl.ds(i * CHUNK, CHUNK)
         if i * CHUNK in starts:
             copies[2 + starts.index(i * CHUNK)].wait()
+        if i * CHUNK == hid * 7 // 8:
+            for copy in copies[2 + len(pieces) :]:
+                copy.wait()
         for m in blocks:
             u = jnp.dot(prof_ref[m, :], w1_ref[:, part], preferred_element_type=jnp.float32)
             u = u + 0.5 * b1_ref[:, part]
@@ -81,17 +88,11 @@
             hidden = u * p
             hidden_ref[m, part] = hidden.astype(jnp.bfloat16)
             factor_ref[m, part] = p + hidden * (2.0 - p)
-    for copy in copies[2 + len(pieces) :]:
-        copy.wait()
     inner = out_ref.shape[0]
     live = lax.broadcasted_iota(jnp.int32, (1, rows), 1) < count_ref[0]
     owner = jnp.where(live, owner_ref[...], -1)
     mine = lax.broadcasted_iota(jnp.int32, (tiles, rows), 0) == owner
     one_hot = mine.astype(jnp.float32)
-    upper = as_bf16(
-        lax.broadcasted_iota(jnp.int32, (rows, rows), 0)
-        <= lax.broadcasted_iota(jnp.int32, (rows, rows), 1)
-    )
     running = jnp.dot(one_hot.astype(jnp.bfloat16), upper, preferred_element_type=jnp.float32)
     rank = jnp.sum(running * one_hot, axis=0, keepdims=True).astype(jnp.int32) - 1
     pool = tiles // inner * most

time: 40.2 us -> 40.3 us (level)
  no operation moved by 1% of the time
where the time goes in v26:
time: 40.3 us; the launch traced here: 40.1 us
  blocking collectives  19.8 us (49%)
  Pallas kernels  11.8 us (29%)
  waiting for transfers between devices  4.46 us (11%)
  starting transfers between devices  2.66 us (7%)
  other arithmetic  0.69 us (2%)
  between operations  0.67 us (2%)
    all_to_all x1, blocking collectives, per_device(): lax.all_to_all(bucket, 'tile', split_axis=0, concat_axis=0, axis_index_gr...  19.8 us
    pallas_call x1, Pallas kernels, per_device(): pl.pallas_call(functools.partial(rows_kernel, tiles, most), out_shape=jax...  11.2 us
    ppermute x1, waiting for transfers between devices, per_device(): return own + lax.ppermute(other, 'tile', pairs).astype(jnp.float32)  4.46 us
    ppermute x1, starting transfers between devices, per_device(): return own + lax.ppermute(other, 'tile', pairs).astype(jnp.float32)  2.66 us
  transfers between devices with their start and end apart: 1, of which 1 were waited for; matrix products, arithmetic and copies ran while one was open for 0% of the time, Pallas kernels for 0%

profile of v26, /device:TPU:0, one launch (start us, length us, event | category | flops | bytes accessed | tf_op | source)
XLA Modules:
  0.0 40.1 jit_solution(3652266042705627870)
XLA Ops:
  0.7 11.2 %rows_kernel.1 = bf16[16,200,128]{2,1,0:T(8,128)(2,1)S(1)} custom-call(s32[1]{0:T(128)} %bitcast.me_ref, s32[1]{0:T(128)S(6)} %copy.11.count_ref, s32[1,512]{1,0:T(1,128)} %bitcast.7, s32[1,512]{1,0:T(1,128)} %bitcast.8, bf16[512,384]{1,0:T(8,128)(2,1)} %prof_hbm.1, bf16[512,512]{1,0:T(8,128)(2,1)} %rad_hbm.1, bf16[384,4096]{1,0:T(8,128)(2,1)} %w1_hbm.1, ...), custom_call_target="tpu_custom_call" | custom-call | tf_op jit(solution)/shard_map/rows_kernel/pallas_call | solution.py:199
  11.9 19.8 %all_to_all.5.got_ref = bf16[16,200,128]{2,1,0:T(8,128)(2,1)S(1)} all-to-all(bf16[16,200,128]{2,1,0:T(8,128)(2,1)S(1)} %rows_kernel.1), channel_id=1, replica_groups={{0,1,2,3,4,5,6,7,8,9,10,11,12,13,14,15},{16,17,18,19,20,21,22,23,24,25,..., dimensions={0} | all-to-all | bytes 1638400 | tf_op jit(solution)/shard_map/all_to_all | solution.py:240
  31.7 0.6 %blocks_kernel.1 = (f32[128,384]{1,0:T(8,128)S(1)}, bf16[128,384]{1,0:T(8,128)(2,1)S(1)}) custom-call(s32[1]{0:T(128)} %bitcast.me_ref, bf16[16,200,128]{2,1,0:T(8,128)(2,1)S(1)} %all_to_all.5.got_ref), custom_call_target="tpu_custom_call" | custom-call | tf_op jit(solution)/shard_map/blocks_kernel/pallas_call | solution.py:243
  32.3 2.7 %collective-permute-start = (bf16[128,384]{1,0:T(8,128)(2,1)S(1)}, bf16[128,384]{1,0:T(8,128)(2,1)S(1)}, u32[]{:S(2)}, u32[]{:S(2)}) collective-permute-start(bf16[128,384]{1,0:T(8,128)(2,1)S(1)} %get-tuple-element.8), channel_id=1, source_target_pairs={{0,16},{1,17},{2,18},{3,19},{4,20},{5,21},{6,22},{7,23},{8,24},{9,... | collective-permute-start | bytes 294920 | tf_op jit(solution)/shard_map/ppermute | solution.py:255
  35.0 4.5 %collective-permute-done = bf16[128,384]{1,0:T(8,128)(2,1)S(1)} collective-permute-done((bf16[128,384]{1,0:T(8,128)(2,1)S(1)}, bf16[128,384]{1,0:T(8,128)(2,1)S(1)}, u32[]{:S(2)}, u32[]{:S(2)}) %collective-permute-start) | collective-permute-done | bytes 98336 | tf_op jit(solution)/shard_map/ppermute | solution.py:255
  39.4 0.7 %convert_add_fusion = f32[128,384]{1,0:T(8,128)} fusion(f32[128,384]{1,0:T(8,128)S(1)} %get-tuple-element.7, bf16[128,384]{1,0:T(8,128)(2,1)S(1)} %collective-permute-done), kind=kLoop, calls=%fused_computation | loop fusion | flops 98304 | bytes 491520 | tf_op jit(solution)/shard_map/add | solution.py:255
Async XLA Ops:
  32.3 7.1 %collective-permute-start = (bf16[128,384]{1,0:T(8,128)(2,1)S(1)}, bf16[128,384]{1,0:T(8,128)(2,1)S(1)}, u32[]{:S(2)}, u32[]{:S(2)}) collective-permute-start(bf16[128,384]{1,0:T(8,128)(2,1)S(1)} %get-tuple-element.8), channel_id=1, source_target_pairs={{0,16},{1,17},{2,18},{3,19},{4,20},{5,21},{6,22},{7,23},{8,24},{9,... | collective-permute-start | bytes 294920 | tf_op jit(solution)/shard_map/ppermute | solution.py:255

commit v27 on v26

--- a/solution.py
+++ b/solution.py
@@ -47,16 +47,17 @@
     hidden_ref,
     factor_ref,
     grads_ref,
+    half_ref,
     sems,
 ):
     rows, width = prof_ref.shape
-    hid = w1_ref.shape[1]
+    depth, hid = w1_ref.shape
     chan = rad_ref.shape[1]
     starts = [0, hid // 4, hid]
     pieces = [pl.ds(lo, hi - lo) for lo, hi in zip(starts[:-1], starts[1:])]
     pairs = (
         [(prof_hbm, prof_ref), (b1_hbm, b1_ref)]
-        + [(w1_hbm.at[:, piece], w1_ref.at[:, piece]) for piece in pieces]
+        + [(w1_hbm.at[:, piece], w1_ref.at[pl.ds(0, width), piece]) for piece in pieces]
         + [(w2_hbm, w2_ref), (rad_hbm, rad_ref), (b2_hbm, b2_ref), (cw_hbm, cw_ref)]
         + [(owner_hbm, owner_ref), (column_hbm, column_ref)]
     )
@@ -70,9 +71,18 @@
         lax.broadcasted_iota(jnp.int32, (rows, rows), 0)
         <= lax.broadcasted_iota(jnp.int32, (rows, rows), 1)
     )
+    ones = lax.broadcasted_iota(jnp.int32, (rows, depth - width), 1) < 3
+    half_ref[:, width:] = as_bf16(ones)
+    w1_ref[width + 16 :, :] = jnp.zeros((depth - width - 16, hid), jnp.bfloat16)
     copies[0].wait()
     copies[1].wait()
-    prof_ref[...] = (prof_ref[...].astype(jnp.float32) * 0.5).astype(jnp.bfloat16)
+    half_ref[:, :width] = (prof_ref[...].astype(jnp.float32) * 0.5).astype(jnp.bfloat16)
+    bias = 0.5 * b1_ref[...]
+    high = bias.astype(jnp.bfloat16).astype(jnp.float32)
+    low = (bias - high).astype(jnp.bfloat16).astype(jnp.float32)
+    line = lax.broadcasted_iota(jnp.int32, (16, hid), 0)
+    terms = jnp.where(line == 0, high, jnp.where(line == 1, low, bias - high - low))
+    w1_ref[width : width + 16, :] = jnp.where(line < 3, terms, 0.0).astype(jnp.bfloat16)
     blocks = [pl.ds(i, ROWS) for i in range(0, rows, ROWS)]
     for i in range(hid // CHUNK):
         part = pl.ds(i * CHUNK, CHUNK)
@@ -82,8 +92,7 @@
             for copy in copies[2 + len(pieces) :]:
                 copy.wait()
         for m in blocks:
-            u = jnp.dot(prof_ref[m, :], w1_ref[:, part], preferred_element_type=jnp.float32)
-            u = u + 0.5 * b1_ref[:, part]
+            u = jnp.dot(half_ref[m, :], w1_ref[:, part], preferred_element_type=jnp.float32)
             p = jnp.tanh(u) + 1.0
             hidden = u * p
             hidden_ref[m, part] = hidden.astype(jnp.bfloat16)
@@ -128,7 +137,7 @@
             hidden_ref[m, part] = (back * factor_ref[m, part]).astype(jnp.bfloat16)
     for m in blocks:
         grads = lax.dot_general(
-            w1_ref[...], hidden_ref[m, :], NT, preferred_element_type=jnp.float32
+            w1_ref[:width, :], hidden_ref[m, :], NT, preferred_element_type=jnp.float32
         )
         grads_ref[:, m] = grads.astype(jnp.bfloat16)
     wide = ROWS // pool
@@ -189,6 +198,7 @@
     hid = inner_weight.shape[1]
     chan = radiances.shape[1]
     most = max(2, 2 * rows // tiles)
+    depth = width + LANES
     inner = tiles // OUTER
     pool = OUTER * most
     high = width // LANES * pool + LABEL_ROWS
@@ -206,7 +216,7 @@
             pltpu.VMEM((1, rows), jnp.int32),
             pltpu.VMEM((rows, width), jnp.bfloat16),
             pltpu.VMEM((rows, chan), jnp.bfloat16),
-            pltpu.VMEM((width, hid), jnp.bfloat16),
+            pltpu.VMEM((depth, hid), jnp.bfloat16),
             pltpu.VMEM((1, hid), jnp.float32),
             pltpu.VMEM((hid, chan), jnp.bfloat16),
             pltpu.VMEM((1, chan), jnp.float32),
@@ -214,6 +224,7 @@
             pltpu.VMEM((rows, hid), jnp.bfloat16),
             pltpu.VMEM((rows, hid), jnp.float32),
             pltpu.VMEM((width, rows), jnp.bfloat16),
+            pltpu.VMEM((rows, depth), jnp.bfloat16),
             pltpu.SemaphoreType.DMA((10,)),
         ],
         compiler_params=pltpu.CompilerParams(vmem_limit_bytes=40 * 1024 * 1024),

time: 40.3 us -> 40.2 us (level)
  no operation moved by 1% of the time
where the time goes in v27:
time: 40.2 us; the launch traced here: 40 us
  blocking collectives  19.8 us (49%)
  Pallas kernels  11.8 us (29%)
  waiting for transfers between devices  4.46 us (11%)
  starting transfers between devices  2.65 us (7%)
  other arithmetic  0.69 us (2%)
  between operations  0.67 us (2%)
    all_to_all x1, blocking collectives, per_device(): lax.all_to_all(bucket, 'tile', split_axis=0, concat_axis=0, axis_index_gr...  19.8 us
    pallas_call x1, Pallas kernels, per_device(): pl.pallas_call(functools.partial(rows_kernel, tiles, most), out_shape=jax...  11.1 us
    ppermute x1, waiting for transfers between devices, per_device(): return own + lax.ppermute(other, 'tile', pairs).astype(jnp.float32)  4.46 us
    ppermute x1, starting transfers between devices, per_device(): return own + lax.ppermute(other, 'tile', pairs).astype(jnp.float32)  2.65 us
  transfers between devices with their start and end apart: 1, of which 1 were waited for; matrix products, arithmetic and copies ran while one was open for 0% of the time, Pallas kernels for 0%

profile of v27, /device:TPU:0, one launch (start us, length us, event | category | flops | bytes accessed | tf_op | source)
XLA Modules:
  0.0 40.0 jit_solution(11139225238641992180)
XLA Ops:
  0.7 11.1 %rows_kernel.1 = bf16[16,200,128]{2,1,0:T(8,128)(2,1)S(1)} custom-call(s32[1]{0:T(128)} %bitcast.me_ref, s32[1]{0:T(128)S(6)} %copy.11.count_ref, s32[1,512]{1,0:T(1,128)} %bitcast.7, s32[1,512]{1,0:T(1,128)} %bitcast.8, bf16[512,384]{1,0:T(8,128)(2,1)} %prof_hbm.1, bf16[512,512]{1,0:T(8,128)(2,1)} %rad_hbm.1, bf16[384,4096]{1,0:T(8,128)(2,1)} %w1_hbm.1, ...), custom_call_target="tpu_custom_call" | custom-call | tf_op jit(solution)/shard_map/rows_kernel/pallas_call | solution.py:209
  11.8 19.8 %all_to_all.5.got_ref = bf16[16,200,128]{2,1,0:T(8,128)(2,1)S(1)} all-to-all(bf16[16,200,128]{2,1,0:T(8,128)(2,1)S(1)} %rows_kernel.1), channel_id=1, replica_groups={{0,1,2,3,4,5,6,7,8,9,10,11,12,13,14,15},{16,17,18,19,20,21,22,23,24,25,..., dimensions={0} | all-to-all | bytes 1638400 | tf_op jit(solution)/shard_map/all_to_all | solution.py:251
  31.6 0.6 %blocks_kernel.1 = (f32[128,384]{1,0:T(8,128)S(1)}, bf16[128,384]{1,0:T(8,128)(2,1)S(1)}) custom-call(s32[1]{0:T(128)} %bitcast.me_ref, bf16[16,200,128]{2,1,0:T(8,128)(2,1)S(1)} %all_to_all.5.got_ref), custom_call_target="tpu_custom_call" | custom-call | tf_op jit(solution)/shard_map/blocks_kernel/pallas_call | solution.py:254
  32.2 2.7 %collective-permute-start = (bf16[128,384]{1,0:T(8,128)(2,1)S(1)}, bf16[128,384]{1,0:T(8,128)(2,1)S(1)}, u32[]{:S(2)}, u32[]{:S(2)}) collective-permute-start(bf16[128,384]{1,0:T(8,128)(2,1)S(1)} %get-tuple-element.8), channel_id=1, source_target_pairs={{0,16},{1,17},{2,18},{3,19},{4,20},{5,21},{6,22},{7,23},{8,24},{9,... | collective-permute-start | bytes 294920 | tf_op jit(solution)/shard_map/ppermute | solution.py:266
  34.9 4.5 %collective-permute-done = bf16[128,384]{1,0:T(8,128)(2,1)S(1)} collective-permute-done((bf16[128,384]{1,0:T(8,128)(2,1)S(1)}, bf16[128,384]{1,0:T(8,128)(2,1)S(1)}, u32[]{:S(2)}, u32[]{:S(2)}) %collective-permute-start) | collective-permute-done | bytes 98336 | tf_op jit(solution)/shard_map/ppermute | solution.py:266
  39.3 0.7 %convert_add_fusion = f32[128,384]{1,0:T(8,128)} fusion(f32[128,384]{1,0:T(8,128)S(1)} %get-tuple-element.7, bf16[128,384]{1,0:T(8,128)(2,1)S(1)} %collective-permute-done), kind=kLoop, calls=%fused_computation | loop fusion | flops 98304 | bytes 491520 | tf_op jit(solution)/shard_map/add | solution.py:266
Async XLA Ops:
  32.2 7.1 %collective-permute-start = (bf16[128,384]{1,0:T(8,128)(2,1)S(1)}, bf16[128,384]{1,0:T(8,128)(2,1)S(1)}, u32[]{:S(2)}, u32[]{:S(2)}) collective-permute-start(bf16[128,384]{1,0:T(8,128)(2,1)S(1)} %get-tuple-element.8), channel_id=1, source_target_pairs={{0,16},{1,17},{2,18},{3,19},{4,20},{5,21},{6,22},{7,23},{8,24},{9,... | collective-permute-start | bytes 294920 | tf_op jit(solution)/shard_map/ppermute | solution.py:266

commit v28 on v26

--- a/solution.py
+++ b/solution.py
@@ -18,6 +18,14 @@
 
 def as_bf16(mask):
     return mask.astype(jnp.float32).astype(jnp.bfloat16)
+
+
+def reversed_bits(value, count):
+    bits = count.bit_length() - 1
+    total = 0
+    for i in range(bits):
+        total = total | (((value >> i) & 1) << (bits - 1 - i))
+    return total
 
 
 def rows_kernel(
@@ -96,11 +104,12 @@
     running = jnp.dot(one_hot.astype(jnp.bfloat16), upper, preferred_element_type=jnp.float32)
     rank = jnp.sum(running * one_hot, axis=0, keepdims=True).astype(jnp.int32) - 1
     pool = tiles // inner * most
-    place = owner & (inner - 1)
+    place = reversed_bits(owner, inner)
     order = lax.shift_right_arithmetic(owner, inner.bit_length() - 1) * most + rank
     slot = jnp.where(live, place * pool + order, -1)
     placing = as_bf16(lax.broadcasted_iota(jnp.int32, (inner * pool, rows), 0) == slot)
-    lane = order + lax.rem(me_ref[0], LANES // pool) * pool
+    mine_at = reversed_bits(me_ref[0], inner)
+    lane = order + (mine_at & (LANES // pool - 1)) * pool
     lane_hot = as_bf16(lax.broadcasted_iota(jnp.int32, (LANES, rows), 0) == lane)
     here = live & (lax.broadcasted_iota(jnp.int32, (inner, rows), 0) == place)
     marked = jnp.where(here, (column_ref[...] + 1).astype(jnp.float32), 0.0)
@@ -165,11 +174,16 @@
         code = jnp.where(label > 0, turn * COL_DEV + label - 1, -1)
         chosen.append(as_bf16(index == code))
     chosen = jnp.concatenate(chosen, axis=1)
-    for k in range(parts):
-        block = got_ref[:, k * pool : (k + 1) * pool, :].reshape(inner * pool, LANES)
-        total = jnp.dot(chosen, block, preferred_element_type=jnp.float32)
-        own_ref[:, k * LANES : (k + 1) * LANES] = total[:COL_DEV]
-        other_ref[:, k * LANES : (k + 1) * LANES] = total[COL_DEV:].astype(jnp.bfloat16)
+    block = jnp.concatenate(
+        [
+            got_ref[:, k * pool : (k + 1) * pool, :].reshape(inner * pool, LANES)
+            for k in range(parts)
+        ],
+        axis=1,
+    )
+    total = jnp.dot(chosen, block, preferred_element_type=jnp.float32)
+    own_ref[...] = total[:COL_DEV]
+    other_ref[...] = total[COL_DEV:].astype(jnp.bfloat16)
 
 
 def per_device(
@@ -236,7 +250,9 @@
             )
         ],
     )
-    halves = [[o * inner + i for i in range(inner)] for o in range(OUTER)]
+    halves = [
+        [o * inner + reversed_bits(i, inner) for i in range(inner)] for o in range(OUTER)
+    ]
     got = lax.all_to_all(
         bucket, "tile", split_axis=0, concat_axis=0, axis_index_groups=halves, tiled=True
     )

time: 40.3 us -> 39.5 us (0.980)
  blocking collectives: 19.8 us -> 19.1 us
    all_to_all x1, blocking collectives: 19.8 us -> 19.1 us  [per_device(): lax.all_to_all(bucket, 'tile', split_axis=0, concat_axis=0, axis_index_gr...]
where the time goes in v28:
time: 39.5 us; the launch traced here: 39.3 us
  blocking collectives  19.1 us (48%)
  Pallas kernels  11.6 us (29%)
  waiting for transfers between devices  4.59 us (12%)
  starting transfers between devices  2.66 us (7%)
  other arithmetic  0.69 us (2%)
  between operations  0.67 us (2%)
    all_to_all x1, blocking collectives, per_device(): lax.all_to_all(bucket, 'tile', split_axis=0, concat_axis=0, axis_index_gr...  19.1 us
    pallas_call x1, Pallas kernels, per_device(): pl.pallas_call(functools.partial(rows_kernel, tiles, most), out_shape=jax...  11.2 us
    ppermute x1, waiting for transfers between devices, per_device(): return own + lax.ppermute(other, 'tile', pairs).astype(jnp.float32)  4.59 us
    ppermute x1, starting transfers between devices, per_device(): return own + lax.ppermute(other, 'tile', pairs).astype(jnp.float32)  2.66 us
  transfers between devices with their start and end apart: 1, of which 1 were waited for; matrix products, arithmetic and copies ran while one was open for 0% of the time, Pallas kernels for 0%

profile of v28, /device:TPU:0, one launch (start us, length us, event | category | flops | bytes accessed | tf_op | source)
XLA Modules:
  0.0 39.3 jit_solution(6418357065980158141)
XLA Ops:
  0.7 11.2 %rows_kernel.1 = bf16[16,200,128]{2,1,0:T(8,128)(2,1)S(1)} custom-call(s32[1]{0:T(128)} %bitcast.me_ref, s32[1]{0:T(128)S(6)} %copy.11.count_ref, s32[1,512]{1,0:T(1,128)} %bitcast.7, s32[1,512]{1,0:T(1,128)} %bitcast.8, bf16[512,384]{1,0:T(8,128)(2,1)} %prof_hbm.1, bf16[512,512]{1,0:T(8,128)(2,1)} %rad_hbm.1, bf16[384,4096]{1,0:T(8,128)(2,1)} %w1_hbm.1, ...), custom_call_target="tpu_custom_call" | custom-call | tf_op jit(solution)/shard_map/rows_kernel/pallas_call | solution.py:213
  11.9 19.1 %all_to_all.5.got_ref = bf16[16,200,128]{2,1,0:T(8,128)(2,1)S(1)} all-to-all(bf16[16,200,128]{2,1,0:T(8,128)(2,1)S(1)} %rows_kernel.1), channel_id=1, replica_groups={{0,8,4,12,2,10,6,14,1,9,5,13,3,11,7,15},{16,24,20,28,18,26,22,30,17,25,..., dimensions={0} | all-to-all | bytes 1638400 | tf_op jit(solution)/shard_map/all_to_all | solution.py:256
  30.9 0.4 %blocks_kernel.1 = (f32[128,384]{1,0:T(8,128)S(1)}, bf16[128,384]{1,0:T(8,128)(2,1)S(1)}) custom-call(s32[1]{0:T(128)} %bitcast.me_ref, bf16[16,200,128]{2,1,0:T(8,128)(2,1)S(1)} %all_to_all.5.got_ref), custom_call_target="tpu_custom_call" | custom-call | tf_op jit(solution)/shard_map/blocks_kernel/pallas_call | solution.py:259
  31.4 2.7 %collective-permute-start = (bf16[128,384]{1,0:T(8,128)(2,1)S(1)}, bf16[128,384]{1,0:T(8,128)(2,1)S(1)}, u32[]{:S(2)}, u32[]{:S(2)}) collective-permute-start(bf16[128,384]{1,0:T(8,128)(2,1)S(1)} %get-tuple-element.8), channel_id=1, source_target_pairs={{0,16},{1,17},{2,18},{3,19},{4,20},{5,21},{6,22},{7,23},{8,24},{9,... | collective-permute-start | bytes 294920 | tf_op jit(solution)/shard_map/ppermute | solution.py:271
  34.0 4.6 %collective-permute-done = bf16[128,384]{1,0:T(8,128)(2,1)S(1)} collective-permute-done((bf16[128,384]{1,0:T(8,128)(2,1)S(1)}, bf16[128,384]{1,0:T(8,128)(2,1)S(1)}, u32[]{:S(2)}, u32[]{:S(2)}) %collective-permute-start) | collective-permute-done | bytes 98336 | tf_op jit(solution)/shard_map/ppermute | solution.py:271
  38.6 0.7 %convert_add_fusion = f32[128,384]{1,0:T(8,128)} fusion(f32[128,384]{1,0:T(8,128)S(1)} %get-tuple-element.7, bf16[128,384]{1,0:T(8,128)(2,1)S(1)} %collective-permute-done), kind=kLoop, calls=%fused_computation | loop fusion | flops 98304 | bytes 491520 | tf_op jit(solution)/shard_map/add | solution.py:271
Async XLA Ops:
  31.4 7.3 %collective-permute-start = (bf16[128,384]{1,0:T(8,128)(2,1)S(1)}, bf16[128,384]{1,0:T(8,128)(2,1)S(1)}, u32[]{:S(2)}, u32[]{:S(2)}) collective-permute-start(bf16[128,384]{1,0:T(8,128)(2,1)S(1)} %get-tuple-element.8), channel_id=1, source_target_pairs={{0,16},{1,17},{2,18},{3,19},{4,20},{5,21},{6,22},{7,23},{8,24},{9,... | collective-permute-start | bytes 294920 | tf_op jit(solution)/shard_map/ppermute | solution.py:271

commit v29 on v28

--- a/solution.py
+++ b/solution.py
@@ -26,6 +26,19 @@
     for i in range(bits):
         total = total | (((value >> i) & 1) << (bits - 1 - i))
     return total
+
+
+def rank_of(device, count):
+    code = reversed_bits(device, count)
+    rank, shift = code, 1
+    while 1 << shift < count:
+        rank = rank ^ (code >> shift)
+        shift += 1
+    return rank
+
+
+def device_at(rank, count):
+    return reversed_bits(rank ^ (rank >> 1), count)
 
 
 def rows_kernel(
@@ -104,11 +117,11 @@
     running = jnp.dot(one_hot.astype(jnp.bfloat16), upper, preferred_element_type=jnp.float32)
     rank = jnp.sum(running * one_hot, axis=0, keepdims=True).astype(jnp.int32) - 1
     pool = tiles // inner * most
-    place = reversed_bits(owner, inner)
+    place = rank_of(owner, inner)
     order = lax.shift_right_arithmetic(owner, inner.bit_length() - 1) * most + rank
     slot = jnp.where(live, place * pool + order, -1)
     placing = as_bf16(lax.broadcasted_iota(jnp.int32, (inner * pool, rows), 0) == slot)
-    mine_at = reversed_bits(me_ref[0], inner)
+    mine_at = rank_of(me_ref[0], inner)
     lane = order + (mine_at & (LANES // pool - 1)) * pool
     lane_hot = as_bf16(lax.broadcasted_iota(jnp.int32, (LANES, rows), 0) == lane)
     here = live & (lax.broadcasted_iota(jnp.int32, (inner, rows), 0) == place)
@@ -251,7 +264,7 @@
         ],
     )
     halves = [
-        [o * inner + reversed_bits(i, inner) for i in range(inner)] for o in range(OUTER)
+        [o * inner + device_at(i, inner) for i in range(inner)] for o in range(OUTER)
     ]
     got = lax.all_to_all(
         bucket, "tile", split_axis=0, concat_axis=0, axis_index_groups=halves, tiled=True

time: 39.5 us -> 39.5 us (level)
  no operation moved by 1% of the time
where the time goes in v29:
time: 39.5 us; the launch traced here: 39.3 us
  blocking collectives  19.4 us (49%)
  Pallas kernels  11.6 us (29%)
  waiting for transfers between devices  4.23 us (11%)
  starting transfers between devices  2.66 us (7%)
  other arithmetic  0.69 us (2%)
  between operations  0.67 us (2%)
    all_to_all x1, blocking collectives, per_device(): lax.all_to_all(bucket, 'tile', split_axis=0, concat_axis=0, axis_index_gr...  19.4 us
    pallas_call x1, Pallas kernels, per_device(): pl.pallas_call(functools.partial(rows_kernel, tiles, most), out_shape=jax...  11.2 us
    ppermute x1, waiting for transfers between devices, per_device(): return own + lax.ppermute(other, 'tile', pairs).astype(jnp.float32)  4.23 us
    ppermute x1, starting transfers between devices, per_device(): return own + lax.ppermute(other, 'tile', pairs).astype(jnp.float32)  2.66 us
  transfers between devices with their start and end apart: 1, of which 1 were waited for; matrix products, arithmetic and copies ran while one was open for 0% of the time, Pallas kernels for 0%

profile of v29, /device:TPU:0, one launch (start us, length us, event | category | flops | bytes accessed | tf_op | source)
XLA Modules:
  0.0 39.3 jit_solution(14394608955822749340)
XLA Ops:
  0.7 11.2 %rows_kernel.1 = bf16[16,200,128]{2,1,0:T(8,128)(2,1)S(1)} custom-call(s32[1]{0:T(128)} %bitcast.me_ref, s32[1]{0:T(128)S(6)} %copy.11.count_ref, s32[1,512]{1,0:T(1,128)} %bitcast.7, s32[1,512]{1,0:T(1,128)} %bitcast.8, bf16[512,384]{1,0:T(8,128)(2,1)} %prof_hbm.1, bf16[512,512]{1,0:T(8,128)(2,1)} %rad_hbm.1, bf16[384,4096]{1,0:T(8,128)(2,1)} %w1_hbm.1, ...), custom_call_target="tpu_custom_call" | custom-call | tf_op jit(solution)/shard_map/rows_kernel/pallas_call | solution.py:226
  11.9 19.4 %all_to_all.5.got_ref = bf16[16,200,128]{2,1,0:T(8,128)(2,1)S(1)} all-to-all(bf16[16,200,128]{2,1,0:T(8,128)(2,1)S(1)} %rows_kernel.1), channel_id=1, replica_groups={{0,8,12,4,6,14,10,2,3,11,15,7,5,13,9,1},{16,24,28,20,22,30,26,18,19,27,..., dimensions={0} | all-to-all | bytes 1638400 | tf_op jit(solution)/shard_map/all_to_all | solution.py:269
  31.3 0.4 %blocks_kernel.1 = (f32[128,384]{1,0:T(8,128)S(1)}, bf16[128,384]{1,0:T(8,128)(2,1)S(1)}) custom-call(s32[1]{0:T(128)} %bitcast.me_ref, bf16[16,200,128]{2,1,0:T(8,128)(2,1)S(1)} %all_to_all.5.got_ref), custom_call_target="tpu_custom_call" | custom-call | tf_op jit(solution)/shard_map/blocks_kernel/pallas_call | solution.py:272
  31.7 2.7 %collective-permute-start = (bf16[128,384]{1,0:T(8,128)(2,1)S(1)}, bf16[128,384]{1,0:T(8,128)(2,1)S(1)}, u32[]{:S(2)}, u32[]{:S(2)}) collective-permute-start(bf16[128,384]{1,0:T(8,128)(2,1)S(1)} %get-tuple-element.8), channel_id=1, source_target_pairs={{0,16},{1,17},{2,18},{3,19},{4,20},{5,21},{6,22},{7,23},{8,24},{9,... | collective-permute-start | bytes 294920 | tf_op jit(solution)/shard_map/ppermute | solution.py:284
  34.4 4.2 %collective-permute-done = bf16[128,384]{1,0:T(8,128)(2,1)S(1)} collective-permute-done((bf16[128,384]{1,0:T(8,128)(2,1)S(1)}, bf16[128,384]{1,0:T(8,128)(2,1)S(1)}, u32[]{:S(2)}, u32[]{:S(2)}) %collective-permute-start) | collective-permute-done | bytes 98336 | tf_op jit(solution)/shard_map/ppermute | solution.py:284
  38.6 0.7 %convert_add_fusion = f32[128,384]{1,0:T(8,128)} fusion(f32[128,384]{1,0:T(8,128)S(1)} %get-tuple-element.7, bf16[128,384]{1,0:T(8,128)(2,1)S(1)} %collective-permute-done), kind=kLoop, calls=%fused_computation | loop fusion | flops 98304 | bytes 491520 | tf_op jit(solution)/shard_map/add | solution.py:284
Async XLA Ops:
  31.7 6.9 %collective-permute-start = (bf16[128,384]{1,0:T(8,128)(2,1)S(1)}, bf16[128,384]{1,0:T(8,128)(2,1)S(1)}, u32[]{:S(2)}, u32[]{:S(2)}) collective-permute-start(bf16[128,384]{1,0:T(8,128)(2,1)S(1)} %get-tuple-element.8), channel_id=1, source_target_pairs={{0,16},{1,17},{2,18},{3,19},{4,20},{5,21},{6,22},{7,23},{8,24},{9,... | collective-permute-start | bytes 294920 | tf_op jit(solution)/shard_map/ppermute | solution.py:284

commit v30 on v29

--- a/solution.py
+++ b/solution.py
@@ -143,7 +143,7 @@
         rad_ref[m, :] = jnp.where(alive, misfit, 0.0).astype(jnp.bfloat16)
     for i in range(hid // CHUNK):
         part = pl.ds(i * CHUNK, CHUNK)
-        for m in blocks:
+        for m in [pl.ds(0, rows)]:
             back = lax.dot_general(
                 rad_ref[m, :], w2_ref[part, :], NT, preferred_element_type=jnp.float32
             )

time: 39.5 us -> 39.5 us (level)
  no operation moved by 1% of the time
where the time goes in v30:
time: 39.5 us; the launch traced here: 39.3 us
  blocking collectives  19.4 us (49%)
  Pallas kernels  11.6 us (29%)
  waiting for transfers between devices  4.23 us (11%)
  starting transfers between devices  2.66 us (7%)
  other arithmetic  0.69 us (2%)
  between operations  0.67 us (2%)
    all_to_all x1, blocking collectives, per_device(): lax.all_to_all(bucket, 'tile', split_axis=0, concat_axis=0, axis_index_gr...  19.4 us
    pallas_call x1, Pallas kernels, per_device(): pl.pallas_call(functools.partial(rows_kernel, tiles, most), out_shape=jax...  11.2 us
    ppermute x1, waiting for transfers between devices, per_device(): return own + lax.ppermute(other, 'tile', pairs).astype(jnp.float32)  4.23 us
    ppermute x1, starting transfers between devices, per_device(): return own + lax.ppermute(other, 'tile', pairs).astype(jnp.float32)  2.66 us
  transfers between devices with their start and end apart: 1, of which 1 were waited for; matrix products, arithmetic and copies ran while one was open for 0% of the time, Pallas kernels for 0%

profile of v30, /device:TPU:0, one launch (start us, length us, event | category | flops | bytes accessed | tf_op | source)
XLA Modules:
  0.0 39.3 jit_solution(2656608176008657884)
XLA Ops:
  0.7 11.2 %rows_kernel.1 = bf16[16,200,128]{2,1,0:T(8,128)(2,1)S(1)} custom-call(s32[1]{0:T(128)} %bitcast.me_ref, s32[1]{0:T(128)S(6)} %copy.11.count_ref, s32[1,512]{1,0:T(1,128)} %bitcast.7, s32[1,512]{1,0:T(1,128)} %bitcast.8, bf16[512,384]{1,0:T(8,128)(2,1)} %prof_hbm.1, bf16[512,512]{1,0:T(8,128)(2,1)} %rad_hbm.1, bf16[384,4096]{1,0:T(8,128)(2,1)} %w1_hbm.1, ...), custom_call_target="tpu_custom_call" | custom-call | tf_op jit(solution)/shard_map/rows_kernel/pallas_call | solution.py:226
  11.9 19.4 %all_to_all.5.got_ref = bf16[16,200,128]{2,1,0:T(8,128)(2,1)S(1)} all-to-all(bf16[16,200,128]{2,1,0:T(8,128)(2,1)S(1)} %rows_kernel.1), channel_id=1, replica_groups={{0,8,12,4,6,14,10,2,3,11,15,7,5,13,9,1},{16,24,28,20,22,30,26,18,19,27,..., dimensions={0} | all-to-all | bytes 1638400 | tf_op jit(solution)/shard_map/all_to_all | solution.py:269
  31.3 0.4 %blocks_kernel.1 = (f32[128,384]{1,0:T(8,128)S(1)}, bf16[128,384]{1,0:T(8,128)(2,1)S(1)}) custom-call(s32[1]{0:T(128)} %bitcast.me_ref, bf16[16,200,128]{2,1,0:T(8,128)(2,1)S(1)} %all_to_all.5.got_ref), custom_call_target="tpu_custom_call" | custom-call | tf_op jit(solution)/shard_map/blocks_kernel/pallas_call | solution.py:272
  31.7 2.7 %collective-permute-start = (bf16[128,384]{1,0:T(8,128)(2,1)S(1)}, bf16[128,384]{1,0:T(8,128)(2,1)S(1)}, u32[]{:S(2)}, u32[]{:S(2)}) collective-permute-start(bf16[128,384]{1,0:T(8,128)(2,1)S(1)} %get-tuple-element.8), channel_id=1, source_target_pairs={{0,16},{1,17},{2,18},{3,19},{4,20},{5,21},{6,22},{7,23},{8,24},{9,... | collective-permute-start | bytes 294920 | tf_op jit(solution)/shard_map/ppermute | solution.py:284
  34.4 4.2 %collective-permute-done = bf16[128,384]{1,0:T(8,128)(2,1)S(1)} collective-permute-done((bf16[128,384]{1,0:T(8,128)(2,1)S(1)}, bf16[128,384]{1,0:T(8,128)(2,1)S(1)}, u32[]{:S(2)}, u32[]{:S(2)}) %collective-permute-start) | collective-permute-done | bytes 98336 | tf_op jit(solution)/shard_map/ppermute | solution.py:284
  38.6 0.7 %convert_add_fusion = f32[128,384]{1,0:T(8,128)} fusion(f32[128,384]{1,0:T(8,128)S(1)} %get-tuple-element.7, bf16[128,384]{1,0:T(8,128)(2,1)S(1)} %collective-permute-done), kind=kLoop, calls=%fused_computation | loop fusion | flops 98304 | bytes 491520 | tf_op jit(solution)/shard_map/add | solution.py:284
Async XLA Ops:
  31.7 6.9 %collective-permute-start = (bf16[128,384]{1,0:T(8,128)(2,1)S(1)}, bf16[128,384]{1,0:T(8,128)(2,1)S(1)}, u32[]{:S(2)}, u32[]{:S(2)}) collective-permute-start(bf16[128,384]{1,0:T(8,128)(2,1)S(1)} %get-tuple-element.8), channel_id=1, source_target_pairs={{0,16},{1,17},{2,18},{3,19},{4,20},{5,21},{6,22},{7,23},{8,24},{9,... | collective-permute-start | bytes 294920 | tf_op jit(solution)/shard_map/ppermute | solution.py:284

commit v31 on v29

--- a/solution.py
+++ b/solution.py
@@ -168,14 +168,13 @@
             ].reshape(wide, pool, LANES)
 
 
-def blocks_kernel(tiles, most, me_ref, got_ref, own_ref, other_ref):
+def sums_kernel(tiles, most, side, me_ref, got_ref, out_ref):
     inner = got_ref.shape[0]
-    outer = tiles // inner
-    pool = outer * most
+    pool = tiles // inner * most
     group = LANES // pool
-    parts = own_ref.shape[1] // LANES
+    parts = out_ref.shape[1] // LANES
     marks = got_ref[:, parts * pool :, :].astype(jnp.float32)[:, 0, :]
-    index = lax.broadcasted_iota(jnp.int32, (outer * COL_DEV, LANES), 0)
+    index = lax.broadcasted_iota(jnp.int32, (COL_DEV, LANES), 0)
     lane = lax.broadcasted_iota(jnp.int32, (1, LANES), 1) & (pool - 1)
     turn = lax.shift_right_arithmetic(lane, most.bit_length() - 1) ^ (
         lax.shift_right_arithmetic(me_ref[0], inner.bit_length() - 1)
@@ -184,7 +183,7 @@
     for g in range(inner // group):
         label = jnp.sum(marks[g * group : (g + 1) * group], axis=0, keepdims=True)
         label = label.astype(jnp.int32)
-        code = jnp.where(label > 0, turn * COL_DEV + label - 1, -1)
+        code = jnp.where((label > 0) & (turn == side), label - 1, -1)
         chosen.append(as_bf16(index == code))
     chosen = jnp.concatenate(chosen, axis=1)
     block = jnp.concatenate(
@@ -195,8 +194,7 @@
         axis=1,
     )
     total = jnp.dot(chosen, block, preferred_element_type=jnp.float32)
-    own_ref[...] = total[:COL_DEV]
-    other_ref[...] = total[COL_DEV:].astype(jnp.bfloat16)
+    out_ref[...] = total.astype(out_ref.dtype)
 
 
 def per_device(
@@ -269,19 +267,23 @@
     got = lax.all_to_all(
         bucket, "tile", split_axis=0, concat_axis=0, axis_index_groups=halves, tiled=True
     )
-    own, other = pl.pallas_call(
-        functools.partial(blocks_kernel, tiles, most),
-        out_shape=[
-            jax.ShapeDtypeStruct((COL_DEV, width), jnp.float32),
-            jax.ShapeDtypeStruct((COL_DEV, width), jnp.bfloat16),
-        ],
-        in_specs=[smem, vmem],
-        out_specs=[vmem, vmem],
-        compiler_params=pltpu.CompilerParams(vmem_limit_bytes=24 * 1024 * 1024),
-        name="blocks_kernel",
-    )(me, got)
+
+    def sums(side, dtype):
+        return pl.pallas_call(
+            functools.partial(sums_kernel, tiles, most, side),
+            out_shape=jax.ShapeDtypeStruct((COL_DEV, width), dtype),
+            in_specs=[smem, vmem],
+            out_specs=vmem,
+            compiler_params=pltpu.CompilerParams(vmem_limit_bytes=24 * 1024 * 1024),
+            cost_estimate=pl.CostEstimate(
+                flops=1 << 28, bytes_accessed=1 << 20, transcendentals=0
+            ),
+            name="sums_kernel",
+        )(me, got)
+
     pairs = [(t, (t + inner) % tiles) for t in range(tiles)]
-    return own + lax.ppermute(other, "tile", pairs).astype(jnp.float32)
+    came = lax.ppermute(sums(1, jnp.bfloat16), "tile", pairs)
+    return sums(0, jnp.float32) + came.astype(jnp.float32)
 
 
 def solution(mesh):

time: 39.5 us -> 39.3 us (level)
  transfers between devices with their start and end apart: 1 -> 1, of which waited for: 1 -> 1; matrix products, arithmetic and copies ran while one was open for 0% -> 0% of each run, Pallas kernels for 0% -> 1%
where the time goes in v31:
time: 39.3 us; the launch traced here: 39.2 us
  blocking collectives  19.4 us (49%)
  Pallas kernels  11.8 us (30%)
  waiting for transfers between devices  3.92 us (10%)
  starting transfers between devices  2.66 us (7%)
  other arithmetic  0.69 us (2%)
  between operations  0.67 us (2%)
    all_to_all x1, blocking collectives, per_device(): lax.all_to_all(bucket, 'tile', split_axis=0, concat_axis=0, axis_index_gr...  19.4 us
    pallas_call x1, Pallas kernels, per_device(): pl.pallas_call(functools.partial(rows_kernel, tiles, most), out_shape=jax...  11.2 us
    ppermute x1, waiting for transfers between devices, per_device(): came = lax.ppermute(sums(1, jnp.bfloat16), 'tile', pairs)  3.92 us
    ppermute x1, starting transfers between devices, per_device(): came = lax.ppermute(sums(1, jnp.bfloat16), 'tile', pairs)  2.66 us
  transfers between devices with their start and end apart: 1, of which 1 were waited for; matrix products, arithmetic and copies ran while one was open for 0% of the time, Pallas kernels for 1%

profile of v31, /device:TPU:0, one launch (start us, length us, event | category | flops | bytes accessed | tf_op | source)
XLA Modules:
  0.0 39.2 jit_solution(17838039850292313304)
XLA Ops:
  0.7 11.2 %rows_kernel.1 = bf16[16,200,128]{2,1,0:T(8,128)(2,1)S(1)} custom-call(s32[1]{0:T(128)} %bitcast.me_ref, s32[1]{0:T(128)S(6)} %copy.11.count_ref, s32[1,512]{1,0:T(1,128)} %bitcast.7, s32[1,512]{1,0:T(1,128)} %bitcast.8, bf16[512,384]{1,0:T(8,128)(2,1)} %prof_hbm.1, bf16[512,512]{1,0:T(8,128)(2,1)} %rad_hbm.1, bf16[384,4096]{1,0:T(8,128)(2,1)} %w1_hbm.1, ...), custom_call_target="tpu_custom_call" | custom-call | tf_op jit(solution)/shard_map/rows_kernel/pallas_call | solution.py:224
  11.9 19.4 %all_to_all.5.got_ref = bf16[16,200,128]{2,1,0:T(8,128)(2,1)S(1)} all-to-all(bf16[16,200,128]{2,1,0:T(8,128)(2,1)S(1)} %rows_kernel.1), channel_id=1, replica_groups={{0,8,12,4,6,14,10,2,3,11,15,7,5,13,9,1},{16,24,28,20,22,30,26,18,19,27,..., dimensions={0} | all-to-all | bytes 1638400 | tf_op jit(solution)/shard_map/all_to_all | solution.py:267
  31.3 0.3 sums_kernel.3
  31.6 2.7 %collective-permute-start = (bf16[128,384]{1,0:T(8,128)(2,1)S(1)}, bf16[128,384]{1,0:T(8,128)(2,1)S(1)}, u32[]{:S(2)}, u32[]{:S(2)}) collective-permute-start(bf16[128,384]{1,0:T(8,128)(2,1)S(1)} %sums_kernel.3), channel_id=1, source_target_pairs={{0,16},{1,17},{2,18},{3,19},{4,20},{5,21},{6,22},{7,23},{8,24},{9,... | collective-permute-start | bytes 294920 | tf_op jit(solution)/shard_map/ppermute | solution.py:285
  34.2 0.3 sums_kernel.2
  34.5 3.9 %collective-permute-done = bf16[128,384]{1,0:T(8,128)(2,1)S(1)} collective-permute-done((bf16[128,384]{1,0:T(8,128)(2,1)S(1)}, bf16[128,384]{1,0:T(8,128)(2,1)S(1)}, u32[]{:S(2)}, u32[]{:S(2)}) %collective-permute-start) | collective-permute-done | bytes 98336 | tf_op jit(solution)/shard_map/ppermute | solution.py:285
  38.5 0.7 %convert_add_fusion = f32[128,384]{1,0:T(8,128)} fusion(f32[128,384]{1,0:T(8,128)S(1)} %sums_kernel.2, bf16[128,384]{1,0:T(8,128)(2,1)S(1)} %collective-permute-done), kind=kLoop, calls=%fused_computation | loop fusion | flops 98304 | bytes 491520 | tf_op jit(solution)/shard_map/add | solution.py:286
Async XLA Ops:
  31.6 6.9 %collective-permute-start = (bf16[128,384]{1,0:T(8,128)(2,1)S(1)}, bf16[128,384]{1,0:T(8,128)(2,1)S(1)}, u32[]{:S(2)}, u32[]{:S(2)}) collective-permute-start(bf16[128,384]{1,0:T(8,128)(2,1)S(1)} %sums_kernel.3), channel_id=1, source_target_pairs={{0,16},{1,17},{2,18},{3,19},{4,20},{5,21},{6,22},{7,23},{8,24},{9,... | collective-permute-start | bytes 294920 | tf_op jit(solution)/shard_map/ppermute | solution.py:285

commit v32 on v31

--- a/solution.py
+++ b/solution.py
@@ -73,7 +73,7 @@
     rows, width = prof_ref.shape
     hid = w1_ref.shape[1]
     chan = rad_ref.shape[1]
-    starts = [0, hid // 4, hid]
+    starts = [0, hid // 4, hid // 2, hid]
     pieces = [pl.ds(lo, hi - lo) for lo, hi in zip(starts[:-1], starts[1:])]
     pairs = (
         [(prof_hbm, prof_ref), (b1_hbm, b1_ref)]
@@ -239,7 +239,7 @@
             pltpu.VMEM((rows, hid), jnp.bfloat16),
             pltpu.VMEM((rows, hid), jnp.float32),
             pltpu.VMEM((width, rows), jnp.bfloat16),
-            pltpu.SemaphoreType.DMA((10,)),
+            pltpu.SemaphoreType.DMA((11,)),
         ],
         compiler_params=pltpu.CompilerParams(vmem_limit_bytes=40 * 1024 * 1024),
         name="rows_kernel",

time: 39.3 us -> 39.6 us (level)
  no operation moved by 1% of the time
where the time goes in v32:
time: 39.6 us; the launch traced here: 39.4 us
  blocking collectives  19.4 us (49%)
  Pallas kernels  12 us (30%)
  waiting for transfers between devices  3.93 us (10%)
  starting transfers between devices  2.65 us (7%)
  other arithmetic  0.69 us (2%)
  between operations  0.67 us (2%)
    all_to_all x1, blocking collectives, per_device(): lax.all_to_all(bucket, 'tile', split_axis=0, concat_axis=0, axis_index_gr...  19.4 us
    pallas_call x1, Pallas kernels, per_device(): pl.pallas_call(functools.partial(rows_kernel, tiles, most), out_shape=jax...  11.4 us
    ppermute x1, waiting for transfers between devices, per_device(): came = lax.ppermute(sums(1, jnp.bfloat16), 'tile', pairs)  3.93 us
    ppermute x1, starting transfers between devices, per_device(): came = lax.ppermute(sums(1, jnp.bfloat16), 'tile', pairs)  2.65 us
  transfers between devices with their start and end apart: 1, of which 1 were waited for; matrix products, arithmetic and copies ran while one was open for 0% of the time, Pallas kernels for 1%

profile of v32, /device:TPU:0, one launch (start us, length us, event | category | flops | bytes accessed | tf_op | source)
XLA Modules:
  0.0 39.4 jit_solution(7308478560061727621)
XLA Ops:
  0.7 11.4 %rows_kernel.1 = bf16[16,200,128]{2,1,0:T(8,128)(2,1)S(1)} custom-call(s32[1]{0:T(128)} %bitcast.me_ref, s32[1]{0:T(128)S(6)} %copy.11.count_ref, s32[1,512]{1,0:T(1,128)} %bitcast.7, s32[1,512]{1,0:T(1,128)} %bitcast.8, bf16[512,384]{1,0:T(8,128)(2,1)} %prof_hbm.1, bf16[512,512]{1,0:T(8,128)(2,1)} %rad_hbm.1, bf16[384,4096]{1,0:T(8,128)(2,1)} %w1_hbm.1, ...), custom_call_target="tpu_custom_call" | custom-call | tf_op jit(solution)/shard_map/rows_kernel/pallas_call | solution.py:224
  12.1 19.4 %all_to_all.5.got_ref = bf16[16,200,128]{2,1,0:T(8,128)(2,1)S(1)} all-to-all(bf16[16,200,128]{2,1,0:T(8,128)(2,1)S(1)} %rows_kernel.1), channel_id=1, replica_groups={{0,8,12,4,6,14,10,2,3,11,15,7,5,13,9,1},{16,24,28,20,22,30,26,18,19,27,..., dimensions={0} | all-to-all | bytes 1638400 | tf_op jit(solution)/shard_map/all_to_all | solution.py:267
  31.5 0.3 sums_kernel.3
  31.8 2.7 %collective-permute-start = (bf16[128,384]{1,0:T(8,128)(2,1)S(1)}, bf16[128,384]{1,0:T(8,128)(2,1)S(1)}, u32[]{:S(2)}, u32[]{:S(2)}) collective-permute-start(bf16[128,384]{1,0:T(8,128)(2,1)S(1)} %sums_kernel.3), channel_id=1, source_target_pairs={{0,16},{1,17},{2,18},{3,19},{4,20},{5,21},{6,22},{7,23},{8,24},{9,... | collective-permute-start | bytes 294920 | tf_op jit(solution)/shard_map/ppermute | solution.py:285
  34.4 0.3 sums_kernel.2
  34.8 3.9 %collective-permute-done = bf16[128,384]{1,0:T(8,128)(2,1)S(1)} collective-permute-done((bf16[128,384]{1,0:T(8,128)(2,1)S(1)}, bf16[128,384]{1,0:T(8,128)(2,1)S(1)}, u32[]{:S(2)}, u32[]{:S(2)}) %collective-permute-start) | collective-permute-done | bytes 98336 | tf_op jit(solution)/shard_map/ppermute | solution.py:285
  38.7 0.7 %convert_add_fusion = f32[128,384]{1,0:T(8,128)} fusion(f32[128,384]{1,0:T(8,128)S(1)} %sums_kernel.2, bf16[128,384]{1,0:T(8,128)(2,1)S(1)} %collective-permute-done), kind=kLoop, calls=%fused_computation | loop fusion | flops 98304 | bytes 491520 | tf_op jit(solution)/shard_map/add | solution.py:286
Async XLA Ops:
  31.8 6.9 %collective-permute-start = (bf16[128,384]{1,0:T(8,128)(2,1)S(1)}, bf16[128,384]{1,0:T(8,128)(2,1)S(1)}, u32[]{:S(2)}, u32[]{:S(2)}) collective-permute-start(bf16[128,384]{1,0:T(8,128)(2,1)S(1)} %sums_kernel.3), channel_id=1, source_target_pairs={{0,16},{1,17},{2,18},{3,19},{4,20},{5,21},{6,22},{7,23},{8,24},{9,... | collective-permute-start | bytes 294920 | tf_op jit(solution)/shard_map/ppermute | solution.py:285

commit v33 on v31

--- a/solution.py
+++ b/solution.py
@@ -153,10 +153,11 @@
             w1_ref[...], hidden_ref[m, :], NT, preferred_element_type=jnp.float32
         )
         grads_ref[:, m] = grads.astype(jnp.bfloat16)
-    wide = ROWS // pool
+    step = 2 * ROWS
+    wide = step // pool
     for n in range(inner // wide):
         placed = lax.dot_general(
-            placing[n * ROWS : (n + 1) * ROWS],
+            placing[n * step : (n + 1) * step],
             grads_ref[...],
             NT,
             preferred_element_type=jnp.float32,

time: 39.3 us -> 39.3 us (level)
  no operation moved by 1% of the time
where the time goes in v33:
time: 39.3 us; the launch traced here: 39.1 us
  blocking collectives  19.4 us (49%)
  Pallas kernels  11.8 us (30%)
  waiting for transfers between devices  3.93 us (10%)
  starting transfers between devices  2.66 us (7%)
  other arithmetic  0.69 us (2%)
  between operations  0.67 us (2%)
    all_to_all x1, blocking collectives, per_device(): lax.all_to_all(bucket, 'tile', split_axis=0, concat_axis=0, axis_index_gr...  19.4 us
    pallas_call x1, Pallas kernels, per_device(): pl.pallas_call(functools.partial(rows_kernel, tiles, most), out_shape=jax...  11.2 us
    ppermute x1, waiting for transfers between devices, per_device(): came = lax.ppermute(sums(1, jnp.bfloat16), 'tile', pairs)  3.93 us
    ppermute x1, starting transfers between devices, per_device(): came = lax.ppermute(sums(1, jnp.bfloat16), 'tile', pairs)  2.66 us
  transfers between devices with their start and end apart: 1, of which 1 were waited for; matrix products, arithmetic and copies ran while one was open for 0% of the time, Pallas kernels for 1%

profile of v33, /device:TPU:0, one launch (start us, length us, event | category | flops | bytes accessed | tf_op | source)
XLA Modules:
  0.0 39.1 jit_solution(17753248822298287873)
XLA Ops:
  0.7 11.2 %rows_kernel.1 = bf16[16,200,128]{2,1,0:T(8,128)(2,1)S(1)} custom-call(s32[1]{0:T(128)} %bitcast.me_ref, s32[1]{0:T(128)S(6)} %copy.11.count_ref, s32[1,512]{1,0:T(1,128)} %bitcast.7, s32[1,512]{1,0:T(1,128)} %bitcast.8, bf16[512,384]{1,0:T(8,128)(2,1)} %prof_hbm.1, bf16[512,512]{1,0:T(8,128)(2,1)} %rad_hbm.1, bf16[384,4096]{1,0:T(8,128)(2,1)} %w1_hbm.1, ...), custom_call_target="tpu_custom_call" | custom-call | tf_op jit(solution)/shard_map/rows_kernel/pallas_call | solution.py:225
  11.8 19.4 %all_to_all.5.got_ref = bf16[16,200,128]{2,1,0:T(8,128)(2,1)S(1)} all-to-all(bf16[16,200,128]{2,1,0:T(8,128)(2,1)S(1)} %rows_kernel.1), channel_id=1, replica_groups={{0,8,12,4,6,14,10,2,3,11,15,7,5,13,9,1},{16,24,28,20,22,30,26,18,19,27,..., dimensions={0} | all-to-all | bytes 1638400 | tf_op jit(solution)/shard_map/all_to_all | solution.py:268
  31.2 0.3 sums_kernel.3
  31.5 2.7 %collective-permute-start = (bf16[128,384]{1,0:T(8,128)(2,1)S(1)}, bf16[128,384]{1,0:T(8,128)(2,1)S(1)}, u32[]{:S(2)}, u32[]{:S(2)}) collective-permute-start(bf16[128,384]{1,0:T(8,128)(2,1)S(1)} %sums_kernel.3), channel_id=1, source_target_pairs={{0,16},{1,17},{2,18},{3,19},{4,20},{5,21},{6,22},{7,23},{8,24},{9,... | collective-permute-start | bytes 294920 | tf_op jit(solution)/shard_map/ppermute | solution.py:286
  34.2 0.3 sums_kernel.2
  34.5 3.9 %collective-permute-done = bf16[128,384]{1,0:T(8,128)(2,1)S(1)} collective-permute-done((bf16[128,384]{1,0:T(8,128)(2,1)S(1)}, bf16[128,384]{1,0:T(8,128)(2,1)S(1)}, u32[]{:S(2)}, u32[]{:S(2)}) %collective-permute-start) | collective-permute-done | bytes 98336 | tf_op jit(solution)/shard_map/ppermute | solution.py:286
  38.4 0.7 %convert_add_fusion = f32[128,384]{1,0:T(8,128)} fusion(f32[128,384]{1,0:T(8,128)S(1)} %sums_kernel.2, bf16[128,384]{1,0:T(8,128)(2,1)S(1)} %collective-permute-done), kind=kLoop, calls=%fused_computation | loop fusion | flops 98304 | bytes 491520 | tf_op jit(solution)/shard_map/add | solution.py:287
Async XLA Ops:
  31.5 6.9 %collective-permute-start = (bf16[128,384]{1,0:T(8,128)(2,1)S(1)}, bf16[128,384]{1,0:T(8,128)(2,1)S(1)}, u32[]{:S(2)}, u32[]{:S(2)}) collective-permute-start(bf16[128,384]{1,0:T(8,128)(2,1)S(1)} %sums_kernel.3), channel_id=1, source_target_pairs={{0,16},{1,17},{2,18},{3,19},{4,20},{5,21},{6,22},{7,23},{8,24},{9,... | collective-permute-start | bytes 294920 | tf_op jit(solution)/shard_map/ppermute | solution.py:286
